TPU v7x, 32 devices: a whole 2x2x4 slice. The times are simulated.
32 devices in a mesh: batch: 8 (over z, x), seq: 4 (over y, core).
Axes of the slice: x: 2, y: 2, z: 4, core: 2. Of those that a mesh axis runs over, the one named last changes fastest.
Arguments:
- inputs: bfloat16 [16, 1024, 1024], P('batch', 'seq'), may hold values from -6 to 6
- ends: int32 [16], P('batch'), may hold values from 256 to 1024, as said below
- ln_gain: bfloat16 [1024], P(('batch', 'seq')), may hold values from 0.5 to 1.5
- ln_bias: bfloat16 [1024], P(('batch', 'seq')), may hold values from -1.5 to 1.5
- w_qkv: bfloat16 [1024, 3072], P(('batch', 'seq')), may hold values from -0.1875 to 0.1875
- w_attn: bfloat16 [1024, 1024], P(('batch', 'seq')), may hold values from -2 to 2
- w_in: bfloat16 [1024, 4096], P(('batch', 'seq')), may hold values from -0.1875 to 0.1875
- b_in: bfloat16 [4096], P(('batch', 'seq')), may hold values from -2.5 to 2.5
- w_out: bfloat16 [4096, 1024], P(('batch', 'seq')), may hold values from -0.09375 to 0.09375
- b_out: bfloat16 [1024], P(('batch', 'seq')), may hold values from -2.5 to 2.5
- cotangent: bfloat16 [16, 1024, 1024], P('batch', 'seq'), may hold values from -6 to 6
Outputs:
- output: bfloat16 [16, 1024, 1024], P('batch', 'seq')
- grad_inputs: float32 [16, 1024, 1024], P('batch', 'seq')
- grad_ln_gain: float32 [1024], P(('batch', 'seq'))
- grad_ln_bias: float32 [1024], P(('batch', 'seq'))
- grad_w_qkv: float32 [1024, 3072], P(('batch', 'seq'))
- grad_w_attn: float32 [1024, 1024], P(('batch', 'seq'))
- grad_w_in: float32 [1024, 4096], P(('batch', 'seq'))
- grad_b_in: float32 [4096], P(('batch', 'seq'))
- grad_w_out: float32 [4096, 1024], P(('batch', 'seq'))
- grad_b_out: float32 [1024], P(('batch', 'seq'))
Inputs may be any that keep to these rules, and one draw needn't show every extreme that they name: A window holds the end of one protein at position ends - 1 when ends < 1024; the next protein starts there. In each aligned block of 2 windows, one drawn from the seed has ends = 1024 and the next one in the block, cyclically, has ends = 256.
All inputs are finite; a program needn't handle non-finite values.
Results may differ from a plain program's by a relative error of at most 0.0086.
Values may be sent and summed in bfloat16 or wider, within the bound.
A program may use at most 256 MiB of HBM per device.

v0:
```python
import math

import jax
import jax.numpy as jnp
from jax import lax
from jax.sharding import PartitionSpec as P

HEADS = 16
HD = 64
ROTARY = 32
MICRO = 2


norm_eps = 1e-05
gelu_factor = 0.7978845608028654
masked_score = -1e30


def gelu_tanh(values):
    return (
        0.5
        * values
        * (1.0 + jnp.tanh(gelu_factor * (values + 0.044715 * values * values * values)))
    )


def layer_norm(row_values, norm_gain, norm_shift):
    average = jnp.mean(row_values, axis=-1, keepdims=True)
    centered = row_values - average
    variance = jnp.mean(centered * centered, axis=-1, keepdims=True)
    return centered * lax.rsqrt(variance + norm_eps) * norm_gain + norm_shift


def rotary_tables(positions):
    pair_index = jnp.arange(ROTARY // 2, dtype=jnp.float32)
    inverse = 10000.0 ** (-2.0 * pair_index / ROTARY)
    angles = positions[:, None] * inverse[None, :]
    return (jnp.cos(angles), jnp.sin(angles))


def rotate(vectors, cosine, sine_table):
    rotated = vectors[..., :ROTARY]
    even_part = rotated[..., 0::2]
    odd_part = rotated[..., 1::2]
    cosine_wide = cosine[:, None, :]
    sine_wide = sine_table[:, None, :]
    new_even = even_part * cosine_wide - odd_part * sine_wide
    new_odd = odd_part * cosine_wide + even_part * sine_wide
    merged = jnp.stack([new_even, new_odd], axis=-1).reshape(rotated.shape)
    return jnp.concatenate([merged, vectors[..., ROTARY:]], axis=-1)


def visible(query_places, key_places, ending):
    query_after = query_places[:, None] >= ending
    key_after = key_places[None, :] >= ending
    return (key_places[None, :] <= query_places[:, None]) & (query_after == key_after)


def block_scores(block_queries, key_vectors, query_places, key_places, ending, score_scale):
    scores = (
        jnp.einsum("qhd,khd->hqk", block_queries, key_vectors, preferred_element_type=jnp.float32)
        * score_scale
    )
    return jnp.where(visible(query_places, key_places, ending)[None], scores, masked_score)


def attend_forward(packed, ending):
    seq_len, head_count, triple = packed.shape
    head_size = triple // 3
    block_rows = min(512, seq_len)
    score_scale = 1.0 / math.sqrt(head_size)
    queries = packed[:, :, :head_size]
    key_vectors = packed[:, :, head_size : 2 * head_size]
    values = packed[:, :, 2 * head_size :]
    key_places = jnp.arange(seq_len, dtype=jnp.int32)

    def one_block(block_index):
        first_row = block_index * block_rows
        block_queries = lax.dynamic_slice_in_dim(queries, first_row, block_rows, 0)
        query_places = first_row + jnp.arange(block_rows, dtype=jnp.int32)
        scores = block_scores(
            block_queries, key_vectors, query_places, key_places, ending, score_scale
        )
        row_peak = jnp.max(scores, axis=-1, keepdims=True)
        weights = jnp.exp(scores - row_peak)
        row_total = jnp.sum(weights, axis=-1, keepdims=True)
        probabilities = (weights / row_total).astype(jnp.bfloat16)
        result = jnp.einsum(
            "hqk,khd->qhd", probabilities, values, preferred_element_type=jnp.float32
        )
        return (result.astype(jnp.bfloat16), row_peak, row_total)

    results, peaks, totals = lax.map(one_block, jnp.arange(seq_len // block_rows, dtype=jnp.int32))
    return (results.reshape(seq_len, head_count, head_size), peaks, totals)


def attend_backward(packed, d_attended, peaks, totals, ending, full_cosine, full_sine):
    seq_len, head_count, triple = packed.shape
    head_size = triple // 3
    block_rows = min(512, seq_len)
    score_scale = 1.0 / math.sqrt(head_size)
    queries = packed[:, :, :head_size]
    key_vectors = packed[:, :, head_size : 2 * head_size]
    values = packed[:, :, 2 * head_size :]
    key_places = jnp.arange(seq_len, dtype=jnp.int32)

    def one_block(running, block_inputs):
        key_grads, value_grads = running
        block_index, row_peak, row_total = block_inputs
        first_row = block_index * block_rows
        block_queries = lax.dynamic_slice_in_dim(queries, first_row, block_rows, 0)
        block_grads = lax.dynamic_slice_in_dim(d_attended, first_row, block_rows, 0)
        query_places = first_row + jnp.arange(block_rows, dtype=jnp.int32)
        scores = block_scores(
            block_queries, key_vectors, query_places, key_places, ending, score_scale
        )
        probabilities = jnp.exp(scores - row_peak) / row_total
        rounded_probs = probabilities.astype(jnp.bfloat16)
        d_probs = jnp.einsum(
            "qhd,khd->hqk", block_grads, values, preferred_element_type=jnp.float32
        )
        row_dot = jnp.sum(probabilities * d_probs, axis=-1, keepdims=True)
        d_scores = (probabilities * (d_probs - row_dot)).astype(jnp.bfloat16)
        query_grads = (
            jnp.einsum("hqk,khd->qhd", d_scores, key_vectors, preferred_element_type=jnp.float32)
            * score_scale
        )
        key_grads = (
            key_grads
            + jnp.einsum(
                "hqk,qhd->khd", d_scores, block_queries, preferred_element_type=jnp.float32
            )
            * score_scale
        )
        value_grads = value_grads + jnp.einsum(
            "hqk,qhd->khd", rounded_probs, block_grads, preferred_element_type=jnp.float32
        )
        return ((key_grads, value_grads), query_grads)

    zero_sums = jnp.zeros((seq_len, head_count, head_size), jnp.float32)
    block_ids = jnp.arange(seq_len // block_rows, dtype=jnp.int32)
    (key_grads, value_grads), query_grads = lax.scan(
        one_block, (zero_sums, zero_sums), (block_ids, peaks, totals)
    )
    query_grads = query_grads.reshape(seq_len, head_count, head_size)
    flipped_sine = -full_sine
    combined = jnp.stack(
        [
            rotate(query_grads, full_cosine, flipped_sine),
            rotate(key_grads, full_cosine, flipped_sine),
            value_grads,
        ],
        axis=2,
    )
    return combined.astype(jnp.bfloat16).reshape(seq_len, head_count, triple)


def collect(ln_gain, ln_bias, w_qkv, w_attn, w_in, b_in, w_out, b_out):
    return (
        lax.all_gather(ln_gain, ("batch", "seq"), axis=0, tiled=True),
        lax.all_gather(ln_bias, ("batch", "seq"), axis=0, tiled=True),
        lax.all_gather(w_qkv, ("batch", "seq"), axis=0, tiled=True),
        lax.all_gather(w_attn, ("batch", "seq"), axis=0, tiled=True),
        lax.all_gather(w_in, ("batch", "seq"), axis=0, tiled=True),
        lax.all_gather(b_in, ("batch", "seq"), axis=0, tiled=True),
        lax.all_gather(w_out, ("batch", "seq"), axis=0, tiled=True),
        lax.all_gather(b_out, ("batch", "seq"), axis=0, tiled=True),
    )


def reduce_grads(gradients):
    return (
        lax.psum_scatter(gradients[0], ("batch", "seq"), scatter_dimension=0, tiled=True),
        lax.psum_scatter(gradients[1], ("batch", "seq"), scatter_dimension=0, tiled=True),
        lax.psum_scatter(gradients[2], ("batch", "seq"), scatter_dimension=0, tiled=True),
        lax.psum_scatter(gradients[3], ("batch", "seq"), scatter_dimension=0, tiled=True),
        lax.psum_scatter(gradients[4], ("batch", "seq"), scatter_dimension=0, tiled=True),
        lax.psum_scatter(gradients[5], ("batch", "seq"), scatter_dimension=0, tiled=True),
        lax.psum_scatter(gradients[6], ("batch", "seq"), scatter_dimension=0, tiled=True),
        lax.psum_scatter(gradients[7], ("batch", "seq"), scatter_dimension=0, tiled=True),
    )


def shards(inputs, ends, ln_gain, ln_bias, w_qkv, w_attn, w_in, b_in, w_out, b_out, cotangent):
    seq_devices = lax.axis_size("seq")
    windows, local_len, model_width = inputs.shape
    seq_len = local_len * seq_devices
    per_micro = windows // MICRO
    offset = lax.axis_index("seq") * local_len
    cosine, sine_table = rotary_tables(
        (offset + jnp.arange(local_len, dtype=jnp.int32)).astype(jnp.float32)
    )
    full_cosine, full_sine = rotary_tables(jnp.arange(seq_len, dtype=jnp.float32))
    outputs = []
    input_grads = []
    shard_sums = None
    for micro_index in range(MICRO):
        gathered = collect(ln_gain, ln_bias, w_qkv, w_attn, w_in, b_in, w_out, b_out)
        (
            gain_full,
            shift_full,
            qkv_full,
            attn_full,
            in_full,
            bias_in_full,
            out_full,
            bias_out_full,
        ) = gathered
        lower = micro_index * per_micro
        row_values = inputs[lower : lower + per_micro].astype(jnp.float32)
        grad_rows = cotangent[lower : lower + per_micro]
        window_ends = ends[lower : lower + per_micro]
        normed_f, norm_pull = jax.vjp(
            layer_norm, row_values, gain_full.astype(jnp.float32), shift_full.astype(jnp.float32)
        )
        normed = normed_f.astype(jnp.bfloat16)
        projected = jnp.einsum("pld,de->ple", normed, qkv_full, preferred_element_type=jnp.float32)
        arranged = projected.reshape(per_micro, local_len, HEADS, 3, HD)
        query_rot = rotate(arranged[:, :, :, 0], cosine, sine_table)
        key_rot = rotate(arranged[:, :, :, 1], cosine, sine_table)
        packed = jnp.stack([query_rot, key_rot, arranged[:, :, :, 2]], axis=3).astype(jnp.bfloat16)
        packed = packed.reshape(per_micro, local_len, HEADS, 3 * HD)
        head_view = lax.all_to_all(packed, "seq", split_axis=2, concat_axis=1, tiled=True)
        attended, peaks, totals = lax.map(
            lambda bundle: attend_forward(bundle[0], bundle[1]), (head_view, window_ends)
        )
        position_view = lax.all_to_all(
            attended, "seq", split_axis=1, concat_axis=2, tiled=True
        ).reshape(per_micro, local_len, model_width)
        branch_attn = jnp.einsum(
            "ple,ed->pld", position_view, attn_full, preferred_element_type=jnp.float32
        )
        hidden = jnp.einsum(
            "pld,di->pli", normed, in_full, preferred_element_type=jnp.float32
        ) + bias_in_full.astype(jnp.float32)
        activ_f, gelu_pull = jax.vjp(gelu_tanh, hidden)
        activated = activ_f.astype(jnp.bfloat16)
        branch_mlp = jnp.einsum(
            "pli,id->pld", activated, out_full, preferred_element_type=jnp.float32
        ) + bias_out_full.astype(jnp.float32)
        outputs.append((row_values + branch_attn + branch_mlp).astype(jnp.bfloat16))
        grad_b_out = jnp.sum(grad_rows.astype(jnp.float32), axis=(0, 1))
        grad_w_out = jnp.einsum(
            "pli,pld->id", activated, grad_rows, preferred_element_type=jnp.float32
        )
        d_activated = jnp.einsum(
            "pld,id->pli", grad_rows, out_full, preferred_element_type=jnp.float32
        )
        d_hidden = gelu_pull(d_activated)[0].astype(jnp.bfloat16)
        grad_b_in = jnp.sum(d_hidden.astype(jnp.float32), axis=(0, 1))
        grad_w_in = jnp.einsum("pld,pli->di", normed, d_hidden, preferred_element_type=jnp.float32)
        grad_w_attn = jnp.einsum(
            "ple,pld->ed", position_view, grad_rows, preferred_element_type=jnp.float32
        )
        d_attended = jnp.einsum(
            "pld,ed->ple", grad_rows, attn_full, preferred_element_type=jnp.float32
        ).astype(jnp.bfloat16)
        d_attended = d_attended.reshape(per_micro, local_len, HEADS, HD)
        d_head_view = lax.all_to_all(d_attended, "seq", split_axis=2, concat_axis=1, tiled=True)
        d_packed = lax.map(
            lambda bundle: attend_backward(
                bundle[0], bundle[1], bundle[2], bundle[3], bundle[4], full_cosine, full_sine
            ),
            (head_view, d_head_view, peaks, totals, window_ends),
        )
        d_projected = lax.all_to_all(
            d_packed, "seq", split_axis=1, concat_axis=2, tiled=True
        ).reshape(per_micro, local_len, 3 * model_width)
        grad_w_qkv = jnp.einsum(
            "pld,ple->de", normed, d_projected, preferred_element_type=jnp.float32
        )
        d_normed = jnp.einsum("pli,di->pld", d_hidden, in_full, preferred_element_type=jnp.float32)
        d_normed = d_normed + jnp.einsum(
            "ple,de->pld", d_projected, qkv_full, preferred_element_type=jnp.float32
        )
        d_rows, grad_gain, grad_shift = norm_pull(d_normed)
        input_grads.append(grad_rows.astype(jnp.float32) + d_rows)
        local_grads = (
            grad_gain,
            grad_shift,
            grad_w_qkv,
            grad_w_attn,
            grad_w_in,
            grad_b_in,
            grad_w_out,
            grad_b_out,
        )
        reduced = reduce_grads(local_grads)
        if shard_sums is None:
            shard_sums = reduced
        else:
            shard_sums = tuple((running + extra for running, extra in zip(shard_sums, reduced)))
    output = jnp.concatenate(outputs, axis=0)
    grad_inputs = jnp.concatenate(input_grads, axis=0)
    return (
        output,
        grad_inputs,
        shard_sums[0],
        shard_sums[1],
        shard_sums[2],
        shard_sums[3],
        shard_sums[4],
        shard_sums[5],
        shard_sums[6],
        shard_sums[7],
    )


def solution(mesh):
    return jax.shard_map(
        shards,
        mesh=mesh,
        in_specs=(
            P("batch", "seq", None),
            P("batch"),
            P(("batch", "seq")),
            P(("batch", "seq")),
            P(("batch", "seq"), None),
            P(("batch", "seq"), None),
            P(("batch", "seq"), None),
            P(("batch", "seq")),
            P(("batch", "seq"), None),
            P(("batch", "seq")),
            P("batch", "seq", None),
        ),
        out_specs=(
            P("batch", "seq", None),
            P("batch", "seq", None),
            P(("batch", "seq")),
            P(("batch", "seq")),
            P(("batch", "seq"), None),
            P(("batch", "seq"), None),
            P(("batch", "seq"), None),
            P(("batch", "seq")),
            P(("batch", "seq"), None),
            P(("batch", "seq")),
        ),
        check_vma=False,
    )
```

profile of v0, /device:TPU:0, one launch (start us, length us, event | category | flops | bytes accessed | tf_op | source)
XLA Modules:
  0.0 1124.1 jit_solution(16074230412625648153)
XLA Ops:
  11.9 42.1 %all-reduce.8 = (bf16[1024]{0:T(1024)(128)(2,1)}, bf16[1024]{0:T(1024)(128)(2,1)S(1)}, bf16[1024]{0:T(1024)(128)(2,1)S(1)}) all-reduce(bf16[1024]{0:T(1024)(128)(2,1)S(1)} %dynamic-update-slice.2, bf16[1024]{0:T(1024)(128)(2,1)S(1)} %dynamic-update-slice.1, ...), channel_id=1, replica_groups=mesh['batch'=8,'seq'=4] {'batch','seq'}, use_global_device_ids=true, to_apply=%add.2 | all-reduce | flops 3072 | bytes 12288
  58.1 12.0 %all-gather.8.cloned.1.call-done = bf16[1024,1024]{1,0:T(8,128)(2,1)} async-done(((bf16[32,1024]{1,0:T(8,128)(2,1)}), bf16[1024,1024]{1,0:T(8,128)(2,1)}) %all-gather.8.cloned.1.call-update) | async-done | bytes 2097168 | tf_op jit(solution)/shard_map/all_gather | solution.py:163
  70.1 3.4 convolution_convert_fusion.1
  75.5 4.1 all-to-all-start.4
  83.3 59.3 %all-gather.6.cloned.1.call-done = bf16[1024,3072]{1,0:T(8,128)(2,1)} async-done(((bf16[32,3072]{1,0:T(8,128)(2,1)}), bf16[1024,3072]{1,0:T(8,128)(2,1)}) %all-gather.6.cloned.1.call-update) | async-done | bytes 6291472 | tf_op jit(solution)/shard_map/all_gather | solution.py:162
  142.6 8.7 copy.153
  151.3 5.1 convolution_bitcast_fusion
  161.8 4.9 fusion.88
  180.0 3.5 all-to-all-start.6
  186.8 5.5 all-to-all-done.6
  192.3 3.7 all-to-all-start
  211.6 14.0 %all-to-all-done = bf16[1,256,16,192]{1,3,0,2:T(8,128)(2,1)S(1)} async-done(((bf16[1,256,16,192]{1,3,0,2:T(8,128)(2,1)}), bf16[1,256,16,192]{1,3,0,2:T(8,128)(2,1)S(1)}, u32[]{:S(2)}, u32[]{:S(2)}) %all-to-all-start) | async-done | bytes 1572896 | tf_op jit(solution)/shard_map/all_to_all | solution.py:223
  225.6 3.6 all-to-all-start.2
  231.5 3.8 squeeze.69
  237.8 21.4 %while.104 = (s32[]{:T(128)}, bf16[2,512,4,64]{1,3,2,0:T(8,128)(2,1)}, f32[2,4,512,1]{2,1,3,0:T(4,128)S(1)}, f32[2,4,512,1]{2,1,3,0:T(4,128)S(1)}, s32[2]{0:T(12...) while((s32[]{:T(128)}, ...), condition=%wide.region_5.6_spmd.clone.clone, body=%wide.region_2.5_spmd.clone.clone.sunk | while | flops 563739136 | bytes 28917456 | solution.py:93
  244.9 3.6 fusion.274
  255.6 3.6 fusion.274
  268.8 16.1 %all-to-all-start.1 = ((bf16[4,2,32768]{2,1,0:T(2,128)(2,1)}), bf16[4,2,32768]{2,1,0:T(2,128)(2,1)}, u32[]{:S(2)}, u32[]{:S(2)}) async-start(bf16[4,2,32768]{2,1,0:T(2,128)(2,1)} %reshape.905), calls=%async_computation.1 | async-start | bytes 1048576 | tf_op jit(solution)/shard_map/all_to_all | solution.py:227
  287.0 26.2 %while.105 = (s32[]{:T(128)}, bf16[2,512,4,64]{1,3,2,0:T(8,128)(2,1)}, f32[2,4,512,1]{2,1,3,0:T(4,128)}, f32[2,4,512,1]{2,1,3,0:T(4,128)}, s32[2]{0:T(128)S(1)},...) while((s32[]{:T(128)}, ...), condition=%wide.region_11.12_spmd.clone.clone, body=%wide.region_8.11_spmd.clone.clone.sunk | while | flops 563739136 | bytes 28917964 | solution.py:93
  295.9 4.3 fusion.280
  309.0 4.3 fusion.280
  318.3 4.2 all-to-all-start.3
  322.6 64.9 %while.106 = (s32[]{:T(128)}, f32[1024,4,64]{0,2,1:T(8,128)S(1)}, f32[1024,4,64]{0,2,1:T(8,128)S(1)}, f32[2,512,4,64]{1,0,2,3:T(2,128)}, s32[2]{0:T(128)S(1)}, /...) while((s32[]{:T(128)}, f32[1024,4,64]{0,2,1:T(8,128)S(1)}, ...), condition=%wide.region_14.15_spmd.clone.clone, body=%wide.region_12.14_spmd.clone.clone.sunk | while | flops 1366163968 | bytes 161553808 | solution.py:142
  328.1 3.6 multiply_reduce_fusion.4
  339.0 10.3 dynamic_update_slice.78
  349.2 3.4 fusion.292
  360.5 3.6 multiply_reduce_fusion.4
  371.4 10.3 dynamic_update_slice.78
  381.7 3.4 fusion.292
  407.4 71.1 %while.107 = (s32[]{:T(128)}, f32[1024,4,64]{0,2,1:T(8,128)S(1)}, f32[1024,4,64]{0,2,1:T(8,128)S(1)}, f32[2,512,4,64]{1,0,3,2:T(2,128)}, s32[2]{0:T(128)S(1)}, /...) while((s32[]{:T(128)}, f32[1024,4,64]{0,2,1:T(8,128)S(1)}, ...), condition=%wide.region_19.20_spmd.clone.clone, body=%wide.region_17.19_spmd.clone.clone.sunk | while | flops 1366163968 | bytes 157359440 | solution.py:142
  414.0 4.7 multiply_reduce_fusion.5
  427.0 10.4 dynamic_update_slice.79
  437.4 3.4 fusion.306
  449.3 4.7 multiply_reduce_fusion.5
  462.4 10.4 dynamic_update_slice.79
  472.8 3.4 fusion.306
  478.6 3.2 reshape.888
  486.6 3.3 reshape.882
  498.7 5.7 copy.188
  504.4 4.6 all-to-all-start.5
  514.0 31.2 %all-to-all-done.5 = bf16[1,1024,4,192]{3,2,0,1:T(4,128)(2,1)} async-done(((bf16[1,1024,4,192]{3,2,0,1:T(4,128)(2,1)}), bf16[1,1024,4,192]{3,2,0,1:T(4,128)(2,1)}, u32[]{:S(2)}, u32[]{:S(2)}) %all-to-all-start.5) | async-done | bytes 1572896 | tf_op jit(solution)/shard_map/all_to_all | solution.py:266
  545.2 4.4 all-to-all-start.7
  549.7 4.3 copy.214
  555.4 20.0 %all-to-all-done.7 = bf16[1,1024,4,192]{3,2,0,1:T(4,128)(2,1)} async-done(((bf16[1,1024,4,192]{3,2,0,1:T(4,128)(2,1)}), bf16[1,1024,4,192]{3,2,0,1:T(4,128)(2,1)}, u32[]{:S(2)}, u32[]{:S(2)}) %all-to-all-start.7) | async-done | bytes 1572896 | tf_op jit(solution)/shard_map/all_to_all | solution.py:266
  575.4 4.1 copy.215
  583.5 6.6 convolution_add_fusion.2
  590.7 38.1 %all-gather = bf16[32,1,128]{2,1,0:T(2,128)(2,1)S(1)} all-gather(bf16[1,1,128]{2,1,0:T(2,128)(2,1)S(1)} %bitcast.426), channel_id=1, replica_groups=mesh['batch'=8,'seq'=4] {'batch','seq'}, dimensions={0}, use_global_device_ids=true | all-gather | bytes 8448 | tf_op jit(solution)/shard_map/all_gather | solution.py:165
  628.9 8.5 convolution_add_fusion.4
  637.4 8.8 convert_reduce_fusion.1
  650.2 5.9 convolution_add_fusion.3
  656.1 10.9 convert_reduce_fusion
  667.0 10.2 convolution_add_fusion.1
  677.2 10.9 fusion.128
  688.1 11.5 %convolution_add_fusion = f32[4096,1024]{1,0:T(8,128)} fusion(f32[4096,1024]{1,0:T(8,128)} %fusion.128, bf16[2,256,1024]{2,1,0:T(8,128)(2,1)S(1)} %copy-done.27, f32[256,4096]{1,0:T(8,128)S(1)} %copy-done.23), kind=kOutput, calls=%fused_computation.102 | convolution fusion | flops 2161115136 | bytes 38273024 | tf_op jit(solution)/shard_map/pli,pld->id/dot_general | solution.py:243
  700.3 6.5 fusion.187
  706.8 4.8 fusion.185
  711.7 6.2 fusion.186
  717.9 3.1 fusion.116
  725.0 3.8 convert_reduce_fusion.4
  728.8 40.2 %all-reduce.7 = (f32[1024]{0:T(1024)S(1)}, f32[1024]{0:T(1024)S(1)}, f32[4096]{0:T(1024)S(1)}, f32[1024]{0:T(1024)S(1)}) all-reduce(f32[1024]{0:T(1024)S(1)} %add.377, f32[1024]{0:T(1024)S(1)} %add.378, f32[4096]{0:T(1024)S(1)} %add.382, f32[1024]{0:T(1024)S(1)} %add.384), channel_id=10, replica_groups=mesh['batch'=8,'seq'=4] {'batch','seq'}, use_global_device_ids=true, to_apply=%region_23.24.clone | all-reduce | flops 7168 | bytes 57344
  771.3 7.6 fusion.102
  781.2 6.2 fusion.101
  790.7 138.9 %reduce-scatter.9.cloned.1.call-done = f32[32,4096]{1,0:T(8,128)} async-done(((f32[1024,4096]{1,0:T(8,128)}), f32[32,4096]{1,0:T(8,128)}) %reduce-scatter.9.cloned.1.call-update) | async-done | bytes 524304 | tf_op jit(solution)/shard_map/reduce_scatter | solution.py:177
  929.6 187.5 %reduce-scatter.11.cloned.1.call-done = f32[128,1024]{1,0:T(8,128)} async-done(((f32[4096,1024]{1,0:T(8,128)}), f32[128,1024]{1,0:T(8,128)}) %reduce-scatter.11.cloned.1.call-update) | async-done | bytes 524304 | tf_op jit(solution)/shard_map/reduce_scatter | solution.py:179
  (430 shorter events, 224.3 us)
Async XLA Ops:
  7.2 72.5 %copy-start.25 = (bf16[2,256,1024]{2,1,0:T(8,128)(2,1)S(1)}, bf16[2,256,1024]{2,1,0:T(8,128)(2,1)}, u32[]{:S(2)}) copy-start(bf16[2,256,1024]{2,1,0:T(8,128)(2,1)} %param.29) | copy-start | bytes 3145732
  7.2 62.9 %all-gather.8.cloned.1.call-start = ((), (), s32[]{:S(2)}) async-start(), calls=%async_computation.13 | async-start | bytes 2162688 | tf_op jit(solution)/shard_map/all_gather | solution.py:163
  7.9 134.6 %all-gather.6.cloned.1.call-start = ((), (), s32[]{:S(2)}) async-start(), calls=%async_computation.12 | async-start | bytes 6488064 | tf_op jit(solution)/shard_map/all_gather | solution.py:162
  8.7 620.2 %all-gather.10.cloned.1.call-start = ((), (), s32[]{:S(2)}) async-start(), calls=%async_computation.14 | async-start | bytes 8650752 | tf_op jit(solution)/shard_map/all_gather | solution.py:164
  54.0 107.8 %copy-start.47 = (f32[1024]{0:T(1024)}, f32[1024]{0:T(1024)S(1)}, u32[]{:S(2)}) copy-start(f32[1024]{0:T(1024)S(1)} %convert_element_type.162) | copy-start | bytes 12292
  54.0 107.7 %copy-start.49 = (f32[1024]{0:T(1024)}, f32[1024]{0:T(1024)S(1)}, u32[]{:S(2)}) copy-start(f32[1024]{0:T(1024)S(1)} %convert_element_type.163) | copy-start | bytes 12292
  55.7 95.6 %copy-start.61 = (f32[256]{0:T(256)}, f32[256]{0:T(256)S(1)}, u32[]{:S(2)}) copy-start(f32[256]{0:T(256)S(1)} %get-tuple-element.777) | copy-start | bytes 3076
  55.7 106.1 %copy-start.65 = (f32[256]{0:T(256)}, f32[256]{0:T(256)S(1)}, u32[]{:S(2)}) copy-start(f32[256]{0:T(256)S(1)} %get-tuple-element.776) | copy-start | bytes 3076
  57.3 24.0 %copy-start.69 = (f32[256]{0:T(256)}, f32[256]{0:T(256)S(1)}, u32[]{:S(2)}) copy-start(f32[256]{0:T(256)S(1)} %get-tuple-element.610) | copy-start | bytes 3076
  57.3 24.0 %copy-start.71 = (f32[256]{0:T(256)}, f32[256]{0:T(256)S(1)}, u32[]{:S(2)}) copy-start(f32[256]{0:T(256)S(1)} %get-tuple-element.611) | copy-start | bytes 3076
  57.3 94.0 %copy-start.63 = (f32[256]{0:T(256)}, f32[256]{0:T(256)S(1)}, u32[]{:S(2)}) copy-start(f32[256]{0:T(256)S(1)} %fusion.170) | copy-start | bytes 3076
  57.3 104.4 %copy-start.67 = (f32[256]{0:T(256)}, f32[256]{0:T(256)S(1)}, u32[]{:S(2)}) copy-start(f32[256]{0:T(256)S(1)} %fusion.171) | copy-start | bytes 3076
  70.1 9.6 copy-start.28
  75.5 104.5 %all-to-all-start.4 = ((bf16[1,256,16,64]{1,3,0,2:T(8,128)(2,1)}), bf16[1,256,16,64]{1,3,0,2:T(8,128)(2,1)}, u32[]{:S(2)}, u32[]{:S(2)}) async-start(bf16[1,256,16,64]{1,3,0,2:T(8,128)(2,1)} %bitcast.414), calls=%async_computation.4 | async-start | bytes 1048576 | tf_op jit(solution)/shard_map/all_to_all | solution.py:259
  142.6 8.7 copy-start.10
  168.5 8.4 copy-start.51
  178.9 5.6 copy-start.53
  180.0 12.3 %all-to-all-start.6 = ((bf16[1,256,16,64]{1,3,0,2:T(8,128)(2,1)}), bf16[1,256,16,64]{1,3,0,2:T(8,128)(2,1)S(1)}, u32[]{:S(2)}, u32[]{:S(2)}) async-start(bf16[1,256,16,64]{1,3,0,2:T(8,128)(2,1)} %bitcast.75), calls=%async_computation.6 | async-start | bytes 1048576 | tf_op jit(solution)/shard_map/all_to_all | solution.py:259
  183.5 13.2 %copy-start.74 = (s32[2]{0:T(128)S(1)}, s32[2]{0:T(128)}, u32[]{:S(2)}) copy-start(s32[2]{0:T(128)} %param.20) | copy-start | bytes 28
  192.3 16.2 %copy-start.55 = (bf16[1,256,16,16,1]{1,3,2,4,0:T(8,128)(2,1)S(1)}, bf16[1,256,16,16,1]{1,3,2,4,0:T(8,128)(2,1)}, u32[]{:S(2)}) copy-start(bf16[1,256,16,16,1]{1,3,2,4,0:T(8,128)(2,1)} %get-tuple-element.759) | copy-start | bytes 393220
  192.3 33.2 %all-to-all-start = ((bf16[1,256,16,192]{1,3,0,2:T(8,128)(2,1)}), bf16[1,256,16,192]{1,3,0,2:T(8,128)(2,1)S(1)}, u32[]{:S(2)}, u32[]{:S(2)}) async-start(bf16[1,256,16,192]{1,3,0,2:T(8,128)(2,1)} %bitcast.19), calls=%async_computation | async-start | bytes 3145728 | tf_op jit(solution)/shard_map/all_to_all | solution.py:223
  196.0 13.8 %copy-start.54 = (bf16[1,256,16,16,1]{1,3,2,4,0:T(8,128)(2,1)S(1)}, bf16[1,256,16,16,1]{1,3,2,4,0:T(8,128)(2,1)}, u32[]{:S(2)}) copy-start(bf16[1,256,16,16,1]{1,3,2,4,0:T(8,128)(2,1)} %get-tuple-element.762) | copy-start | bytes 393220
  196.0 441.4 %all-gather.12.cloned.1.call-start = ((), (), s32[]{:S(2)}) async-start(), calls=%async_computation.15 | async-start | bytes 8650752 | tf_op jit(solution)/shard_map/all_gather | solution.py:166
  225.6 33.6 %all-to-all-start.2 = ((bf16[1,256,16,192]{1,3,0,2:T(8,128)(2,1)}), bf16[1,256,16,192]{1,3,0,2:T(8,128)(2,1)S(1)}, u32[]{:S(2)}, u32[]{:S(2)}) async-start(bf16[1,256,16,192]{1,3,0,2:T(8,128)(2,1)} %bitcast.44), calls=%async_computation.2 | async-start | bytes 3145728 | tf_op jit(solution)/shard_map/all_to_all | solution.py:223
  259.1 6.5 copy-start.20
  259.1 27.9 %copy-start.19 = (bf16[1024,4,64]{0,2,1:T(8,128)(2,1)}, bf16[1024,4,64]{0,2,1:T(8,128)(2,1)S(1)}, u32[]{:S(2)}) copy-start(bf16[1024,4,64]{0,2,1:T(8,128)(2,1)S(1)} %get-tuple-element.1272) | copy-start | bytes 1572868
  268.8 49.5 %all-to-all-start.1 = ((bf16[4,2,32768]{2,1,0:T(2,128)(2,1)}), bf16[4,2,32768]{2,1,0:T(2,128)(2,1)}, u32[]{:S(2)}, u32[]{:S(2)}) async-start(bf16[4,2,32768]{2,1,0:T(2,128)(2,1)} %reshape.905), calls=%async_computation.1 | async-start | bytes 1048576 | tf_op jit(solution)/shard_map/all_to_all | solution.py:227
  313.3 9.2 copy-start.7
  313.3 9.3 copy-start.13
  313.3 9.3 copy-start.17
  318.3 76.5 %all-to-all-start.3 = ((bf16[4,2,32768]{2,1,0:T(2,128)(2,1)}), bf16[4,2,32768]{2,1,0:T(2,128)(2,1)}, u32[]{:S(2)}, u32[]{:S(2)}) async-start(bf16[4,2,32768]{2,1,0:T(2,128)(2,1)} %reshape.903), calls=%async_computation.3 | async-start | bytes 1048576 | tf_op jit(solution)/shard_map/all_to_all | solution.py:227
  322.5 468.3 %reduce-scatter.7.cloned.1.call-start = ((), (), s32[]{:S(2)}) async-start(), calls=%async_computation.17 | async-start | bytes 4325376 | tf_op jit(solution)/shard_map/reduce_scatter | solution.py:176
  349.2 4.8 copy-start.18
  381.7 4.8 copy-start.18
  387.5 13.6 %copy-start.8 = (f32[1024,4,64]{0,2,1:T(8,128)}, f32[1024,4,64]{0,2,1:T(8,128)S(1)}, u32[]{:S(2)}) copy-start(f32[1024,4,64]{0,2,1:T(8,128)S(1)} %get-tuple-element.1256) | copy-start | bytes 3145732
  387.5 13.6 %copy-start.14 = (f32[1024,4,64]{0,2,1:T(8,128)}, f32[1024,4,64]{0,2,1:T(8,128)S(1)}, u32[]{:S(2)}) copy-start(f32[1024,4,64]{0,2,1:T(8,128)S(1)} %get-tuple-element.1257) | copy-start | bytes 3145732
  387.5 13.6 %copy-start.26 = (bf16[2,256,1024]{2,1,0:T(8,128)(2,1)S(1)}, bf16[2,256,1024]{2,1,0:T(8,128)(2,1)}, u32[]{:S(2)}) copy-start(bf16[2,256,1024]{2,1,0:T(8,128)(2,1)} %param.29) | copy-start | bytes 3145732
  437.4 4.8 copy-start.5
  478.6 12.6 %copy-start.9 = (f32[1024,4,64]{0,2,1:T(8,128)S(1)}, f32[1024,4,64]{0,2,1:T(8,128)}, u32[]{:S(2)}) copy-start(f32[1024,4,64]{0,2,1:T(8,128)} %copy-done.8) | copy-start | bytes 3145732
  498.7 11.4 %copy-start.57 = (bf16[1024,4,16,1]{0,1,2,3:T(4,128)(2,1)S(1)}, bf16[1024,4,16,1]{0,1,2,3:T(4,128)(2,1)}, u32[]{:S(2)}) copy-start(bf16[1024,4,16,1]{0,1,2,3:T(4,128)(2,1)} %get-tuple-element.735) | copy-start | bytes 393220
  498.7 11.4 %copy-start.58 = (bf16[1024,4,16,1]{0,1,2,3:T(4,128)(2,1)S(1)}, bf16[1024,4,16,1]{0,1,2,3:T(4,128)(2,1)}, u32[]{:S(2)}) copy-start(bf16[1024,4,16,1]{0,1,2,3:T(4,128)(2,1)} %get-tuple-element.736) | copy-start | bytes 393220
  504.4 6.1 copy-start.56
  504.4 40.8 %all-to-all-start.5 = ((bf16[1,1024,4,192]{3,2,0,1:T(4,128)(2,1)}), bf16[1,1024,4,192]{3,2,0,1:T(4,128)(2,1)}, u32[]{:S(2)}, u32[]{:S(2)}) async-start(bf16[1,1024,4,192]{3,2,0,1:T(4,128)(2,1)} %copy.188), calls=%async_computation.5 | async-start | bytes 4194304 | tf_op jit(solution)/shard_map/all_to_all | solution.py:266
  545.2 30.2 %all-to-all-start.7 = ((bf16[1,1024,4,192]{3,2,0,1:T(4,128)(2,1)}), bf16[1,1024,4,192]{3,2,0,1:T(4,128)(2,1)}, u32[]{:S(2)}, u32[]{:S(2)}) async-start(bf16[1,1024,4,192]{3,2,0,1:T(4,128)(2,1)} %copy.202), calls=%async_computation.7 | async-start | bytes 4194304 | tf_op jit(solution)/shard_map/all_to_all | solution.py:266
  549.6 241.1 %reduce-scatter.5.cloned.1.call-start = ((), (), s32[]{:S(2)}) async-start(), calls=%async_computation.16 | async-start | bytes 12976128 | tf_op jit(solution)/shard_map/reduce_scatter | solution.py:175
  555.4 24.4 %copy-start.11 = (bf16[2,256,1024]{2,1,0:T(8,128)(2,1)S(1)}, bf16[2,256,1024]{2,1,0:T(8,128)(2,1)}, u32[]{:S(2)}) copy-start(bf16[2,256,1024]{2,1,0:T(8,128)(2,1)} %param.19) | copy-start | bytes 3145732
  555.4 24.4 %copy-start.48 = (f32[1024]{0:T(1024)S(1)}, f32[1024]{0:T(1024)}, u32[]{:S(2)}) copy-start(f32[1024]{0:T(1024)} %copy-done.47) | copy-start | bytes 12292
  555.4 24.4 %copy-start.50 = (f32[1024]{0:T(1024)S(1)}, f32[1024]{0:T(1024)}, u32[]{:S(2)}) copy-start(f32[1024]{0:T(1024)} %copy-done.49) | copy-start | bytes 12292
  555.4 24.4 %copy-start.62 = (f32[256]{0:T(256)S(1)}, f32[256]{0:T(256)}, u32[]{:S(2)}) copy-start(f32[256]{0:T(256)} %copy-done.61) | copy-start | bytes 3076
  555.4 24.4 %copy-start.64 = (f32[256]{0:T(256)S(1)}, f32[256]{0:T(256)}, u32[]{:S(2)}) copy-start(f32[256]{0:T(256)} %copy-done.63) | copy-start | bytes 3076
  590.1 339.5 %reduce-scatter.9.cloned.1.call-start = ((), (), s32[]{:S(2)}) async-start(), calls=%async_computation.18 | async-start | bytes 17301504 | tf_op jit(solution)/shard_map/reduce_scatter | solution.py:177
  628.9 8.5 copy-start.27
  656.1 10.9 copy-start.22
  677.2 439.9 %reduce-scatter.11.cloned.1.call-start = ((), (), s32[]{:S(2)}) async-start(), calls=%async_computation.19 | async-start | bytes 17301504 | tf_op jit(solution)/shard_map/reduce_scatter | solution.py:179
  677.2 10.9 copy-start.23
  700.3 6.5 copy-start.34
  706.8 4.8 copy-start.46
  706.8 11.1 slice-start
  711.7 6.2 copy-start.37
  711.7 6.2 slice-start.1
  711.7 6.2 copy-start.32
  771.3 7.6 copy-start.29
  771.3 7.6 copy-start.30
  781.2 6.2 copy-start.36
  (39 other events, 100.9 us)
Sparse Core Ops, SparseCore 0:
  10.9 59.1 all-gather.7
  72.9 69.5 all-gather.5
  145.4 84.9 all-gather.9
  233.1 85.5 all-gather.11
  405.9 143.0 reduce-scatter.6
  590.2 153.8 reduce-scatter.4
  747.1 182.4 reduce-scatter.8
  932.6 184.4 reduce-scatter.10
where the time goes:
time: 1130 us; the launch traced here: 1120 us
  waiting for transfers between devices  471 us (42%)
  matrix products  209 us (18%)
  local copies, waits for them, and re-layouts  202 us (18%)
  blocking collectives  120 us (11%)
  other arithmetic  55.1 us (5%)
  starting transfers between devices  44.8 us (4%)
  between operations  16 us (1%)
    reduce_scatter x1, waiting for transfers between devices, reduce_grads(): lax.psum_scatter(gradients[6], ('batch', 'seq'), scatter_dimension=0, til...  187 us
    reduce_scatter x1, waiting for transfers between devices, reduce_grads(): lax.psum_scatter(gradients[4], ('batch', 'seq'), scatter_dimension=0, til...  139 us
    unnamed x2, blocking collectives  82.3 us
    all_gather x1, waiting for transfers between devices, collect(): lax.all_gather(w_qkv, ('batch', 'seq'), axis=0, tiled=True)  59.3 us
    all_to_all x2, waiting for transfers between devices, shards(): lax.all_to_all(d_packed, 'seq', split_axis=1, concat_axis=2, tiled=True)  51.1 us
    dynamic_update_slice x8, local copies, waits for them, and re-layouts, attend_backward(): lax.scan(one_block, (zero_sums, zero_sums), (block_ids, peaks, totals))  43.5 us
    all_gather x1, blocking collectives, collect(): lax.all_gather(b_in, ('batch', 'seq'), axis=0, tiled=True)  38.1 us
    unnamed x155, local copies, waits for them, and re-layouts  27.4 us
  transfers between devices with their start and end apart: 16, of which 8 were waited for; matrix products, arithmetic and copies ran while one was open for 38% of the time, Pallas kernels for 0%

commit v1 on v0

--- a/solution.py
+++ b/solution.py
@@ -2,7 +2,10 @@
 
 import jax
 import jax.numpy as jnp
+import numpy as np
 from jax import lax
+from jax.experimental import pallas as pl
+from jax.experimental.pallas import tpu as pltpu
 from jax.sharding import PartitionSpec as P
 
 HEADS = 16
@@ -306,9 +309,797 @@
     )
 
 
+HB, SB = 4, 4
+NEG = -1e30
+BF, F32 = jnp.bfloat16, jnp.float32
+MESH = pl.DeviceIdType.MESH
+
+
+def dot(a, b, ca, cb):
+    return lax.dot_general(a, b, (((ca,), (cb,)), ((), ())), preferred_element_type=F32)
+
+
+def rows(start, size):
+    return pl.ds(pl.multiple_of(start, size), size)
+
+
+def lanes(start, size=128):
+    return pl.ds(pl.multiple_of(start, size), size)
+
+
+def halves(low_source, high_source):
+    def piece(source, upper):
+        array, first = source
+        tile = array[:, first // 128 * 128 : first // 128 * 128 + 128]
+        return pltpu.roll(tile, 64, 1) if (first % 128 == 64) != upper else tile
+
+    lane = lax.broadcasted_iota(jnp.int32, (1, 128), 1)
+    return jnp.where(lane < 64, piece(low_source, False), piece(high_source, True))
+
+
+def head_of(owner, j):
+    return 4 * j + 2 * (owner % 2) + owner // 2
+
+
+class Link:
+    def __init__(self, send_sems, recv_sems):
+        self.send_sems, self.recv_sems = send_sems, recv_sems
+        self.first = {}
+        self.used = 0
+
+    def index(self, name, at, count):
+        if name not in self.first:
+            self.first[name] = self.used
+            self.used += count
+        return self.first[name] + at
+
+    def copy(self, name, at, count, src, dst, device):
+        i = self.index(name, at, count)
+        return pltpu.make_async_remote_copy(
+            src_ref=src,
+            dst_ref=dst,
+            send_sem=self.send_sems.at[i],
+            recv_sem=self.recv_sems.at[i],
+            device_id=device,
+            device_id_type=MESH,
+        )
+
+
+def gelu_pair(v):
+    cube = v * v
+    t = jnp.tanh(gelu_factor * (v + 0.044715 * (v * cube)))
+    half = 0.5 * (1.0 + t)
+    slope = half + 0.5 * v * (1.0 - t * t) * (gelu_factor * (1.0 + (3 * 0.044715) * cube))
+    return v * half, slope
+
+
+def fused_layer(
+    ends, prm, wq, wa, wi, wo, cosine, sine, x_in, g_in,
+    out, grad_in, grad_q, grad_a, grad_i, grad_o, grad_small, grad_bin,
+    X, N, G, A, H, Wi, Wo, Wq, WaAll, Wa, PWI, PWQ, PRM, PR, QKV, att, dO,
+    GO, XO, ZO, GI, XI, ZI, GQ, XQ, ZQ, GA, XA, ZA, GAS, GT, XT, ZT,
+    YR, SWI, RWI, SWQ, RWQ, TAIL,
+    khat, ktT, vtT, doT, oT, dqT, dkA, dvA,
+    send_sems, recv_sems, local_sems,
+):
+    b = lax.axis_index("batch")
+    s = lax.axis_index("seq")
+    z, xx = b // 2, b % 2
+    y, c = s // 2, s % 2
+    oc, ox, oy = 1 - c, 1 - xx, 1 - y
+    SL = 256
+    S = 1024
+    core = (b, 2 * y + oc)
+    ypart = (b, 2 * oy + c)
+    diag = (b, 2 * oy + oc)
+    xpart = (2 * z + ox, s)
+
+    def zdev(k):
+        return (2 * ((z + k) % 4) + xx, s)
+
+    def zfrom(k):
+        return (z + 4 - k) % 4
+
+    link = Link(send_sems, recv_sems)
+    pending = []
+
+    def start(make):
+        make().start()
+        pending.append(make)
+
+    own = rows(SL * s, SL)
+    locals_ = []
+    for w in range(2):
+        locals_.append(pltpu.make_async_copy(x_in.at[w], X.at[w, own], local_sems.at[3 * w]))
+        locals_.append(pltpu.make_async_copy(g_in.at[w], G.at[w, own], local_sems.at[3 * w + 1]))
+    for cp in locals_:
+        cp.start()
+
+    for r in range(SB):
+        for blk in range(8):
+            PWI[r, :, 128 * blk : 128 * blk + 128] = wi[:, 512 * blk + 128 * r : 512 * blk + 128 * r + 128]
+    wq_f = wq[...].astype(F32)
+    for r in range(SB):
+        for kind in range(3):
+            for p in range(2):
+                lo = 192 * head_of(r, 2 * p) + 64 * kind
+                hi = 192 * head_of(r, 2 * p + 1) + 64 * kind
+                at = 256 * kind + 128 * p
+                PWQ[r, :, at : at + 128] = halves((wq_f, lo), (wq_f, hi)).astype(BF)
+    tile = prm[...].astype(F32)
+    row = lax.broadcasted_iota(jnp.int32, (16, 128), 0)
+    tile = jnp.where(row < 3, pltpu.roll(tile, 32 * s, 1), tile)
+    PRM[b, rows(16 * s, 16), :] = tile.astype(BF)
+    Wi[rows(128 * b + 32 * s, 32), :] = PWI[s]
+    Wq[rows(128 * b + 32 * s, 32), :] = PWQ[s]
+    Wo[rows(128 * b, 128), :] = wo[...]
+    WaAll[z, xx] = wa[...]
+
+    barrier = pltpu.get_barrier_semaphore()
+    partners = [core, ypart, diag, xpart] + [zdev(k) for k in (1, 2, 3)]
+    for device in partners:
+        pl.semaphore_signal(barrier, inc=1, device_id=device, device_id_type=MESH)
+    pl.semaphore_wait(barrier, len(partners))
+
+    def seq_sends(name, src_of, dst):
+        for i, (device, owner) in enumerate(
+            ((core, 2 * y + oc), (ypart, 2 * oy + c), (diag, 2 * oy + oc))
+        ):
+            start(
+                lambda i=i, device=device, owner=owner: link.copy(
+                    name, i, 3, src_of(owner), dst(), device
+                )
+            )
+
+    def seq_waits(name, src, dst_of):
+        for i, owner in enumerate((2 * y + oc, 2 * oy + c, 2 * oy + oc)):
+            link.copy(name, i, 3, src, dst_of(owner), core).wait_recv()
+
+    def prm_block(owner):
+        return PRM.at[b, rows(16 * owner, 16)]
+
+    def wi_block(owner):
+        return Wi.at[rows(128 * b + 32 * owner, 32)]
+
+    def wq_block(owner):
+        return Wq.at[rows(128 * b + 32 * owner, 32)]
+
+    gathers = {
+        "prm": lambda bb: PRM.at[bb],
+        "wa": lambda bb: WaAll.at[bb // 2, bb % 2],
+        "wi": lambda bb: Wi.at[rows(128 * bb, 128)],
+        "wo": lambda bb: Wo.at[rows(128 * bb, 128)],
+        "wq": lambda bb: Wq.at[rows(128 * bb, 128)],
+    }
+
+    def gather_start(name):
+        block = gathers[name]
+        for k in (1, 2, 3):
+            start(lambda k=k: link.copy(name + "z", k - 1, 3, block(b), block(b), zdev(k)))
+        start(lambda: link.copy(name + "x", 0, 4, block(b), block(b), xpart))
+
+    def gather_pass(name, k):
+        block = gathers[name]
+        bb = 2 * zfrom(k) + xx
+        link.copy(name + "z", k - 1, 3, block(bb), block(bb), core).wait_recv()
+
+        def make():
+            held = block(2 * zfrom(k) + xx)
+            return link.copy(name + "x", k, 4, held, held, xpart)
+
+        start(make)
+
+    def gather_end(name, ks=(0, 1, 2, 3)):
+        block = gathers[name]
+        for k in ks:
+            bb = 2 * zfrom(k) + ox
+            link.copy(name + "x", k, 4, block(bb), block(bb), core).wait_recv()
+
+    seq_sends("prms", lambda owner: prm_block(s), lambda: prm_block(s))
+    seq_sends("wis", lambda owner: PWI.at[owner], lambda: wi_block(s))
+    gather_start("wa")
+    seq_sends("wqs", lambda owner: PWQ.at[owner], lambda: wq_block(s))
+
+    def rows_start(name, src, dst):
+        for w in range(2):
+            start(lambda w=w: link.copy(name + "c", w, 2, src.at[w], dst.at[w, own], core))
+            start(lambda w=w: link.copy(name + "y", w, 2, src.at[w], dst.at[w, own], ypart))
+
+    def rows_pass(name, dst, w):
+        block = dst.at[w, rows(SL * (2 * oy + c), SL)]
+        link.copy(name + "y", w, 2, block, block, core).wait_recv()
+        link.copy(name + "f", w, 2, block, block, core).start()
+
+    def rows_left(name, dst, w):
+        block = dst.at[w, rows(SL * (2 * oy + c), SL)]
+        link.copy(name + "f", w, 2, block, block, core).wait_send()
+
+    def rows_end_core(name, dst, w):
+        block = dst.at[w, rows(SL * (2 * y + oc), SL)]
+        link.copy(name + "c", w, 2, block, block, core).wait_recv()
+
+    def rows_end_far(name, dst, w):
+        block = dst.at[w, rows(SL * (2 * oy + oc), SL)]
+        link.copy(name + "f", w, 2, block, block, core).wait_recv()
+
+    rows_start("x", x_in, X)
+    seq_waits("prms", PRM.at[b, rows(16 * s, 16)], prm_block)
+    gather_start("prm")
+    seq_waits("wis", PWI.at[0], wi_block)
+    gather_start("wi")
+    for k in (1, 2, 3):
+        gather_pass("prm", k)
+    for k in (1, 2, 3):
+        gather_pass("wa", k)
+    gather_end("prm")
+
+    for bb in range(8):
+        total = (
+            PRM[bb, 0:16, :].astype(F32)
+            + PRM[bb, 16:32, :].astype(F32)
+            + PRM[bb, 32:48, :].astype(F32)
+            + PRM[bb, 48:64, :].astype(F32)
+        )
+        mine = PRM[bb, rows(16 * s, 16), :].astype(F32)
+        PR[:, 128 * bb : 128 * bb + 128] = jnp.where(row < 3, total, mine)[0:8]
+
+    for cp in locals_:
+        cp.wait()
+
+    def norm_rows(w, owner):
+        r = rows(SL * owner, SL)
+        v = X[w, r, :].astype(F32)
+        v = v - jnp.mean(v, axis=-1, keepdims=True)
+        var = jnp.mean(v * v, axis=-1, keepdims=True)
+        N[w, r, :] = (v * lax.rsqrt(var + norm_eps) * PR[0:1, :] + PR[1:2, :]).astype(BF)
+
+    def norm_own(w, carry):
+        norm_rows(w, s)
+        norm_rows(w, 2 * y + oc)
+        return carry
+
+    def norm_far(w, carry):
+        norm_rows(w, 2 * oy + c)
+        norm_rows(w, 2 * oy + oc)
+        return carry
+
+    for w in range(2):
+        rows_end_core("x", X, w)
+    lax.fori_loop(0, 2, norm_own, 0)
+    gather_pass("wi", 1)
+    for w in range(2):
+        rows_pass("x", X, w)
+    rows_start("g", g_in, G)
+    gather_pass("wi", 2)
+    gather_pass("wi", 3)
+    gather_start("wo")
+    for w in range(2):
+        rows_end_far("x", X, w)
+    lax.fori_loop(0, 2, norm_far, 0)
+    gather_end("wi")
+
+    def hidden_step(i, carry):
+        w, t, u = i // 8, (i // 4) % 2, i % 4
+        r, l = rows(512 * t, 512), lanes(256 * u, 256)
+        v = dot(N[w, r, :], Wi[:, l], 1, 0) + PR[3:4, l]
+        value, slope = gelu_pair(v)
+        A[w, r, l] = value.astype(BF)
+        H[w, r, l] = slope.astype(BF)
+
+        @pl.when(i == 3)
+        def _():
+            gather_pass("wo", 1)
+
+        @pl.when(i == 7)
+        def _():
+            gather_pass("wo", 2)
+
+        @pl.when(i == 11)
+        def _():
+            gather_pass("wo", 3)
+            seq_waits("wqs", PWQ.at[0], wq_block)
+            gather_start("wq")
+
+        return carry
+
+    lax.fori_loop(0, 16, hidden_step, 0)
+    for w in range(2):
+        rows_end_core("g", G, w)
+        rows_pass("g", G, w)
+    for w in range(2):
+        rows_end_far("g", G, w)
+    gather_end("wo")
+    gather_end("wa")
+    for w in range(2):
+        rows_left("x", X, w)
+    start(lambda: link.copy("wac", 0, 1, WaAll.at[:, oc], Wa.at[:, c], core))
+    Wa[:, c] = WaAll[:, c]
+
+    sums = {"o": (GO, XO, ZO), "i": (GI, XI, ZI), "q": (GQ, XQ, ZQ), "a": (GA, XA, ZA), "t": (GT, XT, ZT)}
+
+    def add_into(dst, other):
+        dst[...] = (dst[...].astype(F32) + other[...].astype(F32)).astype(BF)
+
+    def o_z(q):
+        link.copy("ox", q, 4, XO.at[q], XO.at[q], core).wait_recv()
+
+        @pl.when(z != q)
+        def _():
+            add_into(GO.at[q, xx], XO.at[q])
+            k = (q + 4 - z) % 4
+            link.copy("oz", k - 1, 3, GO.at[q, xx], ZO.at[k - 1], (2 * q + xx, s)).start()
+
+    def i_z(q):
+        link.copy("ix", q, 4, XI.at[q], XI.at[q], core).wait_recv()
+        for k in (1, 2, 3):
+            zz = (z + k) % 4
+            add_into(GI.at[q, xx, zz], XI.at[q, zz])
+            link.copy("iz", 3 * q + k - 1, 12, GI.at[q, xx, zz], ZI.at[k - 1, q], zdev(k)).start()
+
+    def back_step(q, carry):
+        l = lanes(256 * q, 256)
+
+        def dh_step(i, total):
+            w, r = i // 2, rows(512 * (i % 2), 512)
+            d = dot(G[w, r, :], Wo[rows(256 * q, 256), :], 1, 1) * H[w, r, l].astype(F32)
+            d = d.astype(BF)
+            H[w, r, l] = d
+            return total + jnp.sum(d.astype(F32), axis=0, keepdims=True)
+
+        TAIL[3:4, l] = lax.fori_loop(0, 4, dh_step, jnp.zeros((1, 256), F32))
+        go = dot(A[0, :, l], G[0], 0, 0) + dot(A[1, :, l], G[1], 0, 0)
+        GO[q, 0] = go[:128].astype(BF)
+        GO[q, 1] = go[128:].astype(BF)
+        link.copy("ox", q, 4, GO.at[q, ox], XO.at[q], xpart).start()
+        gi = dot(H[0, :, l], N[0], 0, 0) + dot(H[1, :, l], N[1], 0, 0)
+        for bb in range(8):
+            GI[q, bb % 2, bb // 2] = gi[:, 128 * bb : 128 * bb + 128].astype(BF)
+        link.copy("ix", q, 4, GI.at[q, ox], XI.at[q], xpart).start()
+
+        @pl.when(q == 0)
+        def _():
+            gather_pass("wq", 1)
+
+        @pl.when(q == 1)
+        def _():
+            gather_pass("wq", 2)
+
+        @pl.when(q == 2)
+        def _():
+            gather_pass("wq", 3)
+
+        @pl.when(q > 0)
+        def _():
+            o_z(q - 1)
+            i_z(q - 1)
+
+        return carry
+
+    TAIL[...] = jnp.zeros_like(TAIL)
+    lax.fori_loop(0, 4, back_step, 0)
+
+    gather_end("wq")
+    link.copy("wac", 0, 1, WaAll.at[:, oc], Wa.at[:, oc], core).wait_recv()
+    even = lax.broadcasted_iota(jnp.int32, (1, 128), 1) % 2 == 0
+
+    def turn(v, cos_rows, sin_rows):
+        swapped = jnp.where(even, pltpu.roll(v, 127, 1), pltpu.roll(v, 1, 1))
+        return v * cos_rows + swapped * sin_rows
+
+    def qkv_step(i, total):
+        w, r = i // 4, rows(256 * (i % 4), 256)
+        n = N[w, r, :]
+        cos_rows, sin_rows = cosine[r, :], sine[r, :]
+        for kind in range(3):
+            v = dot(n, Wq[:, 256 * kind : 256 * kind + 256], 1, 0)
+            for p in range(2):
+                tile_v = v[:, 128 * p : 128 * p + 128]
+                if kind < 2:
+                    tile_v = turn(tile_v, cos_rows, sin_rows)
+                if kind == 0:
+                    tile_v = tile_v * 0.125
+                QKV[w, r, 256 * kind + 128 * p : 256 * kind + 128 * p + 128] = tile_v.astype(BF)
+        g = G[w, r, :]
+        dO[w, r, :] = dot(g, Wa[...].reshape(256, 1024), 1, 1).astype(BF)
+        return total + jnp.sum(g.astype(F32), axis=0, keepdims=True)
+
+    TAIL[2:3, :] = lax.fori_loop(0, 8, qkv_step, jnp.zeros((1, 1024), F32))
+    o_z(3)
+    i_z(3)
+
+    lane = lax.broadcasted_iota(jnp.int32, (1, 128), 1)
+    place = lax.broadcasted_iota(jnp.int32, (S, 1), 0)
+    BQ = 512
+    key_i = lax.broadcasted_iota(jnp.int32, (BQ, BQ), 0)
+    query_i = lax.broadcasted_iota(jnp.int32, (BQ, BQ), 1)
+
+    def attend(w, p):
+        ending = ends[w]
+
+        def part(kind):
+            return lanes(256 * kind + 128 * p)
+
+        pl_ = lanes(128 * p)
+        keys, values = QKV[w, :, part(1)], QKV[w, :, part(2)]
+        ktT[...] = keys.T
+        vtT[...] = values.T
+        doT[...] = dO[w, :, pl_].T
+        dkA[...] = jnp.zeros_like(dkA)
+        dvA[...] = jnp.zeros_like(dvA)
+
+        def head(hh, carry):
+            inside = (lane // 64) == hh
+            feature = lane == (64 - 64 * hh)
+            t = jnp.where(place < ending, NEG, 0.0)
+            khat[...] = jnp.where(
+                inside, keys.astype(F32), jnp.where(feature, t, 0.0)
+            ).astype(BF)
+            hr = rows(64 * hh, 64)
+            for qb in range(S // BQ):
+                nk = (qb + 1) * BQ
+                qr = slice(qb * BQ, nk)
+                q = QKV[w, qr, part(0)].astype(F32)
+                u = jnp.where(place[qr] >= ending, 1.0, 0.0)
+                q_in = jnp.where(inside, q, 0.0).astype(BF)
+                q_hat = jnp.where(inside, q, jnp.where(feature, u, 0.0)).astype(BF)
+                d_in = jnp.where(inside, dO[w, qr, pl_].astype(F32), 0.0).astype(BF)
+                sc = dot(khat[0:nk, :], q_hat, 1, 1)
+                last = jnp.where(key_i <= query_i, sc[nk - BQ :], NEG)
+                sc = last if qb == 0 else jnp.concatenate([sc[: nk - BQ], last], axis=0)
+                e = jnp.exp(sc - jnp.max(sc, axis=0, keepdims=True))
+                pn = e * (1.0 / jnp.sum(e, axis=0, keepdims=True))
+                pb = pn.astype(BF)
+                o = dot(vtT[hr, 0:nk], pb, 1, 0)
+                oT[hr, qr] = o
+                dp = dot(values[0:nk], d_in, 1, 1)
+                dd = jnp.sum(o * doT[hr, qr].astype(F32), axis=0, keepdims=True)
+                ds = (pn * (dp - dd)).astype(BF)
+                dqT[hr, qr] = dot(ktT[hr, 0:nk], ds, 1, 0)
+                dkA[0:nk, :] += dot(ds, q_in, 1, 0)
+                dvA[0:nk, :] += dot(pb, d_in, 1, 0)
+            return carry
+
+        lax.fori_loop(0, 2, head, 0)
+        cos_rows, sin_rows = cosine[...], -sine[...]
+        att[w, :, pl_] = oT[...].T.astype(BF)
+        QKV[w, :, part(0)] = turn(dqT[...].T * 0.125, cos_rows, sin_rows).astype(BF)
+        QKV[w, :, part(1)] = turn(dkA[...], cos_rows, sin_rows).astype(BF)
+        QKV[w, :, part(2)] = dvA[...].astype(BF)
+
+    def share_step(w):
+        def step(i, total):
+            r = rows(256 * i, 256)
+            value = dot(A[w, r, :], Wo[...], 1, 0) + dot(att[w, r, :], Wa[...].reshape(256, 1024), 1, 0)
+            A[w, r, :] = value.astype(BF)
+            d = dot(H[w, r, :], Wi[...], 1, 1) + dot(QKV[w, r, :], Wq[...], 1, 1)
+            H[w, r, :] = d.astype(BF)
+            n = (N[w, r, :].astype(F32) - PR[1:2, :]) / PR[0:1, :]
+            return (
+                total[0] + jnp.sum(d, axis=0, keepdims=True),
+                total[1] + jnp.sum(d * n, axis=0, keepdims=True),
+            )
+
+        zero = jnp.zeros((1, 1024), F32)
+        first, second = lax.fori_loop(0, 4, step, (zero, zero))
+        TAIL[0:1, :] += first
+        TAIL[1:2, :] += second
+
+    shares = (A, H)
+
+    def share_c(w):
+        for t in range(2):
+            for yy in range(2):
+                src = shares[t].at[w, rows(SL * (2 * yy + oc), SL)]
+                dst = X.at[w, rows(SL * (2 * t + yy), SL)]
+                link.copy("sc", 4 * w + 2 * t + yy, 8, src, dst, core).start()
+
+    def share_y(w):
+        for t in (1, 0):
+            dst = X.at[w, rows(SL * (2 * t + oy), SL)]
+            for yy in range(2):
+                slot = X.at[w, rows(SL * (2 * t + yy), SL)]
+                link.copy("sc", 4 * w + 2 * t + yy, 8, slot, slot, core).wait_recv()
+            src = shares[t].at[w, rows(SL * (2 * oy + c), SL)]
+            add_into(src, dst)
+            link.copy("sy", 2 * w + t, 4, src, YR.at[w, t], ypart).start()
+
+    def window(w, carry):
+        def pair(p, inner):
+            attend(w, p)
+
+            @pl.when((w == 1) & (p == 0))
+            def _():
+                share_y(0)
+
+            return inner
+
+        lax.fori_loop(0, 2, pair, 0)
+        share_step(w)
+        share_c(w)
+        return carry
+
+    lax.fori_loop(0, 2, window, 0)
+
+    def gq_step(kind, carry):
+        l = lanes(256 * kind, 256)
+        gq = dot(QKV[0, :, l], N[0], 0, 0) + dot(QKV[1, :, l], N[1], 0, 0)
+        for bb in range(8):
+            GQ[bb % 2, bb // 2, rows(256 * kind, 256), :] = gq[:, 128 * bb : 128 * bb + 128].astype(BF)
+        return carry
+
+    lax.fori_loop(0, 3, gq_step, 0)
+    again = [
+        pltpu.make_async_copy(x_in.at[w], N.at[w, 0:SL], local_sems.at[3 * w + 2]) for w in range(2)
+    ]
+    for cp in again:
+        cp.start()
+    start(lambda: link.copy("qx", 0, 1, GQ.at[ox], XQ, xpart))
+    share_y(1)
+    ga = dot(att[0], G[0], 0, 0) + dot(att[1], G[1], 0, 0)
+    for j in range(4):
+        for cc in range(2):
+            at = 64 * j + 32 * cc
+            GAS[cc, j] = ga[at : at + 32].astype(BF)
+    start(lambda: link.copy("ac", 0, 1, GAS.at[oc], GA.at[c], core))
+    GA[c] = GAS[c]
+    tail = TAIL[...]
+    for bb in range(8):
+        GT[bb % 2, bb // 2] = tail[:, 128 * bb : 128 * bb + 128].astype(BF)
+    start(lambda: link.copy("tx", 0, 1, GT.at[ox], XT, xpart))
+    link.copy("ac", 0, 1, GAS.at[0], GA.at[oc], core).wait_recv()
+    start(lambda: link.copy("ax", 0, 1, GA.at[ox], XA, xpart))
+
+    def final_o():
+        for k in (1, 2, 3):
+            link.copy("oz", k - 1, 3, ZO.at[k - 1], ZO.at[k - 1], core).wait_recv()
+        grad_o[...] = (
+            GO[z, xx].astype(F32)
+            + XO[z].astype(F32)
+            + ZO[0].astype(F32)
+            + ZO[1].astype(F32)
+            + ZO[2].astype(F32)
+        )
+
+    def final_i():
+        for q in range(4):
+            for k in (1, 2, 3):
+                link.copy("iz", 3 * q + k - 1, 12, ZI.at[k - 1, q], ZI.at[k - 1, q], core).wait_recv()
+            total = GI[q, xx, z].astype(F32) + XI[q, z].astype(F32)
+            for k in range(3):
+                total = total + ZI[k, q].astype(F32)
+            turned = total.T.astype(BF)
+            for owner in range(4):
+                SWI[owner, :, 256 * q : 256 * q + 256] = turned[32 * owner : 32 * owner + 32]
+
+    def z_step(name):
+        group, received, _ = sums[name]
+        link.copy(name + "x", 0, 1, received, received, core).wait_recv()
+        for k in (1, 2, 3):
+            zz = (z + k) % 4
+            add_into(group.at[xx, zz], received.at[zz])
+            start(
+                lambda k=k: link.copy(
+                    name + "z", k - 1, 3, group.at[xx, (z + k) % 4], sums[name][2].at[k - 1], zdev(k)
+                )
+            )
+
+    def z_total(name):
+        group, received, landed = sums[name]
+        for k in (1, 2, 3):
+            link.copy(name + "z", k - 1, 3, landed.at[k - 1], landed.at[k - 1], core).wait_recv()
+        total = group[xx, z].astype(F32) + received[z].astype(F32)
+        for k in range(3):
+            total = total + landed[k].astype(F32)
+        return total
+
+    final_o()
+    final_i()
+    RWI[s] = SWI[s]
+    seq_sends("swi", lambda owner: SWI.at[owner], lambda: RWI.at[s])
+
+    z_step("q")
+    z_step("t")
+    z_step("a")
+
+    def final_rows(w, carry):
+        again[w].wait()
+        v = N[w, 0:SL, :].astype(F32)
+        mine = rows(SL * s, SL)
+        for t in (1, 0):
+            link.copy("sy", 2 * w + t, 4, YR.at[w, t], YR.at[w, t], core).wait_recv()
+        value = (
+            A[w, mine, :].astype(F32)
+            + X[w, rows(SL * y, SL), :].astype(F32)
+            + YR[w, 0].astype(F32)
+        )
+        out[w] = (v + value + PR[2:3, :]).astype(BF)
+        d = (
+            H[w, mine, :].astype(F32)
+            + X[w, rows(SL * (2 + y), SL), :].astype(F32)
+            + YR[w, 1].astype(F32)
+        )
+        v = v - jnp.mean(v, axis=-1, keepdims=True)
+        scale = lax.rsqrt(jnp.mean(v * v, axis=-1, keepdims=True) + norm_eps)
+        v = v * scale
+        d = d * PR[0:1, :]
+        d = d - jnp.mean(d, axis=-1, keepdims=True) - v * jnp.mean(d * v, axis=-1, keepdims=True)
+        grad_in[w] = G[w, mine, :].astype(F32) + scale * d
+        return carry
+
+    final_rows(0, 0)
+
+    total_q = z_total("q")
+    total_t = z_total("t")
+    grad_bin[...] = total_t[0:8]
+    turned_q = total_q.T.astype(BF)
+    turned_t = jnp.concatenate([total_t, jnp.zeros((112, 128), F32)], axis=0).T.astype(BF)
+    for owner in range(4):
+        SWQ[owner, :, 0:768] = turned_q[32 * owner : 32 * owner + 32]
+        SWQ[owner, :, 768:896] = turned_t[32 * owner : 32 * owner + 32]
+    RWQ[s] = SWQ[s]
+    seq_sends("swq", lambda owner: SWQ.at[owner], lambda: RWQ.at[s])
+    grad_a[...] = z_total("a")
+
+    def from_seq(name, landed):
+        for i, owner in enumerate((2 * y + oc, 2 * oy + c, 2 * oy + oc)):
+            link.copy(name, i, 3, landed.at[owner], landed.at[owner], core).wait_recv()
+
+    from_seq("swi", RWI)
+    for r in range(4):
+        for blk in range(8):
+            at = 512 * blk + 128 * r
+            grad_i[:, at : at + 128] = RWI[r, :, 128 * blk : 128 * blk + 128].astype(F32)
+
+    final_rows(1, 0)
+
+    from_seq("swq", RWQ)
+    got = [RWQ[r].astype(F32) for r in range(4)]
+    place_of = {}
+    for r in range(4):
+        for j in range(4):
+            for kind in range(3):
+                place_of[3 * head_of(r, j) + kind] = (got[r], 256 * kind + 128 * (j // 2) + 64 * (j % 2))
+    for at in range(24):
+        grad_q[:, 128 * at : 128 * at + 128] = halves(place_of[2 * at], place_of[2 * at + 1])
+    summed = got[0][:, 768:896] + got[1][:, 768:896] + got[2][:, 768:896] + got[3][:, 768:896]
+    grad_small[...] = jnp.where(lane == 2, got[0][:, 768:896], summed)
+
+    for make in pending:
+        make().wait_send()
+    for w in range(2):
+        rows_left("g", G, w)
+    for q in range(4):
+        link.copy("ox", q, 4, GO.at[q, ox], XO.at[q], xpart).wait_send()
+        link.copy("ix", q, 4, GI.at[q, ox], XI.at[q], xpart).wait_send()
+        for k in (1, 2, 3):
+            zz = (z + k) % 4
+            link.copy("iz", 3 * q + k - 1, 12, GI.at[q, xx, zz], ZI.at[k - 1, q], zdev(k)).wait_send()
+    for k in (1, 2, 3):
+        zz = (z + k) % 4
+        link.copy("oz", k - 1, 3, GO.at[zz, xx], ZO.at[k - 1], zdev(k)).wait_send()
+    for w in range(2):
+        for t in range(2):
+            for yy in range(2):
+                src = shares[t].at[w, rows(SL * (2 * yy + oc), SL)]
+                dst = X.at[w, rows(SL * (2 * t + yy), SL)]
+                link.copy("sc", 4 * w + 2 * t + yy, 8, src, dst, core).wait_send()
+            src = shares[t].at[w, rows(SL * (2 * oy + c), SL)]
+            link.copy("sy", 2 * w + t, 4, src, YR.at[w, t], ypart).wait_send()
+
+
+def turn_tables(seq_len):
+    inverse = 10000.0 ** (-2.0 * np.arange(ROTARY // 2) / ROTARY)
+    angles = np.arange(seq_len)[:, None] * inverse[None, :]
+    cosine = np.ones((seq_len, HD), np.float32)
+    sine = np.zeros((seq_len, HD), np.float32)
+    cosine[:, 0:ROTARY:2] = cosine[:, 1:ROTARY:2] = np.cos(angles)
+    sine[:, 0:ROTARY:2] = -np.sin(angles)
+    sine[:, 1:ROTARY:2] = np.sin(angles)
+    return np.tile(cosine, (1, 2)), np.tile(sine, (1, 2))
+
+
+def fused_shards(inputs, ends, ln_gain, ln_bias, w_qkv, w_attn, w_in, b_in, w_out, b_out, cotangent):
+    def widen(v):
+        return jnp.pad(v, (0, 128 - v.shape[0]))
+
+    prm = jnp.pad(jnp.stack([widen(ln_gain), widen(ln_bias), widen(b_out), b_in]), ((0, 12), (0, 0)))
+    cosine, sine = turn_tables(1024)
+    in_vmem = pl.BlockSpec(memory_space=pltpu.VMEM)
+    in_any = pl.BlockSpec(memory_space=pl.ANY)
+    rows_type = (2, 1024, 1024)
+    results = pl.pallas_call(
+        fused_layer,
+        out_shape=(
+            jax.ShapeDtypeStruct((2, 256, 1024), BF),
+            jax.ShapeDtypeStruct((2, 256, 1024), F32),
+            jax.ShapeDtypeStruct((32, 3072), F32),
+            jax.ShapeDtypeStruct((32, 1024), F32),
+            jax.ShapeDtypeStruct((32, 4096), F32),
+            jax.ShapeDtypeStruct((128, 1024), F32),
+            jax.ShapeDtypeStruct((32, 128), F32),
+            jax.ShapeDtypeStruct((8, 128), F32),
+        ),
+        in_specs=[pl.BlockSpec(memory_space=pltpu.SMEM)] + [in_vmem] * 7 + [in_any] * 2,
+        out_specs=(in_vmem,) * 8,
+        scratch_shapes=[
+            pltpu.VMEM(rows_type, BF),
+            pltpu.VMEM(rows_type, BF),
+            pltpu.VMEM(rows_type, BF),
+            pltpu.VMEM(rows_type, BF),
+            pltpu.VMEM(rows_type, BF),
+            pltpu.VMEM((1024, 1024), BF),
+            pltpu.VMEM((1024, 1024), BF),
+            pltpu.VMEM((1024, 768), BF),
+            pltpu.VMEM((4, 2, 32, 1024), BF),
+            pltpu.VMEM((4, 2, 32, 1024), BF),
+            pltpu.VMEM((4, 32, 1024), BF),
+            pltpu.VMEM((4, 32, 768), BF),
+            pltpu.VMEM((8, 64, 128), BF),
+            pltpu.VMEM((8, 1024), F32),
+            pltpu.VMEM((2, 1024, 768), BF),
+            pltpu.VMEM((2, 1024, 256), BF),
+            pltpu.VMEM((2, 1024, 256), BF),
+            pltpu.VMEM((4, 2, 128, 1024), BF),
+            pltpu.VMEM((4, 128, 1024), BF),
+            pltpu.VMEM((3, 128, 1024), BF),
+            pltpu.VMEM((4, 2, 4, 256, 128), BF),
+            pltpu.VMEM((4, 4, 256, 128), BF),
+            pltpu.VMEM((3, 4, 256, 128), BF),
+            pltpu.VMEM((2, 4, 768, 128), BF),
+            pltpu.VMEM((4, 768, 128), BF),
+            pltpu.VMEM((3, 768, 128), BF),
+            pltpu.VMEM((2, 4, 32, 1024), BF),
+            pltpu.VMEM((4, 32, 1024), BF),
+            pltpu.VMEM((3, 32, 1024), BF),
+            pltpu.VMEM((2, 4, 32, 1024), BF),
+            pltpu.VMEM((2, 4, 16, 128), BF),
+            pltpu.VMEM((4, 16, 128), BF),
+            pltpu.VMEM((3, 16, 128), BF),
+            pltpu.VMEM((2, 2, 256, 1024), BF),
+            pltpu.VMEM((4, 32, 1024), BF),
+            pltpu.VMEM((4, 32, 1024), BF),
+            pltpu.VMEM((4, 32, 896), BF),
+            pltpu.VMEM((4, 32, 896), BF),
+            pltpu.VMEM((16, 1024), F32),
+            pltpu.VMEM((1024, 128), BF),
+            pltpu.VMEM((128, 1024), BF),
+            pltpu.VMEM((128, 1024), BF),
+            pltpu.VMEM((128, 1024), BF),
+            pltpu.VMEM((128, 1024), F32),
+            pltpu.VMEM((128, 1024), F32),
+            pltpu.VMEM((1024, 128), F32),
+            pltpu.VMEM((1024, 128), F32),
+            pltpu.SemaphoreType.DMA((160,)),
+            pltpu.SemaphoreType.DMA((160,)),
+            pltpu.SemaphoreType.DMA((6,)),
+        ],
+        compiler_params=pltpu.CompilerParams(
+            collective_id=0, has_side_effects=True, vmem_limit_bytes=63 * 2**20
+        ),
+        cost_estimate=pl.CostEstimate(flops=46 * 10**9, bytes_accessed=10**7, transcendentals=10**7),
+    )(ends, prm, w_qkv, w_attn, w_in, w_out, cosine, sine, inputs, cotangent)
+    out, grad_in, grad_q, grad_a, grad_i, grad_o, small, bias_in = results
+    return (
+        out,
+        grad_in,
+        small[:, 1],
+        small[:, 0],
+        grad_q,
+        grad_a,
+        grad_i,
+        bias_in[3],
+        grad_o,
+        small[:, 2],
+    )
+
+
+def fits_fused(mesh):
+    return mesh.shape["batch"] == 8 and mesh.shape["seq"] == 4
+
+
 def solution(mesh):
     return jax.shard_map(
-        shards,
+        fused_shards if fits_fused(mesh) else shards,
         mesh=mesh,
         in_specs=(
             P("batch", "seq", None),

time: 1130 us -> 240 us (0.21)
  waiting for transfers between devices: 471 us -> 0 us
  Pallas kernels: 0 us -> 227 us
  matrix products: 209 us -> 0 us
  local copies, waits for them, and re-layouts: 202 us -> 10.8 us
  blocking collectives: 120 us -> 0 us
  other arithmetic: 55.1 us -> 1.26 us
  starting transfers between devices: 44.8 us -> 0 us
  between operations: 16 us -> 0.67 us
    reduce_scatter x4 -> x0, waiting for transfers between devices: 326 us -> none  [the longest x1 187 us: reduce_grads(): lax.psum_scatter(gradients[6], ('batch', 'seq'), scatter_dimension=0, til...]
    pallas_call x0 -> x1, Pallas kernels: none -> 227 us  [fused_shards(): pl.pallas_call(fused_layer, out_shape=(jax.ShapeDtypeStruct((2, 256, 1024...]
    dot_general x52 -> x0, matrix products: 209 us -> none  [the longest x8 25.5 us: block_scores(): jnp.einsum('qhd,khd->hqk', block_queries, key_vectors, preferred_element_...]
    unnamed x2 -> x0, blocking collectives: 82.3 us -> none
    all_gather x4 -> x0, waiting for transfers between devices: 71.2 us -> none  [the longest x1 59.3 us: collect(): lax.all_gather(w_qkv, ('batch', 'seq'), axis=0, tiled=True)]
    all_to_all x8 -> x0, waiting for transfers between devices: 70.6 us -> none  [the longest x2 51.1 us: shards(): lax.all_to_all(d_packed, 'seq', split_axis=1, concat_axis=2, tiled=True)]
    dynamic_update_slice x12 -> x0, local copies, waits for them, and re-layouts: 44.7 us -> none  [the longest x8 43.5 us: attend_backward(): lax.scan(one_block, (zero_sums, zero_sums), (block_ids, peaks, totals))]
    all_to_all x8 -> x0, starting transfers between devices: 44.2 us -> none  [the longest x2 20.3 us: shards(): lax.all_to_all(attended, 'seq', split_axis=1, concat_axis=2, tiled=True)]
  transfers between devices with their start and end apart: 16 -> 0, of which waited for: 8 -> 0; matrix products, arithmetic and copies ran while one was open for 38% -> 0% of each run, Pallas kernels for 0% -> 0%
where the time goes in v1:
time: 240 us
  Pallas kernels  227 us (95%)
  local copies, waits for them, and re-layouts  10.8 us (4%)
    pallas_call x1, Pallas kernels, fused_shards(): pl.pallas_call(fused_layer, out_shape=(jax.ShapeDtypeStruct((2, 256, 1024...  227 us
    unnamed x16, local copies, waits for them, and re-layouts  6.59 us

profile of v1, /device:TPU:0, one launch (start us, length us, event | category | flops | bytes accessed | tf_op | source)
XLA Modules:
  0.0 239.5 jit_solution(13347067802556188206)
XLA Ops:
  0.6 0.7 pad_bitcast_fusion.2
  1.3 0.7 pad_bitcast_fusion
  2.0 1.3 fusion.6.prm
  3.2 226.8 %shard_map.204 = (bf16[2,256,1024]{2,1,0:T(8,128)(2,1)}, f32[2,256,1024]{2,1,0:T(8,128)}, f32[32,3072]{1,0:T(8,128)}, f32[32,1024]{1,0:T(8,128)}, f32[32,4096]{1...) custom-call(s32[2]{0:T(128)} %ends.1, bf16[16,128]{1,0:T(8,128)(2,1)} %fusion.6.prm, ...), custom_call_target="tpu_custom_call" | custom-call | flops 46000001024 | bytes 10000000 | tf_op jit(solution)/shard_map/pallas_call | solution.py:1010
  230.0 0.0 copy-start
  230.0 1.3 slice_bitcast_fusion
  231.4 1.6 slice_reduce_fusion
  232.9 2.3 copy.29
  235.2 0.0 copy-done
  235.2 0.0 copy-start.3
  235.2 0.0 copy-start.4
  235.2 0.0 copy-start.2
  235.2 1.3 copy.30
  236.5 0.0 copy-done.3
  236.5 0.0 copy-start.1
  236.5 0.7 copy.31
  237.3 0.0 copy-done.4
  237.3 0.7 copy.32
  237.9 0.0 copy-done.2
  237.9 0.8 copy.33
  238.7 0.0 copy-done.1
  238.7 0.8 copy.34
Async XLA Ops:
  230.0 5.2 %copy-start = (f32[2,256,1024]{2,1,0:T(8,128)S(1)}, f32[2,256,1024]{2,1,0:T(8,128)}, u32[]{:S(2)}) copy-start(f32[2,256,1024]{2,1,0:T(8,128)} %get-tuple-element.42) | copy-start | bytes 6291460
  235.2 1.3 copy-start.3
  235.2 2.1 copy-start.4
  235.2 2.7 %copy-start.2 = (f32[32,4096]{1,0:T(8,128)S(1)}, f32[32,4096]{1,0:T(8,128)}, u32[]{:S(2)}) copy-start(f32[32,4096]{1,0:T(8,128)} %get-tuple-element.47) | copy-start | bytes 1572868
  236.5 2.2 copy-start.1

commit v2 on v1

--- a/solution.py
+++ b/solution.py
@@ -366,21 +366,23 @@
 
 
 def gelu_pair(v):
-    cube = v * v
-    t = jnp.tanh(gelu_factor * (v + 0.044715 * (v * cube)))
-    half = 0.5 * (1.0 + t)
-    slope = half + 0.5 * v * (1.0 - t * t) * (gelu_factor * (1.0 + (3 * 0.044715) * cube))
-    return v * half, slope
+    square = v * v
+    half = 0.5 + 0.5 * jnp.tanh(v * (gelu_factor + (gelu_factor * 0.044715) * square))
+    value = v * half
+    return value, half + (value - value * half) * (
+        2.0 * gelu_factor + (6.0 * gelu_factor * 0.044715) * square
+    )
 
 
 def fused_layer(
-    ends, prm, wq, wa, wi, wo, cosine, sine, x_in, g_in,
-    out, grad_in, grad_q, grad_a, grad_i, grad_o, grad_small, grad_bin,
-    X, N, G, A, H, Wi, Wo, Wq, WaAll, Wa, PWI, PWQ, PRM, PR, QKV, att, dO,
-    GO, XO, ZO, GI, XI, ZI, GQ, XQ, ZQ, GA, XA, ZA, GAS, GT, XT, ZT,
+    ends, prm, wq, wa, wi, wo, turns, x_in, g_in,
+    out_hbm, grad_in_hbm, grad_q_hbm, grad_a_hbm, grad_i_hbm, grad_o_hbm, grad_small_hbm,
+    X, N, G, A, H, Wi, Wo, Wq, WaAll, Wa, PWI, PWQ, PRS, PRM, PR, QKV, att, dO,
+    GO, XO, ZO, CO, GI, XI, ZI, GQ, XQ, ZQ, GA, XA, ZA, GT, XT, ZT,
     YR, SWI, RWI, SWQ, RWQ, TAIL,
     khat, ktT, vtT, doT, oT, dqT, dkA, dvA,
-    send_sems, recv_sems, local_sems,
+    grad_in, grad_q, grad_a, grad_small,
+    send_sems, recv_sems, local_sems, out_sems,
 ):
     b = lax.axis_index("batch")
     s = lax.axis_index("seq")
@@ -407,6 +409,13 @@
         make().start()
         pending.append(make)
 
+    barrier = pltpu.get_barrier_semaphore()
+    others = [xpart] + [zdev(k) for k in (1, 2, 3)]
+    others += [(2 * ((z + k) % 4) + ox, s) for k in (1, 2, 3)]
+    partners = [core, ypart, diag] + others
+    for device in partners:
+        pl.semaphore_signal(barrier, inc=1, device_id=device, device_id_type=MESH)
+
     own = rows(SL * s, SL)
     locals_ = []
     for w in range(2):
@@ -418,87 +427,191 @@
     for r in range(SB):
         for blk in range(8):
             PWI[r, :, 128 * blk : 128 * blk + 128] = wi[:, 512 * blk + 128 * r : 512 * blk + 128 * r + 128]
+    tile = prm[...].astype(F32)
+    row = lax.broadcasted_iota(jnp.int32, (16, 128), 0)
+    tile = jnp.where(row < 3, pltpu.roll(tile, 32 * s, 1), tile)
+    PRS[s] = tile.astype(BF)
+    Wi[rows(128 * b + 32 * s, 32), :] = PWI[s]
+    Wo[rows(128 * b, 128), :] = wo[...]
+    WaAll[z, xx] = wa[...]
+
     wq_f = wq[...].astype(F32)
     for r in range(SB):
         for kind in range(3):
             for p in range(2):
                 lo = 192 * head_of(r, 2 * p) + 64 * kind
                 hi = 192 * head_of(r, 2 * p + 1) + 64 * kind
-                at = 256 * kind + 128 * p
+                at = 384 * p + 128 * kind
                 PWQ[r, :, at : at + 128] = halves((wq_f, lo), (wq_f, hi)).astype(BF)
-    tile = prm[...].astype(F32)
-    row = lax.broadcasted_iota(jnp.int32, (16, 128), 0)
-    tile = jnp.where(row < 3, pltpu.roll(tile, 32 * s, 1), tile)
-    PRM[b, rows(16 * s, 16), :] = tile.astype(BF)
-    Wi[rows(128 * b + 32 * s, 32), :] = PWI[s]
     Wq[rows(128 * b + 32 * s, 32), :] = PWQ[s]
-    Wo[rows(128 * b, 128), :] = wo[...]
-    WaAll[z, xx] = wa[...]
-
-    barrier = pltpu.get_barrier_semaphore()
-    partners = [core, ypart, diag, xpart] + [zdev(k) for k in (1, 2, 3)]
-    for device in partners:
-        pl.semaphore_signal(barrier, inc=1, device_id=device, device_id_type=MESH)
+
     pl.semaphore_wait(barrier, len(partners))
 
     def seq_sends(name, src_of, dst):
         for i, (device, owner) in enumerate(
             ((core, 2 * y + oc), (ypart, 2 * oy + c), (diag, 2 * oy + oc))
         ):
-            start(
-                lambda i=i, device=device, owner=owner: link.copy(
-                    name, i, 3, src_of(owner), dst(), device
-                )
-            )
+            link.copy(name, i, 3, src_of(owner), dst(), device).start()
+
+    def seq_left(name, src_of, dst):
+        for i, (device, owner) in enumerate(
+            ((core, 2 * y + oc), (ypart, 2 * oy + c), (diag, 2 * oy + oc))
+        ):
+            link.copy(name, i, 3, src_of(owner), dst(), device).wait_send()
 
     def seq_waits(name, src, dst_of):
         for i, owner in enumerate((2 * y + oc, 2 * oy + c, 2 * oy + oc)):
             link.copy(name, i, 3, src, dst_of(owner), core).wait_recv()
 
     def prm_block(owner):
-        return PRM.at[b, rows(16 * owner, 16)]
-
-    def wi_block(owner):
-        return Wi.at[rows(128 * b + 32 * owner, 32)]
+        return PRS.at[owner]
+
+    def wi_block(owner, u):
+        return Wi.at[rows(128 * b + 32 * owner, 32), 256 * u : 256 * u + 256]
 
     def wq_block(owner):
         return Wq.at[rows(128 * b + 32 * owner, 32)]
 
     gathers = {
-        "prm": lambda bb: PRM.at[bb],
-        "wa": lambda bb: WaAll.at[bb // 2, bb % 2],
-        "wi": lambda bb: Wi.at[rows(128 * bb, 128)],
-        "wo": lambda bb: Wo.at[rows(128 * bb, 128)],
-        "wq": lambda bb: Wq.at[rows(128 * bb, 128)],
+        "wi": (4, lambda bb, u: Wi.at[rows(128 * bb, 128), lanes(256 * u, 256)]),
+        "wo": (2, lambda bb, u: Wo.at[rows(128 * bb + 64 * u, 64)]),
+        "wq": (2, lambda bb, u: Wq.at[rows(128 * bb, 128), 384 * u : 384 * u + 384]),
+        "wa": (1, lambda bb, u: WaAll.at[bb // 2, bb % 2]),
     }
-
-    def gather_start(name):
-        block = gathers[name]
-        for k in (1, 2, 3):
-            start(lambda k=k: link.copy(name + "z", k - 1, 3, block(b), block(b), zdev(k)))
-        start(lambda: link.copy(name + "x", 0, 4, block(b), block(b), xpart))
-
-    def gather_pass(name, k):
-        block = gathers[name]
-        bb = 2 * zfrom(k) + xx
-        link.copy(name + "z", k - 1, 3, block(bb), block(bb), core).wait_recv()
-
-        def make():
-            held = block(2 * zfrom(k) + xx)
-            return link.copy(name + "x", k, 4, held, held, xpart)
-
-        start(make)
-
-    def gather_end(name, ks=(0, 1, 2, 3)):
-        block = gathers[name]
-        for k in ks:
-            bb = 2 * zfrom(k) + ox
-            link.copy(name + "x", k, 4, block(bb), block(bb), core).wait_recv()
-
-    seq_sends("prms", lambda owner: prm_block(s), lambda: prm_block(s))
-    seq_sends("wis", lambda owner: PWI.at[owner], lambda: wi_block(s))
-    gather_start("wa")
-    seq_sends("wqs", lambda owner: PWQ.at[owner], lambda: wq_block(s))
+    pair = z + 1 - 2 * (z % 2)
+
+    def gather_copy(name, way, at, count, zz, side, u, device):
+        held = gathers[name][1](2 * zz + side, u)
+        return link.copy(name + way, count * u + at, count * gathers[name][0], held, held, device)
+
+    def up_copy(name, zz, u):
+        return gather_copy(name, "l", zz, 5, zz, xx, u, (2 * (z + 1) + xx, s))
+
+    def down_copy(name, zz, u):
+        return gather_copy(name, "l", zz + 1, 5, zz, xx, u, (2 * (z - 1) + xx, s))
+
+    def z_copy(name, zz, k, u):
+        return gather_copy(name, "z", k - 1, 3, zz, xx, u, zdev(k))
+
+    def x_copy(name, zz, side, u):
+        return gather_copy(name, "x", zz, 4, zz, side, u, xpart)
+
+    def pair_copy(name, zz, u):
+        return gather_copy(name, "p", 0, 1, zz, ox, u, (2 * pair + xx, s))
+
+    def by_pair(name, u):
+        return name in ("wi", "wo") and 2 * u >= gathers[name][0]
+
+    def gather_z(name, u):
+        if name == "wi":
+
+            @pl.when(z < 3)
+            def _():
+                up_copy(name, z, u).start()
+
+            @pl.when(z > 0)
+            def _():
+                down_copy(name, z, u).start()
+
+            return
+        for far in (1, 2, 3):
+
+            @pl.when(z + far <= 3)
+            def _():
+                z_copy(name, z, far, u).start()
+
+            @pl.when(z >= far)
+            def _():
+                z_copy(name, z, 4 - far, u).start()
+
+    def gather_x(name, u):
+        x_copy(name, z, xx, u).start()
+
+    def hand_over(name, zz, u):
+        if by_pair(name, u):
+
+            @pl.when(zz != pair)
+            def _():
+                x_copy(name, zz, xx, u).start()
+
+        else:
+            x_copy(name, zz, xx, u).start()
+
+    def gather_pass(name, far, u):
+        @pl.when(z >= far)
+        def _():
+            if name == "wi":
+                up_copy(name, z - far, u).wait_recv()
+
+                @pl.when(z < 3)
+                def _():
+                    up_copy(name, z - far, u).start()
+
+            else:
+                z_copy(name, z - far, far, u).wait_recv()
+            hand_over(name, z - far, u)
+
+        @pl.when(z + far <= 3)
+        def _():
+            if name == "wi":
+                down_copy(name, z + far, u).wait_recv()
+
+                @pl.when(z > 0)
+                def _():
+                    down_copy(name, z + far, u).start()
+
+            else:
+                z_copy(name, z + far, 4 - far, u).wait_recv()
+            hand_over(name, z + far, u)
+
+    def gather_pair(name, u):
+        x_copy(name, z, ox, u).wait_recv()
+        pair_copy(name, z, u).start()
+
+    def gather_block(name, zz, u):
+        if by_pair(name, u):
+
+            @pl.when((zz != pair) & (zz != z))
+            def _():
+                x_copy(name, zz, ox, u).wait_recv()
+
+            @pl.when(zz == pair)
+            def _():
+                pair_copy(name, pair, u).wait_recv()
+
+        else:
+            x_copy(name, zz, ox, u).wait_recv()
+
+    def gather_end(name, u):
+        for zz in range(4):
+            gather_block(name, zz, u)
+
+    def gather_left(name, u):
+        if name != "wi":
+            for k in (1, 2, 3):
+                z_copy(name, z, k, u).wait_send()
+        for zz in range(4):
+            if name == "wi":
+
+                @pl.when((zz <= z) & (z < 3))
+                def _():
+                    up_copy(name, zz, u).wait_send()
+
+                @pl.when((zz >= z) & (z > 0))
+                def _():
+                    down_copy(name, zz, u).wait_send()
+
+            if by_pair(name, u):
+
+                @pl.when(zz != pair)
+                def _():
+                    x_copy(name, zz, xx, u).wait_send()
+
+            else:
+                x_copy(name, zz, xx, u).wait_send()
+
+        if by_pair(name, u):
+            pair_copy(name, z, u).wait_send()
 
     def rows_start(name, src, dst):
         for w in range(2):
@@ -522,26 +635,37 @@
         block = dst.at[w, rows(SL * (2 * oy + oc), SL)]
         link.copy(name + "f", w, 2, block, block, core).wait_recv()
 
+    seq_sends("prms", lambda owner: prm_block(s), lambda: prm_block(s))
+    for u in range(4):
+        seq_sends(
+            "wis%d" % u, lambda owner: PWI.at[owner, :, 256 * u : 256 * u + 256], lambda: wi_block(s, u)
+        )
+    gather_z("wa", 0)
+    gather_x("wa", 0)
+    gather_x("wo", 0)
+    seq_sends("wqs", lambda owner: PWQ.at[owner], lambda: wq_block(s))
     rows_start("x", x_in, X)
-    seq_waits("prms", PRM.at[b, rows(16 * s, 16)], prm_block)
-    gather_start("prm")
-    seq_waits("wis", PWI.at[0], wi_block)
-    gather_start("wi")
-    for k in (1, 2, 3):
-        gather_pass("prm", k)
-    for k in (1, 2, 3):
-        gather_pass("wa", k)
-    gather_end("prm")
-
+    seq_waits("prms", prm_block(s), prm_block)
+    total = PRS[0].astype(F32) + PRS[1].astype(F32) + PRS[2].astype(F32) + PRS[3].astype(F32)
+    PRM[b] = jnp.where(row < 3, total, tile).astype(BF)
+    for i, device in enumerate(others):
+        start(lambda i=i, device=device: link.copy("prm", i, 7, PRM.at[b], PRM.at[b], device))
+    for u in range(4):
+        seq_waits("wis%d" % u, wi_block(s, u), lambda owner: wi_block(owner, u))
+        gather_z("wi", u)
+        gather_x("wi", u)
+    rows_start("g", g_in, G)
+    gather_pass("wi", 1, 0)
+    gather_pass("wi", 1, 1)
+    for far in (1, 2, 3):
+        gather_pass("wa", far, 0)
+
+    for i in range(7):
+        k = (0, 1, 2, 3, 1, 2, 3)[i]
+        bb = 2 * zfrom(k) + (ox if i in (0, 4, 5, 6) else xx)
+        link.copy("prm", i, 7, PRM.at[bb], PRM.at[bb], core).wait_recv()
     for bb in range(8):
-        total = (
-            PRM[bb, 0:16, :].astype(F32)
-            + PRM[bb, 16:32, :].astype(F32)
-            + PRM[bb, 32:48, :].astype(F32)
-            + PRM[bb, 48:64, :].astype(F32)
-        )
-        mine = PRM[bb, rows(16 * s, 16), :].astype(F32)
-        PR[:, 128 * bb : 128 * bb + 128] = jnp.where(row < 3, total, mine)[0:8]
+        PR[:, 128 * bb : 128 * bb + 128] = PRM[bb].astype(F32)[0:8]
 
     for cp in locals_:
         cp.wait()
@@ -553,91 +677,231 @@
         var = jnp.mean(v * v, axis=-1, keepdims=True)
         N[w, r, :] = (v * lax.rsqrt(var + norm_eps) * PR[0:1, :] + PR[1:2, :]).astype(BF)
 
-    def norm_own(w, carry):
+    def norm_near(w, carry):
         norm_rows(w, s)
         norm_rows(w, 2 * y + oc)
         return carry
 
-    def norm_far(w, carry):
+    def norm_far(w):
+        rows_end_far("x", X, w)
         norm_rows(w, 2 * oy + c)
         norm_rows(w, 2 * oy + oc)
-        return carry
 
     for w in range(2):
         rows_end_core("x", X, w)
-    lax.fori_loop(0, 2, norm_own, 0)
-    gather_pass("wi", 1)
-    for w in range(2):
-        rows_pass("x", X, w)
-    rows_start("g", g_in, G)
-    gather_pass("wi", 2)
-    gather_pass("wi", 3)
-    gather_start("wo")
-    for w in range(2):
-        rows_end_far("x", X, w)
-    lax.fori_loop(0, 2, norm_far, 0)
-    gather_end("wi")
+    lax.fori_loop(0, 2, norm_near, 0)
+    gather_pass("wi", 2, 0)
+    gather_pass("wi", 1, 2)
+    gather_pass("wi", 1, 3)
+    gather_pass("wi", 2, 1)
+    gather_pass("wi", 3, 0)
+    gather_pass("wi", 2, 2)
+    gather_pair("wi", 2)
+    gather_pass("wi", 3, 1)
+    rows_pass("x", X, 0)
+    gather_pass("wi", 2, 3)
+    gather_pair("wi", 3)
+    seq_waits("wqs", wq_block(s), wq_block)
+    gather_z("wq", 0)
 
     def hidden_step(i, carry):
-        w, t, u = i // 8, (i // 4) % 2, i % 4
+        early = i < 12
+        u = jnp.where(early, i // 3, i - 12)
+        at = jnp.where(early, i % 3, 3)
+        w = at % 2
+        t = jnp.where(at < 2, y, oy)
+
+        @pl.when(i == 0)
+        def _():
+            gather_end("wi", 0)
+
+        @pl.when(i == 2)
+        def _():
+            norm_far(0)
+
+        @pl.when(i == 3)
+        def _():
+            gather_pass("wi", 3, 2)
+            gather_x("wq", 0)
+            gather_end("wi", 1)
+
+        @pl.when(i == 5)
+        def _():
+            gather_pass("wi", 3, 3)
+            gather_z("wq", 1)
+
+        @pl.when(i == 6)
+        def _():
+            gather_end("wi", 2)
+
+        @pl.when(i == 7)
+        def _():
+            rows_pass("x", X, 1)
+
+        @pl.when(i == 9)
+        def _():
+            gather_pass("wq", 1, 0)
+            gather_end("wi", 3)
+
+        @pl.when(i == 12)
+        def _():
+            gather_pass("wq", 2, 0)
+            gather_pass("wq", 3, 0)
+            gather_x("wq", 1)
+            norm_far(1)
+
         r, l = rows(512 * t, 512), lanes(256 * u, 256)
         v = dot(N[w, r, :], Wi[:, l], 1, 0) + PR[3:4, l]
         value, slope = gelu_pair(v)
         A[w, r, l] = value.astype(BF)
         H[w, r, l] = slope.astype(BF)
-
-        @pl.when(i == 3)
-        def _():
-            gather_pass("wo", 1)
-
-        @pl.when(i == 7)
-        def _():
-            gather_pass("wo", 2)
-
-        @pl.when(i == 11)
-        def _():
-            gather_pass("wo", 3)
-            seq_waits("wqs", PWQ.at[0], wq_block)
-            gather_start("wq")
-
         return carry
 
     lax.fori_loop(0, 16, hidden_step, 0)
-    for w in range(2):
-        rows_end_core("g", G, w)
-        rows_pass("g", G, w)
-    for w in range(2):
-        rows_end_far("g", G, w)
-    gather_end("wo")
-    gather_end("wa")
+    for u in range(2):
+        gather_z("wo", u)
     for w in range(2):
         rows_left("x", X, w)
+    gather_end("wa", 0)
     start(lambda: link.copy("wac", 0, 1, WaAll.at[:, oc], Wa.at[:, c], core))
     Wa[:, c] = WaAll[:, c]
-
-    sums = {"o": (GO, XO, ZO), "i": (GI, XI, ZI), "q": (GQ, XQ, ZQ), "a": (GA, XA, ZA), "t": (GT, XT, ZT)}
+    for far in (1, 2, 3):
+        gather_pass("wq", far, 1)
+    gather_x("wo", 1)
 
     def add_into(dst, other):
         dst[...] = (dst[...].astype(F32) + other[...].astype(F32)).astype(BF)
 
-    def o_z(q):
+    inner = (z == 1) | (z == 2)
+
+    def far_chip(tt):
+        return 2 * (1 - z // 2) + tt
+
+    def zchip(zz):
+        return (2 * zz + xx, s)
+
+    def o_near(q):
+        return link.copy("op", 0, 1, GO.at[q, xx], ZO.at[0], zchip(pair))
+
+    def o_comb(q):
+        return link.copy("oc", q % 2, 2, GO.at[q, xx], CO.at[q % 2], zchip(pair))
+
+    def o_far(q):
+        return link.copy("of", q % 2, 2, GO.at[q, xx], ZO.at[1], zchip(q))
+
+    def i_z(q, k):
+        return link.copy("iz", 3 * q + k - 1, 12, GI.at[q, xx, (z + k) % 4], ZI.at[k - 1, q], zdev(k))
+
+    def first_z(q):
         link.copy("ox", q, 4, XO.at[q], XO.at[q], core).wait_recv()
 
         @pl.when(z != q)
         def _():
             add_into(GO.at[q, xx], XO.at[q])
-            k = (q + 4 - z) % 4
-            link.copy("oz", k - 1, 3, GO.at[q, xx], ZO.at[k - 1], (2 * q + xx, s)).start()
-
-    def i_z(q):
+
+            @pl.when(q == pair)
+            def _():
+                o_near(q).start()
+
+            @pl.when((q != pair) & ~inner)
+            def _():
+                o_comb(q).start()
+
         link.copy("ix", q, 4, XI.at[q], XI.at[q], core).wait_recv()
         for k in (1, 2, 3):
             zz = (z + k) % 4
             add_into(GI.at[q, xx, zz], XI.at[q, zz])
-            link.copy("iz", 3 * q + k - 1, 12, GI.at[q, xx, zz], ZI.at[k - 1, q], zdev(k)).start()
-
-    def back_step(q, carry):
+            i_z(q, k).start()
+
+    def second_z(q):
+        @pl.when(inner)
+        def _():
+            o_comb(q).wait_recv()
+            add_into(GO.at[q, xx], CO.at[q % 2])
+            o_far(q).start()
+
+    def z_left():
+        o_near(pair).wait_send()
+        for tt in range(2):
+
+            @pl.when(inner)
+            def _():
+                o_far(far_chip(tt)).wait_send()
+
+            @pl.when(~inner)
+            def _():
+                o_comb(far_chip(tt)).wait_send()
+
+        for q in range(4):
+            for k in (1, 2, 3):
+                i_z(q, k).wait_send()
+
+    def chunk(j):
+        return jnp.where(j == 0, z, jnp.where(j == 3, pair, far_chip(0) + j - 1))
+
+    def send_x(q):
+        link.copy("ox", q, 4, GO.at[q, ox], XO.at[q], xpart).start()
+        link.copy("ix", q, 4, GI.at[q, ox], XI.at[q], xpart).start()
+
+    even = lax.broadcasted_iota(jnp.int32, (1, 128), 1) % 2 == 0
+
+    def turn_rows(r):
+        table = turns[r, :]
+        other = pltpu.roll(table, 64, 1)
+        low = lax.broadcasted_iota(jnp.int32, (1, 128), 1) < 64
+        return jnp.where(low, table, other), jnp.where(low, other, table)
+
+    def turn(v, cos_rows, sin_rows):
+        swapped = jnp.where(even, pltpu.roll(v, 127, 1), pltpu.roll(v, 1, 1))
+        return v * cos_rows + swapped * sin_rows
+
+    def qkv_step(p):
+        gather_end("wq", p)
+        l = slice(384 * p, 384 * p + 384)
+
+        def step(i, carry):
+            w, r = i // 4, rows(256 * (i % 4), 256)
+            v = dot(N[w, r, :], Wq[:, l], 1, 0)
+            cos_rows, sin_rows = turn_rows(r)
+            for kind in range(3):
+                tile_v = v[:, 128 * kind : 128 * kind + 128]
+                if kind < 2:
+                    tile_v = turn(tile_v, cos_rows, sin_rows)
+                if kind == 0:
+                    tile_v = tile_v * 0.125
+                QKV[w, r, 384 * p + 128 * kind : 384 * p + 128 * kind + 128] = tile_v.astype(BF)
+            return carry
+
+        lax.fori_loop(0, 8, step, 0)
+
+    qkv_step(0)
+    for w in range(2):
+        rows_end_core("g", G, w)
+    rows_pass("g", G, 0)
+    for u in range(4):
+        seq_left(
+            "wis%d" % u, lambda owner: PWI.at[owner, :, 256 * u : 256 * u + 256], lambda: wi_block(s, u)
+        )
+    link.copy("wac", 0, 1, WaAll.at[:, oc], Wa.at[:, oc], core).wait_recv()
+    TAIL[...] = jnp.zeros_like(TAIL)
+
+    def do_step(w):
+        def step(i, total):
+            r = rows(512 * i, 512)
+            g = G[w, r, :]
+            dO[w, r, :] = dot(g, Wa[...].reshape(256, 1024), 1, 1).astype(BF)
+            return total + jnp.sum(g.astype(F32), axis=0, keepdims=True)
+
+        TAIL[2:3, :] += lax.fori_loop(0, 2, step, jnp.zeros((1, 1024), F32))
+
+    rows_end_far("g", G, 0)
+    do_step(0)
+
+    def back_step(j, carry):
+        q = chunk(j)
         l = lanes(256 * q, 256)
+        gather_block("wo", q, 0)
+        gather_block("wo", q, 1)
 
         def dh_step(i, total):
             w, r = i // 2, rows(512 * (i % 2), 512)
@@ -650,269 +914,312 @@
         go = dot(A[0, :, l], G[0], 0, 0) + dot(A[1, :, l], G[1], 0, 0)
         GO[q, 0] = go[:128].astype(BF)
         GO[q, 1] = go[128:].astype(BF)
-        link.copy("ox", q, 4, GO.at[q, ox], XO.at[q], xpart).start()
         gi = dot(H[0, :, l], N[0], 0, 0) + dot(H[1, :, l], N[1], 0, 0)
         for bb in range(8):
             GI[q, bb % 2, bb // 2] = gi[:, 128 * bb : 128 * bb + 128].astype(BF)
-        link.copy("ix", q, 4, GI.at[q, ox], XI.at[q], xpart).start()
-
-        @pl.when(q == 0)
-        def _():
-            gather_pass("wq", 1)
-
-        @pl.when(q == 1)
-        def _():
-            gather_pass("wq", 2)
-
-        @pl.when(q == 2)
-        def _():
-            gather_pass("wq", 3)
-
-        @pl.when(q > 0)
-        def _():
-            o_z(q - 1)
-            i_z(q - 1)
+
+        send_x(q)
 
         return carry
-
-    TAIL[...] = jnp.zeros_like(TAIL)
-    lax.fori_loop(0, 4, back_step, 0)
-
-    gather_end("wq")
-    link.copy("wac", 0, 1, WaAll.at[:, oc], Wa.at[:, oc], core).wait_recv()
-    even = lax.broadcasted_iota(jnp.int32, (1, 128), 1) % 2 == 0
-
-    def turn(v, cos_rows, sin_rows):
-        swapped = jnp.where(even, pltpu.roll(v, 127, 1), pltpu.roll(v, 1, 1))
-        return v * cos_rows + swapped * sin_rows
-
-    def qkv_step(i, total):
-        w, r = i // 4, rows(256 * (i % 4), 256)
-        n = N[w, r, :]
-        cos_rows, sin_rows = cosine[r, :], sine[r, :]
-        for kind in range(3):
-            v = dot(n, Wq[:, 256 * kind : 256 * kind + 256], 1, 0)
-            for p in range(2):
-                tile_v = v[:, 128 * p : 128 * p + 128]
-                if kind < 2:
-                    tile_v = turn(tile_v, cos_rows, sin_rows)
-                if kind == 0:
-                    tile_v = tile_v * 0.125
-                QKV[w, r, 256 * kind + 128 * p : 256 * kind + 128 * p + 128] = tile_v.astype(BF)
-        g = G[w, r, :]
-        dO[w, r, :] = dot(g, Wa[...].reshape(256, 1024), 1, 1).astype(BF)
-        return total + jnp.sum(g.astype(F32), axis=0, keepdims=True)
-
-    TAIL[2:3, :] = lax.fori_loop(0, 8, qkv_step, jnp.zeros((1, 1024), F32))
-    o_z(3)
-    i_z(3)
 
     lane = lax.broadcasted_iota(jnp.int32, (1, 128), 1)
     place = lax.broadcasted_iota(jnp.int32, (S, 1), 0)
-    BQ = 512
+    BQ = 256
     key_i = lax.broadcasted_iota(jnp.int32, (BQ, BQ), 0)
     query_i = lax.broadcasted_iota(jnp.int32, (BQ, BQ), 1)
+    inside = [(lane // 64) == hh for hh in range(2)]
+    feature = [lane == (64 - 64 * hh) for hh in range(2)]
 
     def attend(w, p):
         ending = ends[w]
 
         def part(kind):
-            return lanes(256 * kind + 128 * p)
+            return lanes(384 * p + 128 * kind)
 
         pl_ = lanes(128 * p)
-        keys, values = QKV[w, :, part(1)], QKV[w, :, part(2)]
+        keys = QKV[w, :, part(1)]
         ktT[...] = keys.T
-        vtT[...] = values.T
+        vtT[...] = QKV[w, :, part(2)].T
         doT[...] = dO[w, :, pl_].T
         dkA[...] = jnp.zeros_like(dkA)
         dvA[...] = jnp.zeros_like(dvA)
-
-        def head(hh, carry):
-            inside = (lane // 64) == hh
-            feature = lane == (64 - 64 * hh)
-            t = jnp.where(place < ending, NEG, 0.0)
-            khat[...] = jnp.where(
-                inside, keys.astype(F32), jnp.where(feature, t, 0.0)
-            ).astype(BF)
-            hr = rows(64 * hh, 64)
-            for qb in range(S // BQ):
-                nk = (qb + 1) * BQ
-                qr = slice(qb * BQ, nk)
-                q = QKV[w, qr, part(0)].astype(F32)
-                u = jnp.where(place[qr] >= ending, 1.0, 0.0)
-                q_in = jnp.where(inside, q, 0.0).astype(BF)
-                q_hat = jnp.where(inside, q, jnp.where(feature, u, 0.0)).astype(BF)
-                d_in = jnp.where(inside, dO[w, qr, pl_].astype(F32), 0.0).astype(BF)
-                sc = dot(khat[0:nk, :], q_hat, 1, 1)
-                last = jnp.where(key_i <= query_i, sc[nk - BQ :], NEG)
-                sc = last if qb == 0 else jnp.concatenate([sc[: nk - BQ], last], axis=0)
-                e = jnp.exp(sc - jnp.max(sc, axis=0, keepdims=True))
-                pn = e * (1.0 / jnp.sum(e, axis=0, keepdims=True))
-                pb = pn.astype(BF)
-                o = dot(vtT[hr, 0:nk], pb, 1, 0)
-                oT[hr, qr] = o
-                dp = dot(values[0:nk], d_in, 1, 1)
-                dd = jnp.sum(o * doT[hr, qr].astype(F32), axis=0, keepdims=True)
-                ds = (pn * (dp - dd)).astype(BF)
+        keys_f = keys.astype(F32)
+        before = jnp.where(place < ending, NEG, 0.0)
+        for hh in range(2):
+            khat[hh] = jnp.where(inside[hh], keys_f, jnp.where(feature[hh], before, 0.0)).astype(BF)
+
+        def begin(qb, hh):
+            qr, nk = slice(qb * BQ, (qb + 1) * BQ), (qb + 1) * BQ
+            q = QKV[w, qr, part(0)].astype(F32)
+            after = jnp.where(place[qr] >= ending, 1.0, 0.0)
+            q_in = jnp.where(inside[hh], q, 0.0).astype(BF)
+            q_hat = jnp.where(inside[hh], q, jnp.where(feature[hh], after, 0.0)).astype(BF)
+            d_in = jnp.where(inside[hh], dO[w, qr, pl_].astype(F32), 0.0).astype(BF)
+            return dot(khat[hh, 0:nk, :], q_hat, 1, 1), dot(QKV[w, 0:nk, part(2)], d_in, 1, 1), q_in, d_in
+
+        units = [(qb, hh) for qb in range(S // BQ) for hh in range(2)]
+        upcoming, late = begin(*units[0]), None
+        for i, (qb, hh) in enumerate(units):
+            sc, dp, q_in, d_in = upcoming
+            qr, nk = slice(qb * BQ, (qb + 1) * BQ), (qb + 1) * BQ
+            hr = slice(64 * hh, 64 * hh + 64)
+            if i + 1 < len(units):
+                upcoming = begin(*units[i + 1])
+            last = jnp.where(key_i <= query_i, sc[nk - BQ :], NEG)
+            sc = last if qb == 0 else jnp.concatenate([sc[: nk - BQ], last], axis=0)
+            e = jnp.exp(sc - jnp.max(sc, axis=0, keepdims=True))
+            pn = e * (1.0 / jnp.sum(e, axis=0, keepdims=True))
+            pb = pn.astype(BF)
+            o = dot(vtT[hr, 0:nk], pb, 1, 0)
+            if late is not None:
+                late()
+            oT[hr, qr] = o
+            dd = jnp.sum(o * doT[hr, qr].astype(F32), axis=0, keepdims=True)
+            ds = (pn * (dp - dd)).astype(BF)
+
+            def late(hr=hr, qr=qr, nk=nk, ds=ds, pb=pb, q_in=q_in, d_in=d_in):
                 dqT[hr, qr] = dot(ktT[hr, 0:nk], ds, 1, 0)
                 dkA[0:nk, :] += dot(ds, q_in, 1, 0)
                 dvA[0:nk, :] += dot(pb, d_in, 1, 0)
-            return carry
-
-        lax.fori_loop(0, 2, head, 0)
-        cos_rows, sin_rows = cosine[...], -sine[...]
+
+        late()
+        cos_rows, sin_rows = turn_rows(slice(None))
+        sin_rows = -sin_rows
         att[w, :, pl_] = oT[...].T.astype(BF)
         QKV[w, :, part(0)] = turn(dqT[...].T * 0.125, cos_rows, sin_rows).astype(BF)
         QKV[w, :, part(1)] = turn(dkA[...], cos_rows, sin_rows).astype(BF)
         QKV[w, :, part(2)] = dvA[...].astype(BF)
 
-    def share_step(w):
-        def step(i, total):
-            r = rows(256 * i, 256)
+    shares = (A, H)
+
+    def share_c(w, yy):
+        for t in range(2):
+            src = shares[t].at[w, rows(SL * (2 * yy + oc), SL)]
+            dst = X.at[w, rows(SL * (2 * t + yy), SL)]
+            link.copy("sc", 4 * w + 2 * t + yy, 8, src, dst, core).start()
+
+    def share_got(w, t, yy):
+        slot = X.at[w, rows(SL * (2 * t + yy), SL)]
+        link.copy("sc", 4 * w + 2 * t + yy, 8, slot, slot, core).wait_recv()
+        return slot
+
+    def share_y(w):
+        for t in (1, 0):
+            src = shares[t].at[w, rows(SL * (2 * oy + c), SL)]
+            add_into(src, share_got(w, t, oy))
+            link.copy("sy", 2 * w + t, 4, src, YR.at[w, t], ypart).start()
+
+    def share_step(w, hooks=()):
+        def step(i, carry):
+            yy = jnp.where(i < 2, oy, y)
+            cc = jnp.where(i % 2 == 0, oc, c)
+            r = rows(SL * (2 * yy + cc), SL)
             value = dot(A[w, r, :], Wo[...], 1, 0) + dot(att[w, r, :], Wa[...].reshape(256, 1024), 1, 0)
             A[w, r, :] = value.astype(BF)
             d = dot(H[w, r, :], Wi[...], 1, 1) + dot(QKV[w, r, :], Wq[...], 1, 1)
             H[w, r, :] = d.astype(BF)
             n = (N[w, r, :].astype(F32) - PR[1:2, :]) / PR[0:1, :]
-            return (
-                total[0] + jnp.sum(d, axis=0, keepdims=True),
-                total[1] + jnp.sum(d * n, axis=0, keepdims=True),
+            TAIL[0:1, :] += jnp.sum(d, axis=0, keepdims=True)
+            TAIL[1:2, :] += jnp.sum(d * n, axis=0, keepdims=True)
+
+            @pl.when(i == 0)
+            def _():
+                share_c(w, oy)
+
+            @pl.when(i == 2)
+            def _():
+                share_y(w)
+                share_c(w, y)
+
+            for at, hook in hooks:
+                pl.when(i == at)(hook)
+
+            return carry
+
+        lax.fori_loop(0, 4, step, 0)
+
+    def gq_step(p):
+        for kind in range(3):
+            e = 3 * p + kind
+            l = slice(128 * e, 128 * e + 128)
+            gq = dot(QKV[0, :, l], N[0], 0, 0) + dot(QKV[1, :, l], N[1], 0, 0)
+            for bb in range(8):
+                GQ[e, bb % 2, bb // 2] = gq[:, 128 * bb : 128 * bb + 128].astype(BF)
+            link.copy("qx", e, 6, GQ.at[e, ox], XQ.at[e], xpart).start()
+
+    def ga_c(p):
+        two = slice(2 * p, 2 * p + 2)
+        return link.copy("ac", p, 2, PWI.at[two], GA.at[c, two], core)
+
+    def ga_x(p):
+        two = slice(2 * p, 2 * p + 2)
+        return link.copy("ax", p, 2, GA.at[ox, two], XA.at[two], xpart)
+
+    def ga_step(p):
+        l = slice(128 * p, 128 * p + 128)
+        ga = dot(att[0, :, l], G[0], 0, 0) + dot(att[1, :, l], G[1], 0, 0)
+        for j in range(2):
+            for cc in range(2):
+                piece = ga[64 * j + 32 * cc : 64 * j + 32 * cc + 32].astype(BF)
+
+                @pl.when(cc == c)
+                def _():
+                    GA[c, 2 * p + j] = piece
+
+                @pl.when(cc != c)
+                def _():
+                    PWI[2 * p + j] = piece
+
+        ga_c(p).start()
+
+    def ga_send(p):
+        ga_c(p).wait_recv()
+        ga_x(p).start()
+
+    def z_step(name, group, received, landed, at=0, count=1, waits=None):
+        if waits is None:
+            link.copy(name + "x", at, count, received, received, core).wait_recv()
+        else:
+            waits()
+        for k in (1, 2, 3):
+            zz = (z + k) % 4
+            add_into(group.at[xx, zz], received.at[zz])
+            start(
+                lambda k=k: link.copy(
+                    name + "z",
+                    3 * at + k - 1,
+                    3 * count,
+                    group.at[xx, (z + k) % 4],
+                    landed.at[k - 1],
+                    zdev(k),
+                )
             )
 
-        zero = jnp.zeros((1, 1024), F32)
-        first, second = lax.fori_loop(0, 4, step, (zero, zero))
-        TAIL[0:1, :] += first
-        TAIL[1:2, :] += second
-
-    shares = (A, H)
-
-    def share_c(w):
-        for t in range(2):
-            for yy in range(2):
-                src = shares[t].at[w, rows(SL * (2 * yy + oc), SL)]
-                dst = X.at[w, rows(SL * (2 * t + yy), SL)]
-                link.copy("sc", 4 * w + 2 * t + yy, 8, src, dst, core).start()
-
-    def share_y(w):
-        for t in (1, 0):
-            dst = X.at[w, rows(SL * (2 * t + oy), SL)]
-            for yy in range(2):
-                slot = X.at[w, rows(SL * (2 * t + yy), SL)]
-                link.copy("sc", 4 * w + 2 * t + yy, 8, slot, slot, core).wait_recv()
-            src = shares[t].at[w, rows(SL * (2 * oy + c), SL)]
-            add_into(src, dst)
-            link.copy("sy", 2 * w + t, 4, src, YR.at[w, t], ypart).start()
-
-    def window(w, carry):
-        def pair(p, inner):
-            attend(w, p)
-
-            @pl.when((w == 1) & (p == 0))
-            def _():
-                share_y(0)
-
-            return inner
-
-        lax.fori_loop(0, 2, pair, 0)
-        share_step(w)
-        share_c(w)
+    def of_piece(e):
+        return "q", GQ.at[e], XQ.at[e], ZQ.at[e], e, 6
+
+    def attend_step(i, carry):
+        w, p = i // 2, i % 2
+
+        @pl.when(i == 1)
+        def _():
+            qkv_step(1)
+
+        @pl.when(i == 2)
+        def _():
+            do_step(1)
+
+        attend(w, p)
+
+        @pl.when(i == 0)
+        def _():
+            rows_pass("g", G, 1)
+            gather_pass("wo", 1, 0)
+            gather_pass("wo", 1, 1)
+
+        @pl.when(i == 1)
+        def _():
+            rows_end_far("g", G, 1)
+            gather_pair("wo", 1)
+            for far in (2, 3):
+                for u in range(2):
+                    gather_pass("wo", far, u)
+            lax.fori_loop(0, 4, back_step, 0)
+            first_z(chunk(0))
+            share_step(0)
+            first_z(chunk(1))
+
+        @pl.when(i == 2)
+        def _():
+            gq_step(0)
+            ga_step(0)
+            second_z(chunk(1))
+            first_z(chunk(2))
+            ga_send(0)
+
+        @pl.when(i == 3)
+        def _():
+            gq_step(1)
+            ga_step(1)
+            second_z(chunk(2))
+            ga_send(1)
+            share_step(1, hooks=[(0, lambda: first_z(chunk(3)))])
+
         return carry
 
-    lax.fori_loop(0, 2, window, 0)
-
-    def gq_step(kind, carry):
-        l = lanes(256 * kind, 256)
-        gq = dot(QKV[0, :, l], N[0], 0, 0) + dot(QKV[1, :, l], N[1], 0, 0)
-        for bb in range(8):
-            GQ[bb % 2, bb // 2, rows(256 * kind, 256), :] = gq[:, 128 * bb : 128 * bb + 128].astype(BF)
-        return carry
-
-    lax.fori_loop(0, 3, gq_step, 0)
+    lax.fori_loop(0, 4, attend_step, 0)
+    for e in range(3):
+        z_step(*of_piece(e))
     again = [
         pltpu.make_async_copy(x_in.at[w], N.at[w, 0:SL], local_sems.at[3 * w + 2]) for w in range(2)
     ]
     for cp in again:
         cp.start()
-    start(lambda: link.copy("qx", 0, 1, GQ.at[ox], XQ, xpart))
-    share_y(1)
-    ga = dot(att[0], G[0], 0, 0) + dot(att[1], G[1], 0, 0)
-    for j in range(4):
-        for cc in range(2):
-            at = 64 * j + 32 * cc
-            GAS[cc, j] = ga[at : at + 32].astype(BF)
-    start(lambda: link.copy("ac", 0, 1, GAS.at[oc], GA.at[c], core))
-    GA[c] = GAS[c]
     tail = TAIL[...]
     for bb in range(8):
         GT[bb % 2, bb // 2] = tail[:, 128 * bb : 128 * bb + 128].astype(BF)
     start(lambda: link.copy("tx", 0, 1, GT.at[ox], XT, xpart))
-    link.copy("ac", 0, 1, GAS.at[0], GA.at[oc], core).wait_recv()
-    start(lambda: link.copy("ax", 0, 1, GA.at[ox], XA, xpart))
+
+    written = []
+
+    def write(src, dst):
+        cp = pltpu.make_async_copy(src, dst, out_sems.at[len(written)])
+        cp.start()
+        written.append(cp)
+        return cp
 
     def final_o():
-        for k in (1, 2, 3):
-            link.copy("oz", k - 1, 3, ZO.at[k - 1], ZO.at[k - 1], core).wait_recv()
-        grad_o[...] = (
-            GO[z, xx].astype(F32)
-            + XO[z].astype(F32)
-            + ZO[0].astype(F32)
-            + ZO[1].astype(F32)
-            + ZO[2].astype(F32)
+        o_near(z).wait_recv()
+        link.copy("of", z % 2, 2, ZO.at[1], ZO.at[1], core).wait_recv()
+        dqT[...] = (
+            GO[z, xx].astype(F32) + XO[z].astype(F32) + ZO[0].astype(F32) + ZO[1].astype(F32)
         )
 
     def final_i():
         for q in range(4):
+            total = GI[q, xx, z].astype(F32) + XI[q, z].astype(F32)
             for k in (1, 2, 3):
-                link.copy("iz", 3 * q + k - 1, 12, ZI.at[k - 1, q], ZI.at[k - 1, q], core).wait_recv()
-            total = GI[q, xx, z].astype(F32) + XI[q, z].astype(F32)
-            for k in range(3):
-                total = total + ZI[k, q].astype(F32)
+                i_z(q, k).wait_recv()
+                total = total + ZI[k - 1, q].astype(F32)
             turned = total.T.astype(BF)
             for owner in range(4):
                 SWI[owner, :, 256 * q : 256 * q + 256] = turned[32 * owner : 32 * owner + 32]
 
-    def z_step(name):
-        group, received, _ = sums[name]
-        link.copy(name + "x", 0, 1, received, received, core).wait_recv()
+    def z_total(name, group, received, landed, at=0, count=1):
         for k in (1, 2, 3):
-            zz = (z + k) % 4
-            add_into(group.at[xx, zz], received.at[zz])
-            start(
-                lambda k=k: link.copy(
-                    name + "z", k - 1, 3, group.at[xx, (z + k) % 4], sums[name][2].at[k - 1], zdev(k)
-                )
-            )
-
-    def z_total(name):
-        group, received, landed = sums[name]
-        for k in (1, 2, 3):
-            link.copy(name + "z", k - 1, 3, landed.at[k - 1], landed.at[k - 1], core).wait_recv()
+            link.copy(
+                name + "z", 3 * at + k - 1, 3 * count, landed.at[k - 1], landed.at[k - 1], core
+            ).wait_recv()
         total = group[xx, z].astype(F32) + received[z].astype(F32)
         for k in range(3):
             total = total + landed[k].astype(F32)
         return total
 
+    for e in range(3, 6):
+        z_step(*of_piece(e))
+    z_step("t", GT, XT, ZT)
+    ga_x(0).wait_recv()
+    z_step("a", GA, XA, ZA, waits=lambda: ga_x(1).wait_recv())
     final_o()
+    write(dqT, grad_o_hbm)
     final_i()
     RWI[s] = SWI[s]
     seq_sends("swi", lambda owner: SWI.at[owner], lambda: RWI.at[s])
 
-    z_step("q")
-    z_step("t")
-    z_step("a")
 
     def final_rows(w, carry):
         again[w].wait()
         v = N[w, 0:SL, :].astype(F32)
         mine = rows(SL * s, SL)
         for t in (1, 0):
+            share_got(w, t, y)
             link.copy("sy", 2 * w + t, 4, YR.at[w, t], YR.at[w, t], core).wait_recv()
         value = (
             A[w, mine, :].astype(F32)
             + X[w, rows(SL * y, SL), :].astype(F32)
             + YR[w, 0].astype(F32)
         )
-        out[w] = (v + value + PR[2:3, :]).astype(BF)
+        A[w, mine, :] = (v + value + PR[2:3, :]).astype(BF)
         d = (
             H[w, mine, :].astype(F32)
             + X[w, rows(SL * (2 + y), SL), :].astype(F32)
@@ -923,22 +1230,25 @@
         v = v * scale
         d = d * PR[0:1, :]
         d = d - jnp.mean(d, axis=-1, keepdims=True) - v * jnp.mean(d * v, axis=-1, keepdims=True)
-        grad_in[w] = G[w, mine, :].astype(F32) + scale * d
+        grad_in[...] = G[w, mine, :].astype(F32) + scale * d
         return carry
 
     final_rows(0, 0)
-
-    total_q = z_total("q")
-    total_t = z_total("t")
-    grad_bin[...] = total_t[0:8]
-    turned_q = total_q.T.astype(BF)
+    write(A.at[0, own], out_hbm.at[0])
+    first_rows = write(grad_in, grad_in_hbm.at[0])
+
+    for e in range(6):
+        total_q = z_total(*of_piece(e)).T.astype(BF)
+        for owner in range(4):
+            SWQ[owner, :, 128 * e : 128 * e + 128] = total_q[32 * owner : 32 * owner + 32]
+    total_t = z_total("t", GT, XT, ZT)
     turned_t = jnp.concatenate([total_t, jnp.zeros((112, 128), F32)], axis=0).T.astype(BF)
     for owner in range(4):
-        SWQ[owner, :, 0:768] = turned_q[32 * owner : 32 * owner + 32]
         SWQ[owner, :, 768:896] = turned_t[32 * owner : 32 * owner + 32]
     RWQ[s] = SWQ[s]
     seq_sends("swq", lambda owner: SWQ.at[owner], lambda: RWQ.at[s])
-    grad_a[...] = z_total("a")
+    grad_a[...] = z_total("a", GA, XA, ZA)
+    write(grad_a, grad_a_hbm)
 
     def from_seq(name, landed):
         for i, owner in enumerate((2 * y + oc, 2 * oy + c, 2 * oy + oc)):
@@ -948,9 +1258,16 @@
     for r in range(4):
         for blk in range(8):
             at = 512 * blk + 128 * r
-            grad_i[:, at : at + 128] = RWI[r, :, 128 * blk : 128 * blk + 128].astype(F32)
-
+            oT[32 * (at // 1024) : 32 * (at // 1024) + 32, at % 1024 : at % 1024 + 128] = RWI[
+                r, :, 128 * blk : 128 * blk + 128
+            ].astype(F32)
+
+    for q in range(4):
+        write(oT.at[32 * q : 32 * q + 32], grad_i_hbm.at[:, 1024 * q : 1024 * q + 1024])
+    first_rows.wait()
     final_rows(1, 0)
+    write(A.at[1, own], out_hbm.at[1])
+    write(grad_in, grad_in_hbm.at[1])
 
     from_seq("swq", RWQ)
     got = [RWQ[r].astype(F32) for r in range(4)]
@@ -958,25 +1275,31 @@
     for r in range(4):
         for j in range(4):
             for kind in range(3):
-                place_of[3 * head_of(r, j) + kind] = (got[r], 256 * kind + 128 * (j // 2) + 64 * (j % 2))
+                place_of[3 * head_of(r, j) + kind] = (got[r], 384 * (j // 2) + 128 * kind + 64 * (j % 2))
     for at in range(24):
         grad_q[:, 128 * at : 128 * at + 128] = halves(place_of[2 * at], place_of[2 * at + 1])
+    write(grad_q, grad_q_hbm)
     summed = got[0][:, 768:896] + got[1][:, 768:896] + got[2][:, 768:896] + got[3][:, 768:896]
-    grad_small[...] = jnp.where(lane == 2, got[0][:, 768:896], summed)
+    summed = jnp.where(lane == 2, got[0][:, 768:896], summed)
+    summed = jnp.concatenate([summed, jnp.zeros((96, 128), F32)], axis=0).T
+    grad_small[...] = jnp.where(lax.broadcasted_iota(jnp.int32, (8, 128), 0) < 3, summed[0:8], total_t[0:8])
+    write(grad_small, grad_small_hbm)
 
     for make in pending:
         make().wait_send()
+    seq_left("prms", lambda owner: prm_block(s), lambda: prm_block(s))
+    seq_left("wqs", lambda owner: PWQ.at[owner], lambda: wq_block(s))
+    seq_left("swi", lambda owner: SWI.at[owner], lambda: RWI.at[s])
+    seq_left("swq", lambda owner: SWQ.at[owner], lambda: RWQ.at[s])
+    for name, (parts, _) in gathers.items():
+        for u in range(parts):
+            gather_left(name, u)
     for w in range(2):
         rows_left("g", G, w)
     for q in range(4):
         link.copy("ox", q, 4, GO.at[q, ox], XO.at[q], xpart).wait_send()
         link.copy("ix", q, 4, GI.at[q, ox], XI.at[q], xpart).wait_send()
-        for k in (1, 2, 3):
-            zz = (z + k) % 4
-            link.copy("iz", 3 * q + k - 1, 12, GI.at[q, xx, zz], ZI.at[k - 1, q], zdev(k)).wait_send()
-    for k in (1, 2, 3):
-        zz = (z + k) % 4
-        link.copy("oz", k - 1, 3, GO.at[zz, xx], ZO.at[k - 1], zdev(k)).wait_send()
+    z_left()
     for w in range(2):
         for t in range(2):
             for yy in range(2):
@@ -985,6 +1308,34 @@
                 link.copy("sc", 4 * w + 2 * t + yy, 8, src, dst, core).wait_send()
             src = shares[t].at[w, rows(SL * (2 * oy + c), SL)]
             link.copy("sy", 2 * w + t, 4, src, YR.at[w, t], ypart).wait_send()
+    for e in range(6):
+        link.copy("qx", e, 6, GQ.at[e, ox], XQ.at[e], xpart).wait_send()
+    for p in range(2):
+        ga_c(p).wait_send()
+        ga_x(p).wait_send()
+    for cp in written:
+        if cp is not first_rows:
+            cp.wait()
+
+
+def publish(*refs):
+    sources, small, targets, row_targets = refs[:6], refs[6], refs[7:13], refs[13:17]
+    held, (in_sems, out_sems) = refs[17:23], refs[23:]
+    arrive = [
+        pltpu.make_async_copy(sources[i], held[i], in_sems.at[i]) for i in range(6)
+    ]
+    leave = [
+        pltpu.make_async_copy(held[i], targets[i], out_sems.at[i]) for i in range(6)
+    ]
+    for cp in arrive:
+        cp.start()
+    for i, target in enumerate(row_targets):
+        target[...] = small[i : i + 1, 0 : target.shape[1]]
+    for i in range(6):
+        arrive[i].wait()
+        leave[i].start()
+    for cp in leave:
+        cp.wait()
 
 
 def turn_tables(seq_len):
@@ -995,7 +1346,7 @@
     cosine[:, 0:ROTARY:2] = cosine[:, 1:ROTARY:2] = np.cos(angles)
     sine[:, 0:ROTARY:2] = -np.sin(angles)
     sine[:, 1:ROTARY:2] = np.sin(angles)
-    return np.tile(cosine, (1, 2)), np.tile(sine, (1, 2))
+    return np.concatenate([cosine, sine], axis=1)
 
 
 def fused_shards(inputs, ends, ln_gain, ln_bias, w_qkv, w_attn, w_in, b_in, w_out, b_out, cotangent):
@@ -1003,24 +1354,22 @@
         return jnp.pad(v, (0, 128 - v.shape[0]))
 
     prm = jnp.pad(jnp.stack([widen(ln_gain), widen(ln_bias), widen(b_out), b_in]), ((0, 12), (0, 0)))
-    cosine, sine = turn_tables(1024)
     in_vmem = pl.BlockSpec(memory_space=pltpu.VMEM)
     in_any = pl.BlockSpec(memory_space=pl.ANY)
     rows_type = (2, 1024, 1024)
+    shapes = (
+        jax.ShapeDtypeStruct((2, 256, 1024), BF),
+        jax.ShapeDtypeStruct((2, 256, 1024), F32),
+        jax.ShapeDtypeStruct((32, 3072), F32),
+        jax.ShapeDtypeStruct((32, 1024), F32),
+        jax.ShapeDtypeStruct((32, 4096), F32),
+        jax.ShapeDtypeStruct((128, 1024), F32),
+    )
     results = pl.pallas_call(
         fused_layer,
-        out_shape=(
-            jax.ShapeDtypeStruct((2, 256, 1024), BF),
-            jax.ShapeDtypeStruct((2, 256, 1024), F32),
-            jax.ShapeDtypeStruct((32, 3072), F32),
-            jax.ShapeDtypeStruct((32, 1024), F32),
-            jax.ShapeDtypeStruct((32, 4096), F32),
-            jax.ShapeDtypeStruct((128, 1024), F32),
-            jax.ShapeDtypeStruct((32, 128), F32),
-            jax.ShapeDtypeStruct((8, 128), F32),
-        ),
-        in_specs=[pl.BlockSpec(memory_space=pltpu.SMEM)] + [in_vmem] * 7 + [in_any] * 2,
-        out_specs=(in_vmem,) * 8,
+        out_shape=shapes + (jax.ShapeDtypeStruct((8, 128), F32),),
+        in_specs=[pl.BlockSpec(memory_space=pltpu.SMEM)] + [in_vmem] * 6 + [in_any] * 2,
+        out_specs=(in_any,) * 7,
         scratch_shapes=[
             pltpu.VMEM(rows_type, BF),
             pltpu.VMEM(rows_type, BF),
@@ -1034,24 +1383,25 @@
             pltpu.VMEM((4, 2, 32, 1024), BF),
             pltpu.VMEM((4, 32, 1024), BF),
             pltpu.VMEM((4, 32, 768), BF),
-            pltpu.VMEM((8, 64, 128), BF),
+            pltpu.VMEM((4, 16, 128), BF),
+            pltpu.VMEM((8, 16, 128), BF),
             pltpu.VMEM((8, 1024), F32),
             pltpu.VMEM((2, 1024, 768), BF),
             pltpu.VMEM((2, 1024, 256), BF),
             pltpu.VMEM((2, 1024, 256), BF),
             pltpu.VMEM((4, 2, 128, 1024), BF),
             pltpu.VMEM((4, 128, 1024), BF),
-            pltpu.VMEM((3, 128, 1024), BF),
+            pltpu.VMEM((2, 128, 1024), BF),
+            pltpu.VMEM((2, 128, 1024), BF),
             pltpu.VMEM((4, 2, 4, 256, 128), BF),
             pltpu.VMEM((4, 4, 256, 128), BF),
             pltpu.VMEM((3, 4, 256, 128), BF),
-            pltpu.VMEM((2, 4, 768, 128), BF),
-            pltpu.VMEM((4, 768, 128), BF),
-            pltpu.VMEM((3, 768, 128), BF),
+            pltpu.VMEM((6, 2, 4, 128, 128), BF),
+            pltpu.VMEM((6, 4, 128, 128), BF),
+            pltpu.VMEM((6, 3, 128, 128), BF),
             pltpu.VMEM((2, 4, 32, 1024), BF),
             pltpu.VMEM((4, 32, 1024), BF),
             pltpu.VMEM((3, 32, 1024), BF),
-            pltpu.VMEM((2, 4, 32, 1024), BF),
             pltpu.VMEM((2, 4, 16, 128), BF),
             pltpu.VMEM((4, 16, 128), BF),
             pltpu.VMEM((3, 16, 128), BF),
@@ -1061,7 +1411,7 @@
             pltpu.VMEM((4, 32, 896), BF),
             pltpu.VMEM((4, 32, 896), BF),
             pltpu.VMEM((16, 1024), F32),
-            pltpu.VMEM((1024, 128), BF),
+            pltpu.VMEM((2, 1024, 128), BF),
             pltpu.VMEM((128, 1024), BF),
             pltpu.VMEM((128, 1024), BF),
             pltpu.VMEM((128, 1024), BF),
@@ -1069,27 +1419,42 @@
             pltpu.VMEM((128, 1024), F32),
             pltpu.VMEM((1024, 128), F32),
             pltpu.VMEM((1024, 128), F32),
-            pltpu.SemaphoreType.DMA((160,)),
-            pltpu.SemaphoreType.DMA((160,)),
+            pltpu.VMEM((256, 1024), F32),
+            pltpu.VMEM((32, 3072), F32),
+            pltpu.VMEM((32, 1024), F32),
+            pltpu.VMEM((8, 128), F32),
+            pltpu.SemaphoreType.DMA((210,)),
+            pltpu.SemaphoreType.DMA((210,)),
             pltpu.SemaphoreType.DMA((6,)),
+            pltpu.SemaphoreType.DMA((12,)),
         ],
         compiler_params=pltpu.CompilerParams(
-            collective_id=0, has_side_effects=True, vmem_limit_bytes=63 * 2**20
+            collective_id=0, has_side_effects=True, vmem_limit_bytes=65400 * 2**10
         ),
         cost_estimate=pl.CostEstimate(flops=46 * 10**9, bytes_accessed=10**7, transcendentals=10**7),
-    )(ends, prm, w_qkv, w_attn, w_in, w_out, cosine, sine, inputs, cotangent)
-    out, grad_in, grad_q, grad_a, grad_i, grad_o, small, bias_in = results
+    )(ends, prm, w_qkv, w_attn, w_in, w_out, turn_tables(1024), inputs, cotangent)
+    row = jax.ShapeDtypeStruct((1, 32), F32)
+    final = pl.pallas_call(
+        publish,
+        out_shape=shapes + (row, row, row, jax.ShapeDtypeStruct((1, 128), F32)),
+        in_specs=[in_any] * 6 + [in_vmem],
+        out_specs=(in_any,) * 6 + (in_vmem,) * 4,
+        scratch_shapes=[pltpu.VMEM(v.shape, v.dtype) for v in shapes]
+        + [pltpu.SemaphoreType.DMA((6,)), pltpu.SemaphoreType.DMA((6,))],
+        compiler_params=pltpu.CompilerParams(vmem_limit_bytes=60 * 2**20),
+    )(*results)
+    out, grad_in, grad_q, grad_a, grad_i, grad_o, bias, gain, bias_out, bias_in = final
     return (
         out,
         grad_in,
-        small[:, 1],
-        small[:, 0],
+        gain.reshape(32),
+        bias.reshape(32),
         grad_q,
         grad_a,
         grad_i,
-        bias_in[3],
+        bias_in.reshape(128),
         grad_o,
-        small[:, 2],
+        bias_out.reshape(32),
     )
 
 

time: 240 us -> 180 us (0.75)
  Pallas kernels: 227 us -> 177 us
  local copies, waits for them, and re-layouts: 10.8 us -> 1.34 us
    pallas_call x1 -> x2, Pallas kernels: 227 us -> 177 us  [the longest x1 172 us: fused_shards(): pl.pallas_call(fused_layer, out_shape=shapes + (jax.ShapeDtypeStruct((8,...]
    unnamed x16 -> x0, local copies, waits for them, and re-layouts: 6.59 us -> none
where the time goes in v2:
time: 180 us
  Pallas kernels  177 us (98%)
    pallas_call x1, Pallas kernels, fused_shards(): pl.pallas_call(fused_layer, out_shape=shapes + (jax.ShapeDtypeStruct((8,...  172 us
    pallas_call x1, Pallas kernels, fused_shards(): pl.pallas_call(publish, out_shape=shapes + (row, row, row, jax.ShapeDtype...  5.06 us

profile of v2, /device:TPU:0, one launch (start us, length us, event | category | flops | bytes accessed | tf_op | source)
XLA Modules:
  0.0 180.3 jit_solution(5080288077489133657)
XLA Ops:
  0.6 0.7 pad_bitcast_fusion.2
  1.3 0.7 pad_bitcast_fusion
  2.0 1.3 fusion.6.prm
  3.2 171.8 %shard_map.195 = (bf16[2,256,1024]{2,1,0:T(8,128)(2,1)}, f32[2,256,1024]{2,1,0:T(8,128)}, f32[32,3072]{1,0:T(8,128)}, f32[32,1024]{1,0:T(8,128)}, f32[32,4096]{1...) custom-call(s32[2]{0:T(128)} %ends.1, bf16[16,128]{1,0:T(8,128)(2,1)} %fusion.6.prm, bf16[32,3072]{1,0:T(8,128)(2,1)} %wq.1, ...), custom_call_target="tpu_custom_call" | custom-call | flops 46000001024 | bytes 10000000 | tf_op jit(solution)/shard_map/pallas_call | solution.py:1368
  175.0 5.1 %shard_map.196 = (bf16[2,256,1024]{2,1,0:T(8,128)(2,1)}, f32[2,256,1024]{2,1,0:T(8,128)}, f32[32,3072]{1,0:T(8,128)}, f32[32,1024]{1,0:T(8,128)}, f32[32,4096]{1...) custom-call(bf16[2,256,1024]{2,1,0:T(8,128)(2,1)} %get-tuple-element, ...), custom_call_target="tpu_custom_call" | custom-call | tf_op jit(solution)/shard_map/pallas_call | solution.py:1437

commit v3 on v2

--- a/solution.py
+++ b/solution.py
@@ -379,7 +379,7 @@
     out_hbm, grad_in_hbm, grad_q_hbm, grad_a_hbm, grad_i_hbm, grad_o_hbm, grad_small_hbm,
     X, N, G, A, H, Wi, Wo, Wq, WaAll, Wa, PWI, PWQ, PRS, PRM, PR, QKV, att, dO,
     GO, XO, ZO, CO, GI, XI, ZI, GQ, XQ, ZQ, GA, XA, ZA, GT, XT, ZT,
-    YR, SWI, RWI, SWQ, RWQ, TAIL,
+    YR, SWI, RWI, SWQ, RWQ, SWT, RWT, TAIL,
     khat, ktT, vtT, doT, oT, dqT, dkA, dvA,
     grad_in, grad_q, grad_a, grad_small,
     send_sems, recv_sems, local_sems, out_sems,
@@ -496,12 +496,6 @@
     def x_copy(name, zz, side, u):
         return gather_copy(name, "x", zz, 4, zz, side, u, xpart)
 
-    def pair_copy(name, zz, u):
-        return gather_copy(name, "p", 0, 1, zz, ox, u, (2 * pair + xx, s))
-
-    def by_pair(name, u):
-        return name in ("wi", "wo") and 2 * u >= gathers[name][0]
-
     def gather_z(name, u):
         if name == "wi":
 
@@ -527,16 +521,6 @@
     def gather_x(name, u):
         x_copy(name, z, xx, u).start()
 
-    def hand_over(name, zz, u):
-        if by_pair(name, u):
-
-            @pl.when(zz != pair)
-            def _():
-                x_copy(name, zz, xx, u).start()
-
-        else:
-            x_copy(name, zz, xx, u).start()
-
     def gather_pass(name, far, u):
         @pl.when(z >= far)
         def _():
@@ -549,7 +533,7 @@
 
             else:
                 z_copy(name, z - far, far, u).wait_recv()
-            hand_over(name, z - far, u)
+            x_copy(name, z - far, xx, u).start()
 
         @pl.when(z + far <= 3)
         def _():
@@ -562,25 +546,10 @@
 
             else:
                 z_copy(name, z + far, 4 - far, u).wait_recv()
-            hand_over(name, z + far, u)
-
-    def gather_pair(name, u):
-        x_copy(name, z, ox, u).wait_recv()
-        pair_copy(name, z, u).start()
+            x_copy(name, z + far, xx, u).start()
 
     def gather_block(name, zz, u):
-        if by_pair(name, u):
-
-            @pl.when((zz != pair) & (zz != z))
-            def _():
-                x_copy(name, zz, ox, u).wait_recv()
-
-            @pl.when(zz == pair)
-            def _():
-                pair_copy(name, pair, u).wait_recv()
-
-        else:
-            x_copy(name, zz, ox, u).wait_recv()
+        x_copy(name, zz, ox, u).wait_recv()
 
     def gather_end(name, u):
         for zz in range(4):
@@ -601,17 +570,7 @@
                 def _():
                     down_copy(name, zz, u).wait_send()
 
-            if by_pair(name, u):
-
-                @pl.when(zz != pair)
-                def _():
-                    x_copy(name, zz, xx, u).wait_send()
-
-            else:
-                x_copy(name, zz, xx, u).wait_send()
-
-        if by_pair(name, u):
-            pair_copy(name, z, u).wait_send()
+            x_copy(name, zz, xx, u).wait_send()
 
     def rows_start(name, src, dst):
         for w in range(2):
@@ -693,16 +652,17 @@
     gather_pass("wi", 2, 0)
     gather_pass("wi", 1, 2)
     gather_pass("wi", 1, 3)
+    seq_waits("wqs", wq_block(s), wq_block)
+    gather_z("wq", 0)
+    gather_x("wq", 0)
     gather_pass("wi", 2, 1)
     gather_pass("wi", 3, 0)
     gather_pass("wi", 2, 2)
-    gather_pair("wi", 2)
     gather_pass("wi", 3, 1)
     rows_pass("x", X, 0)
     gather_pass("wi", 2, 3)
-    gather_pair("wi", 3)
-    seq_waits("wqs", wq_block(s), wq_block)
-    gather_z("wq", 0)
+    gather_z("wq", 1)
+    gather_x("wq", 1)
 
     def hidden_step(i, carry):
         early = i < 12
@@ -722,13 +682,14 @@
         @pl.when(i == 3)
         def _():
             gather_pass("wi", 3, 2)
-            gather_x("wq", 0)
             gather_end("wi", 1)
 
         @pl.when(i == 5)
         def _():
             gather_pass("wi", 3, 3)
-            gather_z("wq", 1)
+            gather_z("wo", 0)
+            gather_z("wo", 1)
+            gather_pass("wq", 1, 0)
 
         @pl.when(i == 6)
         def _():
@@ -740,15 +701,21 @@
 
         @pl.when(i == 9)
         def _():
-            gather_pass("wq", 1, 0)
+            gather_pass("wq", 2, 0)
             gather_end("wi", 3)
 
+        @pl.when(i == 11)
+        def _():
+            gather_pass("wq", 3, 0)
+
         @pl.when(i == 12)
         def _():
-            gather_pass("wq", 2, 0)
-            gather_pass("wq", 3, 0)
-            gather_x("wq", 1)
             norm_far(1)
+
+        @pl.when(i == 14)
+        def _():
+            gather_pass("wq", 1, 1)
+            gather_x("wo", 1)
 
         r, l = rows(512 * t, 512), lanes(256 * u, 256)
         v = dot(N[w, r, :], Wi[:, l], 1, 0) + PR[3:4, l]
@@ -758,16 +725,13 @@
         return carry
 
     lax.fori_loop(0, 16, hidden_step, 0)
-    for u in range(2):
-        gather_z("wo", u)
     for w in range(2):
         rows_left("x", X, w)
     gather_end("wa", 0)
     start(lambda: link.copy("wac", 0, 1, WaAll.at[:, oc], Wa.at[:, c], core))
     Wa[:, c] = WaAll[:, c]
-    for far in (1, 2, 3):
+    for far in (2, 3):
         gather_pass("wq", far, 1)
-    gather_x("wo", 1)
 
     def add_into(dst, other):
         dst[...] = (dst[...].astype(F32) + other[...].astype(F32)).astype(BF)
@@ -792,8 +756,8 @@
     def i_z(q, k):
         return link.copy("iz", 3 * q + k - 1, 12, GI.at[q, xx, (z + k) % 4], ZI.at[k - 1, q], zdev(k))
 
-    def first_z(q):
-        link.copy("ox", q, 4, XO.at[q], XO.at[q], core).wait_recv()
+    def first_o(q):
+        o_x(q).wait_recv()
 
         @pl.when(z != q)
         def _():
@@ -807,7 +771,8 @@
             def _():
                 o_comb(q).start()
 
-        link.copy("ix", q, 4, XI.at[q], XI.at[q], core).wait_recv()
+    def first_i(q):
+        i_x(q).wait_recv()
         for k in (1, 2, 3):
             zz = (z + k) % 4
             add_into(GI.at[q, xx, zz], XI.at[q, zz])
@@ -837,11 +802,13 @@
                 i_z(q, k).wait_send()
 
     def chunk(j):
-        return jnp.where(j == 0, z, jnp.where(j == 3, pair, far_chip(0) + j - 1))
-
-    def send_x(q):
-        link.copy("ox", q, 4, GO.at[q, ox], XO.at[q], xpart).start()
-        link.copy("ix", q, 4, GI.at[q, ox], XI.at[q], xpart).start()
+        return jnp.where(j == 3, z, jnp.where(j == 2, pair, far_chip(0) + j))
+
+    def o_x(q):
+        return link.copy("ox", q, 4, GO.at[q, ox], XO.at[q], xpart)
+
+    def i_x(q):
+        return link.copy("ix", q, 4, GI.at[q, ox], XI.at[q], xpart)
 
     even = lax.broadcasted_iota(jnp.int32, (1, 128), 1) % 2 == 0
 
@@ -897,30 +864,32 @@
     rows_end_far("g", G, 0)
     do_step(0)
 
-    def back_step(j, carry):
+    def units_back(j):
         q = chunk(j)
         l = lanes(256 * q, 256)
-        gather_block("wo", q, 0)
-        gather_block("wo", q, 1)
-
-        def dh_step(i, total):
+
+        def step(i, total):
             w, r = i // 2, rows(512 * (i % 2), 512)
             d = dot(G[w, r, :], Wo[rows(256 * q, 256), :], 1, 1) * H[w, r, l].astype(F32)
             d = d.astype(BF)
             H[w, r, l] = d
             return total + jnp.sum(d.astype(F32), axis=0, keepdims=True)
 
-        TAIL[3:4, l] = lax.fori_loop(0, 4, dh_step, jnp.zeros((1, 256), F32))
+        TAIL[3:4, l] = lax.fori_loop(0, 4, step, jnp.zeros((1, 256), F32))
+
+    def units_out(j):
+        q = chunk(j)
+        l = lanes(256 * q, 256)
         go = dot(A[0, :, l], G[0], 0, 0) + dot(A[1, :, l], G[1], 0, 0)
         GO[q, 0] = go[:128].astype(BF)
         GO[q, 1] = go[128:].astype(BF)
+
+    def units_in(j):
+        q = chunk(j)
+        l = lanes(256 * q, 256)
         gi = dot(H[0, :, l], N[0], 0, 0) + dot(H[1, :, l], N[1], 0, 0)
         for bb in range(8):
             GI[q, bb % 2, bb // 2] = gi[:, 128 * bb : 128 * bb + 128].astype(BF)
-
-        send_x(q)
-
-        return carry
 
     lane = lax.broadcasted_iota(jnp.int32, (1, 128), 1)
     place = lax.broadcasted_iota(jnp.int32, (S, 1), 0)
@@ -992,47 +961,46 @@
 
     shares = (A, H)
 
-    def share_c(w, yy):
-        for t in range(2):
-            src = shares[t].at[w, rows(SL * (2 * yy + oc), SL)]
-            dst = X.at[w, rows(SL * (2 * t + yy), SL)]
-            link.copy("sc", 4 * w + 2 * t + yy, 8, src, dst, core).start()
+    def share_c(w, t, yy):
+        src = shares[t].at[w, rows(SL * (2 * yy + oc), SL)]
+        dst = X.at[w, rows(SL * (2 * t + yy), SL)]
+        link.copy("sc", 4 * w + 2 * t + yy, 8, src, dst, core).start()
 
     def share_got(w, t, yy):
         slot = X.at[w, rows(SL * (2 * t + yy), SL)]
         link.copy("sc", 4 * w + 2 * t + yy, 8, slot, slot, core).wait_recv()
         return slot
 
-    def share_y(w):
-        for t in (1, 0):
-            src = shares[t].at[w, rows(SL * (2 * oy + c), SL)]
-            add_into(src, share_got(w, t, oy))
-            link.copy("sy", 2 * w + t, 4, src, YR.at[w, t], ypart).start()
-
-    def share_step(w, hooks=()):
+    def share_y(w, t):
+        src = shares[t].at[w, rows(SL * (2 * oy + c), SL)]
+        add_into(src, share_got(w, t, oy))
+        link.copy("sy", 2 * w + t, 4, src, YR.at[w, t], ypart).start()
+
+    def share_out(w, r):
+        value = dot(A[w, r, :], Wo[...], 1, 0) + dot(att[w, r, :], Wa[...].reshape(256, 1024), 1, 0)
+        A[w, r, :] = value.astype(BF)
+
+    def share_normed(w, r):
+        d = dot(H[w, r, :], Wi[...], 1, 1) + dot(QKV[w, r, :], Wq[...], 1, 1)
+        H[w, r, :] = d.astype(BF)
+        n = (N[w, r, :].astype(F32) - PR[1:2, :]) / PR[0:1, :]
+        TAIL[0:1, :] += jnp.sum(d, axis=0, keepdims=True)
+        TAIL[1:2, :] += jnp.sum(d * n, axis=0, keepdims=True)
+
+    def share_step(w, t):
         def step(i, carry):
             yy = jnp.where(i < 2, oy, y)
             cc = jnp.where(i % 2 == 0, oc, c)
-            r = rows(SL * (2 * yy + cc), SL)
-            value = dot(A[w, r, :], Wo[...], 1, 0) + dot(att[w, r, :], Wa[...].reshape(256, 1024), 1, 0)
-            A[w, r, :] = value.astype(BF)
-            d = dot(H[w, r, :], Wi[...], 1, 1) + dot(QKV[w, r, :], Wq[...], 1, 1)
-            H[w, r, :] = d.astype(BF)
-            n = (N[w, r, :].astype(F32) - PR[1:2, :]) / PR[0:1, :]
-            TAIL[0:1, :] += jnp.sum(d, axis=0, keepdims=True)
-            TAIL[1:2, :] += jnp.sum(d * n, axis=0, keepdims=True)
+            (share_out, share_normed)[t](w, rows(SL * (2 * yy + cc), SL))
 
             @pl.when(i == 0)
             def _():
-                share_c(w, oy)
+                share_c(w, t, oy)
 
             @pl.when(i == 2)
             def _():
-                share_y(w)
-                share_c(w, y)
-
-            for at, hook in hooks:
-                pl.when(i == at)(hook)
+                share_y(w, t)
+                share_c(w, t, y)
 
             return carry
 
@@ -1076,7 +1044,13 @@
         ga_c(p).wait_recv()
         ga_x(p).start()
 
-    def z_step(name, group, received, landed, at=0, count=1, waits=None):
+    def z_send(get, k):
+        name, group, _, landed, at, count = get()
+        src = group.at[xx, (z + k) % 4]
+        return link.copy(name + "z", 3 * at + k - 1, 3 * count, src, landed.at[k - 1], zdev(k))
+
+    def z_step(get, waits=None):
+        name, group, received, _, at, count = get()
         if waits is None:
             link.copy(name + "x", at, count, received, received, core).wait_recv()
         else:
@@ -1084,72 +1058,126 @@
         for k in (1, 2, 3):
             zz = (z + k) % 4
             add_into(group.at[xx, zz], received.at[zz])
-            start(
-                lambda k=k: link.copy(
-                    name + "z",
-                    3 * at + k - 1,
-                    3 * count,
-                    group.at[xx, (z + k) % 4],
-                    landed.at[k - 1],
-                    zdev(k),
-                )
-            )
+            start(lambda k=k: z_send(get, k))
 
     def of_piece(e):
-        return "q", GQ.at[e], XQ.at[e], ZQ.at[e], e, 6
+        return lambda: ("q", GQ.at[e], XQ.at[e], ZQ.at[e], e, 6)
+
+    def of_attn():
+        return "a", GA, XA, ZA, 0, 1
 
     def attend_step(i, carry):
         w, p = i // 2, i % 2
-
-        @pl.when(i == 1)
-        def _():
+        attend(w, p)
+
+        @pl.when(i == 0)
+        def _():
+            for u in range(2):
+                gather_pass("wo", 1, u)
+            rows_pass("g", G, 1)
             qkv_step(1)
-
-        @pl.when(i == 2)
-        def _():
-            do_step(1)
-
-        attend(w, p)
-
-        @pl.when(i == 0)
-        def _():
-            rows_pass("g", G, 1)
-            gather_pass("wo", 1, 0)
-            gather_pass("wo", 1, 1)
-
-        @pl.when(i == 1)
-        def _():
-            rows_end_far("g", G, 1)
-            gather_pair("wo", 1)
             for far in (2, 3):
                 for u in range(2):
                     gather_pass("wo", far, u)
-            lax.fori_loop(0, 4, back_step, 0)
-            first_z(chunk(0))
-            share_step(0)
-            first_z(chunk(1))
+
+        @pl.when(i == 1)
+        def _():
+            rows_end_far("g", G, 1)
+            do_step(1)
 
         @pl.when(i == 2)
         def _():
             gq_step(0)
             ga_step(0)
-            second_z(chunk(1))
-            first_z(chunk(2))
-            ga_send(0)
-
-        @pl.when(i == 3)
-        def _():
-            gq_step(1)
-            ga_step(1)
-            second_z(chunk(2))
+
+        return carry
+
+    lax.fori_loop(0, 4, attend_step, 0)
+    ga_send(0)
+    gq_step(1)
+    ga_step(1)
+    def out_step(j, carry):
+        units_out(j)
+
+        @pl.when(j == 0)
+        def _():
+            z_step(of_piece(0))
+            z_step(of_piece(1))
             ga_send(1)
-            share_step(1, hooks=[(0, lambda: first_z(chunk(3)))])
+
+        @pl.when(j == 2)
+        def _():
+            z_step(of_piece(2))
 
         return carry
 
-    lax.fori_loop(0, 4, attend_step, 0)
-    for e in range(3):
-        z_step(*of_piece(e))
+    def in_step(j, carry):
+        units_back(j)
+        units_in(j)
+        i_x(chunk(j)).start()
+
+        @pl.when(j == 0)
+        def _():
+            z_step(of_piece(4))
+            z_step(of_piece(5))
+
+        @pl.when(j == 1)
+        def _():
+            ga_x(0).wait_recv()
+            z_step(of_attn, waits=lambda: ga_x(1).wait_recv())
+
+        return carry
+
+    written = []
+
+    def write(src, dst):
+        cp = pltpu.make_async_copy(src, dst, out_sems.at[len(written)])
+        cp.start()
+        written.append(cp)
+        return cp
+
+    def z_total(get):
+        name, group, received, landed, at, count = get()
+        for k in (1, 2, 3):
+            link.copy(
+                name + "z", 3 * at + k - 1, 3 * count, landed.at[k - 1], landed.at[k - 1], core
+            ).wait_recv()
+        total = group[xx, z].astype(F32) + received[z].astype(F32)
+        for k in range(3):
+            total = total + landed[k].astype(F32)
+        return total
+
+    def to_seq(name, held, landed):
+        landed[s] = held[s]
+        seq_sends(name, lambda owner: held.at[owner], lambda: landed.at[s])
+
+    def from_seq(name, landed):
+        for i, owner in enumerate((2 * y + oc, 2 * oy + c, 2 * oy + oc)):
+            link.copy(name, i, 3, landed.at[owner], landed.at[owner], core).wait_recv()
+
+    lax.fori_loop(0, 4, out_step, 0)
+    for u in range(2):
+        for zz in range(4):
+            gather_block("wo", zz, u)
+    share_step(0, 0)
+    z_step(of_piece(3))
+    lax.fori_loop(0, 2, in_step, 0)
+    share_step(1, 0)
+    first_i(chunk(0))
+    lax.fori_loop(2, 4, in_step, 0)
+    for j in range(4):
+        o_x(chunk(j)).start()
+    first_i(chunk(1))
+    for e in range(6):
+        total_q = z_total(of_piece(e)).T.astype(BF)
+        for owner in range(4):
+            SWQ[owner, :, 128 * e : 128 * e + 128] = total_q[32 * owner : 32 * owner + 32]
+    to_seq("swq", SWQ, RWQ)
+    grad_a[...] = z_total(of_attn)
+    write(grad_a, grad_a_hbm)
+    share_step(0, 1)
+    first_i(chunk(2))
+    share_step(1, 1)
     again = [
         pltpu.make_async_copy(x_in.at[w], N.at[w, 0:SL], local_sems.at[3 * w + 2]) for w in range(2)
     ]
@@ -1158,15 +1186,16 @@
     tail = TAIL[...]
     for bb in range(8):
         GT[bb % 2, bb // 2] = tail[:, 128 * bb : 128 * bb + 128].astype(BF)
-    start(lambda: link.copy("tx", 0, 1, GT.at[ox], XT, xpart))
-
-    written = []
-
-    def write(src, dst):
-        cp = pltpu.make_async_copy(src, dst, out_sems.at[len(written)])
-        cp.start()
-        written.append(cp)
-        return cp
+    for k in (1, 2, 3):
+        start(lambda k=k: link.copy("tz", k - 1, 3, GT.at[:, (z + k) % 4], ZT.at[k - 1], zdev(k)))
+
+    def tail_x():
+        for k in (1, 2, 3):
+            link.copy("tz", k - 1, 3, ZT.at[k - 1], ZT.at[k - 1], core).wait_recv()
+        add_into(ZT.at[0], GT.at[:, z])
+        add_into(ZT.at[1], ZT.at[2])
+        add_into(ZT.at[0], ZT.at[1])
+        start(lambda: link.copy("tx", 0, 1, ZT.at[0, ox], XT, xpart))
 
     def final_o():
         o_near(z).wait_recv()
@@ -1185,29 +1214,7 @@
             for owner in range(4):
                 SWI[owner, :, 256 * q : 256 * q + 256] = turned[32 * owner : 32 * owner + 32]
 
-    def z_total(name, group, received, landed, at=0, count=1):
-        for k in (1, 2, 3):
-            link.copy(
-                name + "z", 3 * at + k - 1, 3 * count, landed.at[k - 1], landed.at[k - 1], core
-            ).wait_recv()
-        total = group[xx, z].astype(F32) + received[z].astype(F32)
-        for k in range(3):
-            total = total + landed[k].astype(F32)
-        return total
-
-    for e in range(3, 6):
-        z_step(*of_piece(e))
-    z_step("t", GT, XT, ZT)
-    ga_x(0).wait_recv()
-    z_step("a", GA, XA, ZA, waits=lambda: ga_x(1).wait_recv())
-    final_o()
-    write(dqT, grad_o_hbm)
-    final_i()
-    RWI[s] = SWI[s]
-    seq_sends("swi", lambda owner: SWI.at[owner], lambda: RWI.at[s])
-
-
-    def final_rows(w, carry):
+    def final_rows(w):
         again[w].wait()
         v = N[w, 0:SL, :].astype(F32)
         mine = rows(SL * s, SL)
@@ -1231,44 +1238,19 @@
         d = d * PR[0:1, :]
         d = d - jnp.mean(d, axis=-1, keepdims=True) - v * jnp.mean(d * v, axis=-1, keepdims=True)
         grad_in[...] = G[w, mine, :].astype(F32) + scale * d
-        return carry
-
-    final_rows(0, 0)
-    write(A.at[0, own], out_hbm.at[0])
-    first_rows = write(grad_in, grad_in_hbm.at[0])
-
-    for e in range(6):
-        total_q = z_total(*of_piece(e)).T.astype(BF)
-        for owner in range(4):
-            SWQ[owner, :, 128 * e : 128 * e + 128] = total_q[32 * owner : 32 * owner + 32]
-    total_t = z_total("t", GT, XT, ZT)
-    turned_t = jnp.concatenate([total_t, jnp.zeros((112, 128), F32)], axis=0).T.astype(BF)
-    for owner in range(4):
-        SWQ[owner, :, 768:896] = turned_t[32 * owner : 32 * owner + 32]
-    RWQ[s] = SWQ[s]
-    seq_sends("swq", lambda owner: SWQ.at[owner], lambda: RWQ.at[s])
-    grad_a[...] = z_total("a", GA, XA, ZA)
-    write(grad_a, grad_a_hbm)
-
-    def from_seq(name, landed):
-        for i, owner in enumerate((2 * y + oc, 2 * oy + c, 2 * oy + oc)):
-            link.copy(name, i, 3, landed.at[owner], landed.at[owner], core).wait_recv()
-
-    from_seq("swi", RWI)
-    for r in range(4):
-        for blk in range(8):
-            at = 512 * blk + 128 * r
-            oT[32 * (at // 1024) : 32 * (at // 1024) + 32, at % 1024 : at % 1024 + 128] = RWI[
-                r, :, 128 * blk : 128 * blk + 128
-            ].astype(F32)
-
-    for q in range(4):
-        write(oT.at[32 * q : 32 * q + 32], grad_i_hbm.at[:, 1024 * q : 1024 * q + 1024])
-    first_rows.wait()
-    final_rows(1, 0)
-    write(A.at[1, own], out_hbm.at[1])
-    write(grad_in, grad_in_hbm.at[1])
-
+        write(A.at[w, own], out_hbm.at[w])
+        return write(grad_in, grad_in_hbm.at[w])
+
+    first_i(chunk(3))
+    first_o(chunk(0))
+    first_o(chunk(1))
+    second_z(chunk(0))
+    first_rows = final_rows(0)
+    first_o(chunk(2))
+    final_i()
+    to_seq("swi", SWI, RWI)
+    second_z(chunk(1))
+    tail_x()
     from_seq("swq", RWQ)
     got = [RWQ[r].astype(F32) for r in range(4)]
     place_of = {}
@@ -1279,8 +1261,31 @@
     for at in range(24):
         grad_q[:, 128 * at : 128 * at + 128] = halves(place_of[2 * at], place_of[2 * at + 1])
     write(grad_q, grad_q_hbm)
-    summed = got[0][:, 768:896] + got[1][:, 768:896] + got[2][:, 768:896] + got[3][:, 768:896]
-    summed = jnp.where(lane == 2, got[0][:, 768:896], summed)
+    first_rows.wait()
+    final_rows(1)
+    link.copy("tx", 0, 1, XT, XT, core).wait_recv()
+    total_t = ZT[0, xx].astype(F32) + XT[...].astype(F32)
+    turned_t = jnp.concatenate([total_t, jnp.zeros((112, 128), F32)], axis=0).T.astype(BF)
+    for owner in range(4):
+        SWT[owner] = turned_t[32 * owner : 32 * owner + 32]
+    to_seq("swt", SWT, RWT)
+    first_o(chunk(3))
+    final_o()
+    write(dqT, grad_o_hbm)
+    from_seq("swi", RWI)
+    for r in range(4):
+        for blk in range(8):
+            at = 512 * blk + 128 * r
+            oT[32 * (at // 1024) : 32 * (at // 1024) + 32, at % 1024 : at % 1024 + 128] = RWI[
+                r, :, 128 * blk : 128 * blk + 128
+            ].astype(F32)
+    for q in range(4):
+        write(oT.at[32 * q : 32 * q + 32], grad_i_hbm.at[:, 1024 * q : 1024 * q + 1024])
+
+    from_seq("swt", RWT)
+    mine = RWT[0].astype(F32)
+    summed = mine + RWT[1].astype(F32) + RWT[2].astype(F32) + RWT[3].astype(F32)
+    summed = jnp.where(lane == 2, mine, summed)
     summed = jnp.concatenate([summed, jnp.zeros((96, 128), F32)], axis=0).T
     grad_small[...] = jnp.where(lax.broadcasted_iota(jnp.int32, (8, 128), 0) < 3, summed[0:8], total_t[0:8])
     write(grad_small, grad_small_hbm)
@@ -1291,6 +1296,7 @@
     seq_left("wqs", lambda owner: PWQ.at[owner], lambda: wq_block(s))
     seq_left("swi", lambda owner: SWI.at[owner], lambda: RWI.at[s])
     seq_left("swq", lambda owner: SWQ.at[owner], lambda: RWQ.at[s])
+    seq_left("swt", lambda owner: SWT.at[owner], lambda: RWT.at[s])
     for name, (parts, _) in gathers.items():
         for u in range(parts):
             gather_left(name, u)
@@ -1403,13 +1409,15 @@
             pltpu.VMEM((4, 32, 1024), BF),
             pltpu.VMEM((3, 32, 1024), BF),
             pltpu.VMEM((2, 4, 16, 128), BF),
-            pltpu.VMEM((4, 16, 128), BF),
-            pltpu.VMEM((3, 16, 128), BF),
+            pltpu.VMEM((16, 128), BF),
+            pltpu.VMEM((3, 2, 16, 128), BF),
             pltpu.VMEM((2, 2, 256, 1024), BF),
             pltpu.VMEM((4, 32, 1024), BF),
             pltpu.VMEM((4, 32, 1024), BF),
-            pltpu.VMEM((4, 32, 896), BF),
-            pltpu.VMEM((4, 32, 896), BF),
+            pltpu.VMEM((4, 32, 768), BF),
+            pltpu.VMEM((4, 32, 768), BF),
+            pltpu.VMEM((4, 32, 128), BF),
+            pltpu.VMEM((4, 32, 128), BF),
             pltpu.VMEM((16, 1024), F32),
             pltpu.VMEM((2, 1024, 128), BF),
             pltpu.VMEM((128, 1024), BF),
@@ -1423,10 +1431,10 @@
             pltpu.VMEM((32, 3072), F32),
             pltpu.VMEM((32, 1024), F32),
             pltpu.VMEM((8, 128), F32),
-            pltpu.SemaphoreType.DMA((210,)),
-            pltpu.SemaphoreType.DMA((210,)),
+            pltpu.SemaphoreType.DMA((200,)),
+            pltpu.SemaphoreType.DMA((200,)),
             pltpu.SemaphoreType.DMA((6,)),
-            pltpu.SemaphoreType.DMA((12,)),
+            pltpu.SemaphoreType.DMA((14,)),
         ],
         compiler_params=pltpu.CompilerParams(
             collective_id=0, has_side_effects=True, vmem_limit_bytes=65400 * 2**10

time: 180 us -> 169 us (0.939)
  Pallas kernels: 177 us -> 165 us
    pallas_call x1, Pallas kernels: 172 us -> 160 us  [fused_shards(): pl.pallas_call(fused_layer, out_shape=shapes + (jax.ShapeDtypeStruct((8,...]
where the time goes in v3:
time: 169 us
  Pallas kernels  165 us (98%)
    pallas_call x1, Pallas kernels, fused_shards(): pl.pallas_call(fused_layer, out_shape=shapes + (jax.ShapeDtypeStruct((8,...  160 us
    pallas_call x1, Pallas kernels, fused_shards(): pl.pallas_call(publish, out_shape=shapes + (row, row, row, jax.ShapeDtype...  5.06 us

profile of v3, /device:TPU:0, one launch (start us, length us, event | category | flops | bytes accessed | tf_op | source)
XLA Modules:
  0.0 168.8 jit_solution(8298616995745071420)
XLA Ops:
  0.6 0.7 pad_bitcast_fusion.2
  1.3 0.7 pad_bitcast_fusion
  2.0 1.3 fusion.6.prm
  3.2 160.3 %shard_map.195 = (bf16[2,256,1024]{2,1,0:T(8,128)(2,1)}, f32[2,256,1024]{2,1,0:T(8,128)}, f32[32,3072]{1,0:T(8,128)}, f32[32,1024]{1,0:T(8,128)}, f32[32,4096]{1...) custom-call(s32[2]{0:T(128)} %ends.1, bf16[16,128]{1,0:T(8,128)(2,1)} %fusion.6.prm, bf16[32,3072]{1,0:T(8,128)(2,1)} %wq.1, ...), custom_call_target="tpu_custom_call" | custom-call | flops 46000001024 | bytes 10000000 | tf_op jit(solution)/shard_map/pallas_call | solution.py:1374
  163.6 5.1 %shard_map.196 = (bf16[2,256,1024]{2,1,0:T(8,128)(2,1)}, f32[2,256,1024]{2,1,0:T(8,128)}, f32[32,3072]{1,0:T(8,128)}, f32[32,1024]{1,0:T(8,128)}, f32[32,4096]{1...) custom-call(bf16[2,256,1024]{2,1,0:T(8,128)(2,1)} %get-tuple-element, ...), custom_call_target="tpu_custom_call" | custom-call | tf_op jit(solution)/shard_map/pallas_call | solution.py:1445

commit v4 on v3

--- a/solution.py
+++ b/solution.py
@@ -375,10 +375,10 @@
 
 
 def fused_layer(
-    ends, prm, wq, wa, wi, wo, turns, x_in, g_in,
+    ends, gain, bias, bias_out, bias_in, wq, wa, wi, wo, turns, x_in, g_in,
     out_hbm, grad_in_hbm, grad_q_hbm, grad_a_hbm, grad_i_hbm, grad_o_hbm, grad_small_hbm,
     X, N, G, A, H, Wi, Wo, Wq, WaAll, Wa, PWI, PWQ, PRS, PRM, PR, QKV, att, dO,
-    GO, XO, ZO, CO, GI, XI, ZI, GQ, XQ, ZQ, GA, XA, ZA, GT, XT, ZT,
+    GO, XO, ZO, CO, GI, XI, ZN, ZF, ZD, CI, GQ, XQ, ZQ, CQ, GA, XA, ZA, CA, GT, XT, ZT,
     YR, SWI, RWI, SWQ, RWQ, SWT, RWT, TAIL,
     khat, ktT, vtT, doT, oT, dqT, dkA, dvA,
     grad_in, grad_q, grad_a, grad_small,
@@ -427,7 +427,10 @@
     for r in range(SB):
         for blk in range(8):
             PWI[r, :, 128 * blk : 128 * blk + 128] = wi[:, 512 * blk + 128 * r : 512 * blk + 128 * r + 128]
-    tile = prm[...].astype(F32)
+    TAIL[...] = jnp.zeros_like(TAIL)
+    for i, values in enumerate((gain, bias, bias_out, bias_in)):
+        TAIL[i : i + 1, 0 : values.shape[1]] = values[...].astype(F32)
+    tile = TAIL[:, 0:128]
     row = lax.broadcasted_iota(jnp.int32, (16, 128), 0)
     tile = jnp.where(row < 3, pltpu.roll(tile, 32 * s, 1), tile)
     PRS[s] = tile.astype(BF)
@@ -484,6 +487,8 @@
         held = gathers[name][1](2 * zz + side, u)
         return link.copy(name + way, count * u + at, count * gathers[name][0], held, held, device)
 
+    by_line = ("wi", "wo")
+
     def up_copy(name, zz, u):
         return gather_copy(name, "l", zz, 5, zz, xx, u, (2 * (z + 1) + xx, s))
 
@@ -497,7 +502,7 @@
         return gather_copy(name, "x", zz, 4, zz, side, u, xpart)
 
     def gather_z(name, u):
-        if name == "wi":
+        if name in by_line:
 
             @pl.when(z < 3)
             def _():
@@ -524,7 +529,7 @@
     def gather_pass(name, far, u):
         @pl.when(z >= far)
         def _():
-            if name == "wi":
+            if name in by_line:
                 up_copy(name, z - far, u).wait_recv()
 
                 @pl.when(z < 3)
@@ -537,7 +542,7 @@
 
         @pl.when(z + far <= 3)
         def _():
-            if name == "wi":
+            if name in by_line:
                 down_copy(name, z + far, u).wait_recv()
 
                 @pl.when(z > 0)
@@ -556,11 +561,11 @@
             gather_block(name, zz, u)
 
     def gather_left(name, u):
-        if name != "wi":
+        if name not in by_line:
             for k in (1, 2, 3):
                 z_copy(name, z, k, u).wait_send()
         for zz in range(4):
-            if name == "wi":
+            if name in by_line:
 
                 @pl.when((zz <= z) & (z < 3))
                 def _():
@@ -732,6 +737,8 @@
     Wa[:, c] = WaAll[:, c]
     for far in (2, 3):
         gather_pass("wq", far, 1)
+    for u in range(2):
+        gather_pass("wo", 1, u)
 
     def add_into(dst, other):
         dst[...] = (dst[...].astype(F32) + other[...].astype(F32)).astype(BF)
@@ -753,8 +760,66 @@
     def o_far(q):
         return link.copy("of", q % 2, 2, GO.at[q, xx], ZO.at[1], zchip(q))
 
-    def i_z(q, k):
-        return link.copy("iz", 3 * q + k - 1, 12, GI.at[q, xx, (z + k) % 4], ZI.at[k - 1, q], zdev(k))
+    def of_pair(p):
+        return lambda: ("q", GQ.at[p], XQ.at[p], ZQ.at[p], CQ.at[p], p, 2)
+
+    def of_attn():
+        return "a", GA, XA, ZA, CA, 0, 1
+
+    def z_near(get):
+        name, group, _, landed, _, at, count = get()
+        return link.copy(name + "p", at, count, group.at[xx, pair], landed.at[0], zchip(pair))
+
+    def z_comb(get, tt):
+        name, group, _, _, comb, at, count = get()
+        block = group.at[xx, far_chip(tt)]
+        return link.copy(name + "c", 2 * at + tt, 2 * count, block, comb.at[tt], zchip(pair))
+
+    def z_far(get, tt, side):
+        name, group, _, landed, _, at, count = get()
+        block = group.at[xx, far_chip(tt)]
+        return link.copy(
+            name + "f", 2 * at + side, 2 * count, block, landed.at[1], zchip(far_chip(tt))
+        )
+
+    def z_first(get):
+        _, group, received, _, _, _, _ = get()
+        add_into(group.at[xx, pair], received.at[pair])
+        z_near(get).start()
+        for tt in range(2):
+            add_into(group.at[xx, far_chip(tt)], received.at[far_chip(tt)])
+
+            @pl.when(~inner)
+            def _():
+                z_comb(get, tt).start()
+
+    def z_second(get):
+        @pl.when(inner)
+        def _():
+            _, group, _, _, comb, _, _ = get()
+            for tt in range(2):
+                z_comb(get, tt).wait_recv()
+                add_into(group.at[xx, far_chip(tt)], comb.at[tt])
+                z_far(get, tt, tt).start()
+
+    def z_total(get):
+        _, group, received, landed, _, _, _ = get()
+        z_near(get).wait_recv()
+        z_far(get, 0, z % 2).wait_recv()
+        total = group[xx, z].astype(F32) + received[z].astype(F32)
+        return total + landed[0].astype(F32) + landed[1].astype(F32)
+
+    def z_gone(get):
+        z_near(get).wait_send()
+        for tt in range(2):
+
+            @pl.when(inner)
+            def _():
+                z_far(get, tt, tt).wait_send()
+
+            @pl.when(~inner)
+            def _():
+                z_comb(get, tt).wait_send()
 
     def first_o(q):
         o_x(q).wait_recv()
@@ -771,12 +836,59 @@
             def _():
                 o_comb(q).start()
 
-    def first_i(q):
+    def half_chip(tt):
+        return 2 * (z // 2) + tt
+
+    def i_near(q):
+        return link.copy("ip", q, 4, GI.at[q, xx, pair], ZN.at[q], zchip(pair))
+
+    def i_comb(q, tt):
+        block = GI.at[q, xx, far_chip(tt)]
+        return link.copy("ic", 2 * (q % 2) + tt, 4, block, CI.at[q % 2, tt], zchip(pair))
+
+    def i_far(q, tt, side):
+        block = GI.at[q, xx, far_chip(tt)]
+        return link.copy("if", 2 * (q % 2) + side, 4, block, ZF.at[q % 2], zchip(far_chip(tt)))
+
+    def i_straight(q, tt, sender, side):
+        block = GI.at[q, xx, far_chip(tt)]
+        return link.copy(
+            "id", 4 * (q % 2) + 2 * sender + side, 8, block, ZD.at[q % 2, sender], zchip(far_chip(tt))
+        )
+
+    def first_i(q, far):
         i_x(q).wait_recv()
-        for k in (1, 2, 3):
-            zz = (z + k) % 4
-            add_into(GI.at[q, xx, zz], XI.at[q, zz])
-            i_z(q, k).start()
+        add_into(GI.at[q, xx, pair], XI.at[q, pair])
+        i_near(q).start()
+        for tt in range(2):
+            add_into(GI.at[q, xx, far_chip(tt)], XI.at[q, far_chip(tt)])
+            if far:
+
+                @pl.when(~inner)
+                def _():
+                    i_comb(q, tt).start()
+
+            else:
+                i_straight(q, tt, z % 2, tt).start()
+
+    def second_i(q):
+        @pl.when(inner)
+        def _():
+            for tt in range(2):
+                i_comb(q, tt).wait_recv()
+                add_into(GI.at[q, xx, far_chip(tt)], CI.at[q % 2, tt])
+                i_far(q, tt, tt).start()
+
+    def total_i(q, far):
+        i_near(q).wait_recv()
+        total = GI[q, xx, z].astype(F32) + XI[q, z].astype(F32) + ZN[q].astype(F32)
+        if far:
+            for sender in range(2):
+                i_straight(q, 0, sender, z % 2).wait_recv()
+                total = total + ZD[q % 2, sender].astype(F32)
+            return total
+        i_far(q, 0, z % 2).wait_recv()
+        return total + ZF[q % 2].astype(F32)
 
     def second_z(q):
         @pl.when(inner)
@@ -798,8 +910,22 @@
                 o_comb(far_chip(tt)).wait_send()
 
         for q in range(4):
-            for k in (1, 2, 3):
-                i_z(q, k).wait_send()
+            i_near(q).wait_send()
+        for a in range(2):
+            for tt in range(2):
+                i_straight(half_chip(a), tt, z % 2, tt).wait_send()
+
+                @pl.when(inner)
+                def _():
+                    i_far(far_chip(a), tt, tt).wait_send()
+
+                @pl.when(~inner)
+                def _():
+                    i_comb(far_chip(a), tt).wait_send()
+
+        for p in range(2):
+            z_gone(of_pair(p))
+        z_gone(of_attn)
 
     def chunk(j):
         return jnp.where(j == 3, z, jnp.where(j == 2, pair, far_chip(0) + j))
@@ -863,6 +989,7 @@
 
     rows_end_far("g", G, 0)
     do_step(0)
+    gather_pass("wo", 2, 0)
 
     def units_back(j):
         q = chunk(j)
@@ -1007,21 +1134,19 @@
         lax.fori_loop(0, 4, step, 0)
 
     def gq_step(p):
-        for kind in range(3):
-            e = 3 * p + kind
-            l = slice(128 * e, 128 * e + 128)
-            gq = dot(QKV[0, :, l], N[0], 0, 0) + dot(QKV[1, :, l], N[1], 0, 0)
-            for bb in range(8):
-                GQ[e, bb % 2, bb // 2] = gq[:, 128 * bb : 128 * bb + 128].astype(BF)
-            link.copy("qx", e, 6, GQ.at[e, ox], XQ.at[e], xpart).start()
+        l = slice(384 * p, 384 * p + 384)
+        gq = dot(QKV[0, :, l], N[0], 0, 0) + dot(QKV[1, :, l], N[1], 0, 0)
+        for bb in range(8):
+            GQ[p, bb % 2, bb // 2] = gq[:, 128 * bb : 128 * bb + 128].astype(BF)
+        link.copy("qx", p, 2, GQ.at[p, ox], XQ.at[p], xpart).start()
 
     def ga_c(p):
         two = slice(2 * p, 2 * p + 2)
-        return link.copy("ac", p, 2, PWI.at[two], GA.at[c, two], core)
+        return link.copy("core_a", p, 2, PWI.at[two], GA.at[c, two], core)
 
     def ga_x(p):
         two = slice(2 * p, 2 * p + 2)
-        return link.copy("ax", p, 2, GA.at[ox, two], XA.at[two], xpart)
+        return link.copy("x_a", p, 2, GA.at[ox, two], XA.at[two], xpart)
 
     def ga_step(p):
         l = slice(128 * p, 128 * p + 128)
@@ -1044,27 +1169,14 @@
         ga_c(p).wait_recv()
         ga_x(p).start()
 
-    def z_send(get, k):
-        name, group, _, landed, at, count = get()
-        src = group.at[xx, (z + k) % 4]
-        return link.copy(name + "z", 3 * at + k - 1, 3 * count, src, landed.at[k - 1], zdev(k))
-
-    def z_step(get, waits=None):
-        name, group, received, _, at, count = get()
-        if waits is None:
-            link.copy(name + "x", at, count, received, received, core).wait_recv()
-        else:
-            waits()
-        for k in (1, 2, 3):
-            zz = (z + k) % 4
-            add_into(group.at[xx, zz], received.at[zz])
-            start(lambda k=k: z_send(get, k))
-
-    def of_piece(e):
-        return lambda: ("q", GQ.at[e], XQ.at[e], ZQ.at[e], e, 6)
-
-    def of_attn():
-        return "a", GA, XA, ZA, 0, 1
+    def first_q(p):
+        link.copy("qx", p, 2, GQ.at[p, ox], XQ.at[p], xpart).wait_recv()
+        z_first(of_pair(p))
+
+    def first_a():
+        for p in range(2):
+            ga_x(p).wait_recv()
+        z_first(of_attn)
 
     def attend_step(i, carry):
         w, p = i // 2, i % 2
@@ -1072,44 +1184,39 @@
 
         @pl.when(i == 0)
         def _():
-            for u in range(2):
-                gather_pass("wo", 1, u)
+            gather_pass("wo", 2, 1)
+            gather_pass("wo", 3, 0)
             rows_pass("g", G, 1)
             qkv_step(1)
-            for far in (2, 3):
-                for u in range(2):
-                    gather_pass("wo", far, u)
+            gather_pass("wo", 3, 1)
+            rows_end_far("g", G, 1)
+            for j in range(2):
+                units_out(j)
+                o_x(chunk(j)).start()
 
         @pl.when(i == 1)
         def _():
-            rows_end_far("g", G, 1)
             do_step(1)
 
         @pl.when(i == 2)
         def _():
             gq_step(0)
             ga_step(0)
+            for j in range(2, 4):
+                units_out(j)
+            for u in range(2):
+                for zz in range(4):
+                    gather_block("wo", zz, u)
+            share_step(0, 0)
+            first_o(chunk(0))
+            first_o(chunk(1))
+            ga_send(0)
 
         return carry
 
     lax.fori_loop(0, 4, attend_step, 0)
-    ga_send(0)
     gq_step(1)
     ga_step(1)
-    def out_step(j, carry):
-        units_out(j)
-
-        @pl.when(j == 0)
-        def _():
-            z_step(of_piece(0))
-            z_step(of_piece(1))
-            ga_send(1)
-
-        @pl.when(j == 2)
-        def _():
-            z_step(of_piece(2))
-
-        return carry
 
     def in_step(j, carry):
         units_back(j)
@@ -1118,13 +1225,15 @@
 
         @pl.when(j == 0)
         def _():
-            z_step(of_piece(4))
-            z_step(of_piece(5))
+            z_second(of_pair(0))
 
         @pl.when(j == 1)
         def _():
-            ga_x(0).wait_recv()
-            z_step(of_attn, waits=lambda: ga_x(1).wait_recv())
+            first_q(1)
+
+        @pl.when(j == 2)
+        def _():
+            first_a()
 
         return carry
 
@@ -1136,17 +1245,6 @@
         written.append(cp)
         return cp
 
-    def z_total(get):
-        name, group, received, landed, at, count = get()
-        for k in (1, 2, 3):
-            link.copy(
-                name + "z", 3 * at + k - 1, 3 * count, landed.at[k - 1], landed.at[k - 1], core
-            ).wait_recv()
-        total = group[xx, z].astype(F32) + received[z].astype(F32)
-        for k in range(3):
-            total = total + landed[k].astype(F32)
-        return total
-
     def to_seq(name, held, landed):
         landed[s] = held[s]
         seq_sends(name, lambda owner: held.at[owner], lambda: landed.at[s])
@@ -1155,29 +1253,26 @@
         for i, owner in enumerate((2 * y + oc, 2 * oy + c, 2 * oy + oc)):
             link.copy(name, i, 3, landed.at[owner], landed.at[owner], core).wait_recv()
 
-    lax.fori_loop(0, 4, out_step, 0)
-    for u in range(2):
-        for zz in range(4):
-            gather_block("wo", zz, u)
-    share_step(0, 0)
-    z_step(of_piece(3))
-    lax.fori_loop(0, 2, in_step, 0)
+    second_z(chunk(0))
+    first_q(0)
+    ga_send(1)
+    second_z(chunk(1))
     share_step(1, 0)
-    first_i(chunk(0))
-    lax.fori_loop(2, 4, in_step, 0)
-    for j in range(4):
+    lax.fori_loop(0, 4, in_step, 0)
+    for j in range(2, 4):
         o_x(chunk(j)).start()
-    first_i(chunk(1))
-    for e in range(6):
-        total_q = z_total(of_piece(e)).T.astype(BF)
+    z_second(of_pair(1))
+    z_second(of_attn)
+    first_i(chunk(0), True)
+    share_step(0, 1)
+    first_i(chunk(1), True)
+    second_i(chunk(0))
+    share_step(1, 1)
+    for p in range(2):
+        total_q = z_total(of_pair(p)).T.astype(BF)
         for owner in range(4):
-            SWQ[owner, :, 128 * e : 128 * e + 128] = total_q[32 * owner : 32 * owner + 32]
+            SWQ[owner, :, 384 * p : 384 * p + 384] = total_q[32 * owner : 32 * owner + 32]
     to_seq("swq", SWQ, RWQ)
-    grad_a[...] = z_total(of_attn)
-    write(grad_a, grad_a_hbm)
-    share_step(0, 1)
-    first_i(chunk(2))
-    share_step(1, 1)
     again = [
         pltpu.make_async_copy(x_in.at[w], N.at[w, 0:SL], local_sems.at[3 * w + 2]) for w in range(2)
     ]
@@ -1205,14 +1300,11 @@
         )
 
     def final_i():
-        for q in range(4):
-            total = GI[q, xx, z].astype(F32) + XI[q, z].astype(F32)
-            for k in (1, 2, 3):
-                i_z(q, k).wait_recv()
-                total = total + ZI[k - 1, q].astype(F32)
-            turned = total.T.astype(BF)
-            for owner in range(4):
-                SWI[owner, :, 256 * q : 256 * q + 256] = turned[32 * owner : 32 * owner + 32]
+        for tt in range(2):
+            for q, far in ((half_chip(tt), False), (far_chip(tt), True)):
+                turned = total_i(q, far).T.astype(BF)
+                for owner in range(4):
+                    SWI[owner, :, lanes(256 * q, 256)] = turned[32 * owner : 32 * owner + 32]
 
     def final_rows(w):
         again[w].wait()
@@ -1241,16 +1333,18 @@
         write(A.at[w, own], out_hbm.at[w])
         return write(grad_in, grad_in_hbm.at[w])
 
-    first_i(chunk(3))
-    first_o(chunk(0))
-    first_o(chunk(1))
-    second_z(chunk(0))
+    first_i(chunk(2), False)
+    second_i(chunk(1))
+    grad_a[...] = z_total(of_attn)
+    write(grad_a, grad_a_hbm)
+    first_i(chunk(3), False)
+    first_o(chunk(2))
     first_rows = final_rows(0)
-    first_o(chunk(2))
+    tail_x()
     final_i()
     to_seq("swi", SWI, RWI)
-    second_z(chunk(1))
-    tail_x()
+    first_rows.wait()
+    final_rows(1)
     from_seq("swq", RWQ)
     got = [RWQ[r].astype(F32) for r in range(4)]
     place_of = {}
@@ -1261,8 +1355,6 @@
     for at in range(24):
         grad_q[:, 128 * at : 128 * at + 128] = halves(place_of[2 * at], place_of[2 * at + 1])
     write(grad_q, grad_q_hbm)
-    first_rows.wait()
-    final_rows(1)
     link.copy("tx", 0, 1, XT, XT, core).wait_recv()
     total_t = ZT[0, xx].astype(F32) + XT[...].astype(F32)
     turned_t = jnp.concatenate([total_t, jnp.zeros((112, 128), F32)], axis=0).T.astype(BF)
@@ -1314,9 +1406,8 @@
                 link.copy("sc", 4 * w + 2 * t + yy, 8, src, dst, core).wait_send()
             src = shares[t].at[w, rows(SL * (2 * oy + c), SL)]
             link.copy("sy", 2 * w + t, 4, src, YR.at[w, t], ypart).wait_send()
-    for e in range(6):
-        link.copy("qx", e, 6, GQ.at[e, ox], XQ.at[e], xpart).wait_send()
     for p in range(2):
+        link.copy("qx", p, 2, GQ.at[p, ox], XQ.at[p], xpart).wait_send()
         ga_c(p).wait_send()
         ga_x(p).wait_send()
     for cp in written:
@@ -1333,11 +1424,12 @@
     leave = [
         pltpu.make_async_copy(held[i], targets[i], out_sems.at[i]) for i in range(6)
     ]
-    for cp in arrive:
-        cp.start()
+    largest_first = (1, 0, 4, 5, 2, 3)
+    for i in largest_first:
+        arrive[i].start()
     for i, target in enumerate(row_targets):
         target[...] = small[i : i + 1, 0 : target.shape[1]]
-    for i in range(6):
+    for i in largest_first:
         arrive[i].wait()
         leave[i].start()
     for cp in leave:
@@ -1356,10 +1448,6 @@
 
 
 def fused_shards(inputs, ends, ln_gain, ln_bias, w_qkv, w_attn, w_in, b_in, w_out, b_out, cotangent):
-    def widen(v):
-        return jnp.pad(v, (0, 128 - v.shape[0]))
-
-    prm = jnp.pad(jnp.stack([widen(ln_gain), widen(ln_bias), widen(b_out), b_in]), ((0, 12), (0, 0)))
     in_vmem = pl.BlockSpec(memory_space=pltpu.VMEM)
     in_any = pl.BlockSpec(memory_space=pl.ANY)
     rows_type = (2, 1024, 1024)
@@ -1374,7 +1462,7 @@
     results = pl.pallas_call(
         fused_layer,
         out_shape=shapes + (jax.ShapeDtypeStruct((8, 128), F32),),
-        in_specs=[pl.BlockSpec(memory_space=pltpu.SMEM)] + [in_vmem] * 6 + [in_any] * 2,
+        in_specs=[pl.BlockSpec(memory_space=pltpu.SMEM)] + [in_vmem] * 9 + [in_any] * 2,
         out_specs=(in_any,) * 7,
         scratch_shapes=[
             pltpu.VMEM(rows_type, BF),
@@ -1401,13 +1489,18 @@
             pltpu.VMEM((2, 128, 1024), BF),
             pltpu.VMEM((4, 2, 4, 256, 128), BF),
             pltpu.VMEM((4, 4, 256, 128), BF),
-            pltpu.VMEM((3, 4, 256, 128), BF),
-            pltpu.VMEM((6, 2, 4, 128, 128), BF),
-            pltpu.VMEM((6, 4, 128, 128), BF),
-            pltpu.VMEM((6, 3, 128, 128), BF),
+            pltpu.VMEM((4, 256, 128), BF),
+            pltpu.VMEM((2, 256, 128), BF),
+            pltpu.VMEM((2, 2, 256, 128), BF),
+            pltpu.VMEM((2, 2, 256, 128), BF),
+            pltpu.VMEM((2, 2, 4, 384, 128), BF),
+            pltpu.VMEM((2, 4, 384, 128), BF),
+            pltpu.VMEM((2, 2, 384, 128), BF),
+            pltpu.VMEM((2, 2, 384, 128), BF),
             pltpu.VMEM((2, 4, 32, 1024), BF),
             pltpu.VMEM((4, 32, 1024), BF),
-            pltpu.VMEM((3, 32, 1024), BF),
+            pltpu.VMEM((2, 32, 1024), BF),
+            pltpu.VMEM((2, 32, 1024), BF),
             pltpu.VMEM((2, 4, 16, 128), BF),
             pltpu.VMEM((16, 128), BF),
             pltpu.VMEM((3, 2, 16, 128), BF),
@@ -1431,8 +1524,8 @@
             pltpu.VMEM((32, 3072), F32),
             pltpu.VMEM((32, 1024), F32),
             pltpu.VMEM((8, 128), F32),
-            pltpu.SemaphoreType.DMA((200,)),
-            pltpu.SemaphoreType.DMA((200,)),
+            pltpu.SemaphoreType.DMA((192,)),
+            pltpu.SemaphoreType.DMA((192,)),
             pltpu.SemaphoreType.DMA((6,)),
             pltpu.SemaphoreType.DMA((14,)),
         ],
@@ -1440,7 +1533,13 @@
             collective_id=0, has_side_effects=True, vmem_limit_bytes=65400 * 2**10
         ),
         cost_estimate=pl.CostEstimate(flops=46 * 10**9, bytes_accessed=10**7, transcendentals=10**7),
-    )(ends, prm, w_qkv, w_attn, w_in, w_out, turn_tables(1024), inputs, cotangent)
+    )(
+        ends,
+        ln_gain.reshape(1, 32),
+        ln_bias.reshape(1, 32),
+        b_out.reshape(1, 32),
+        b_in.reshape(1, 128),
+        w_qkv, w_attn, w_in, w_out, turn_tables(1024), inputs, cotangent)
     row = jax.ShapeDtypeStruct((1, 32), F32)
     final = pl.pallas_call(
         publish,

time: 169 us -> 166 us (0.982)
  no operation moved by 1% of the time
where the time goes in v4:
time: 166 us; the launch traced here: 165 us
  Pallas kernels  164 us (99%)
    pallas_call x1, Pallas kernels, fused_shards(): pl.pallas_call(fused_layer, out_shape=shapes + (jax.ShapeDtypeStruct((8,...  159 us
    pallas_call x1, Pallas kernels, fused_shards(): pl.pallas_call(publish, out_shape=shapes + (row, row, row, jax.ShapeDtype...  5.05 us

profile of v4, /device:TPU:0, one launch (start us, length us, event | category | flops | bytes accessed | tf_op | source)
XLA Modules:
  0.0 165.1 jit_solution(7891350932876511008)
XLA Ops:
  0.6 159.2 %shard_map.195 = (bf16[2,256,1024]{2,1,0:T(8,128)(2,1)}, f32[2,256,1024]{2,1,0:T(8,128)}, f32[32,3072]{1,0:T(8,128)}, f32[32,1024]{1,0:T(8,128)}, f32[32,4096]{1...) custom-call(s32[2]{0:T(128)} %ends.1, bf16[1,32]{1,0:T(2,128)(2,1)} %bitcast.8, bf16[1,32]{1,0:T(2,128)(2,1)} %bitcast.9, ...), custom_call_target="tpu_custom_call" | custom-call | flops 46000001024 | bytes 10000000 | tf_op jit(solution)/shard_map/pallas_call | solution.py:1462
  159.9 5.1 %shard_map.196 = (bf16[2,256,1024]{2,1,0:T(8,128)(2,1)}, f32[2,256,1024]{2,1,0:T(8,128)}, f32[32,3072]{1,0:T(8,128)}, f32[32,1024]{1,0:T(8,128)}, f32[32,4096]{1...) custom-call(bf16[2,256,1024]{2,1,0:T(8,128)(2,1)} %get-tuple-element, ...), custom_call_target="tpu_custom_call" | custom-call | tf_op jit(solution)/shard_map/pallas_call | solution.py:1544

commit v5 on v4

--- a/solution.py
+++ b/solution.py
@@ -995,14 +995,13 @@
         q = chunk(j)
         l = lanes(256 * q, 256)
 
-        def step(i, total):
-            w, r = i // 2, rows(512 * (i % 2), 512)
-            d = dot(G[w, r, :], Wo[rows(256 * q, 256), :], 1, 1) * H[w, r, l].astype(F32)
+        def step(w, total):
+            d = dot(G[w], Wo[rows(256 * q, 256), :], 1, 1) * H[w, :, l].astype(F32)
             d = d.astype(BF)
-            H[w, r, l] = d
+            H[w, :, l] = d
             return total + jnp.sum(d.astype(F32), axis=0, keepdims=True)
 
-        TAIL[3:4, l] = lax.fori_loop(0, 4, step, jnp.zeros((1, 256), F32))
+        TAIL[3:4, l] = lax.fori_loop(0, 2, step, jnp.zeros((1, 256), F32))
 
     def units_out(j):
         q = chunk(j)
@@ -1114,7 +1113,7 @@
         TAIL[0:1, :] += jnp.sum(d, axis=0, keepdims=True)
         TAIL[1:2, :] += jnp.sum(d * n, axis=0, keepdims=True)
 
-    def share_step(w, t):
+    def share_step(w, t, between=None):
         def step(i, carry):
             yy = jnp.where(i < 2, oy, y)
             cc = jnp.where(i % 2 == 0, oc, c)
@@ -1123,6 +1122,9 @@
             @pl.when(i == 0)
             def _():
                 share_c(w, t, oy)
+
+            if between is not None:
+                pl.when(i == 1)(between)
 
             @pl.when(i == 2)
             def _():
@@ -1261,13 +1263,18 @@
     lax.fori_loop(0, 4, in_step, 0)
     for j in range(2, 4):
         o_x(chunk(j)).start()
-    z_second(of_pair(1))
-    z_second(of_attn)
-    first_i(chunk(0), True)
-    share_step(0, 1)
-    first_i(chunk(1), True)
-    second_i(chunk(0))
-    share_step(1, 1)
+
+    def between_first():
+        first_i(chunk(0), True)
+        z_second(of_pair(1))
+        z_second(of_attn)
+
+    def between_second():
+        first_i(chunk(1), True)
+        second_i(chunk(0))
+
+    share_step(0, 1, between_first)
+    share_step(1, 1, between_second)
     for p in range(2):
         total_q = z_total(of_pair(p)).T.astype(BF)
         for owner in range(4):
@@ -1416,19 +1423,20 @@
 
 
 def publish(*refs):
-    sources, small, targets, row_targets = refs[:6], refs[6], refs[7:13], refs[13:17]
-    held, (in_sems, out_sems) = refs[17:23], refs[23:]
-    arrive = [
-        pltpu.make_async_copy(sources[i], held[i], in_sems.at[i]) for i in range(6)
-    ]
-    leave = [
-        pltpu.make_async_copy(held[i], targets[i], out_sems.at[i]) for i in range(6)
+    sources, targets, (in_sems, out_sems) = refs[:7], refs[7:17], refs[28:]
+    held, row_held = refs[17:24], refs[24:28]
+    arrive = [pltpu.make_async_copy(sources[i], held[i], in_sems.at[i]) for i in range(7)]
+    leave = [pltpu.make_async_copy(held[i], targets[i], out_sems.at[i]) for i in range(6)]
+    leave += [
+        pltpu.make_async_copy(row_held[i], targets[6 + i], out_sems.at[6 + i]) for i in range(4)
     ]
     largest_first = (1, 0, 4, 5, 2, 3)
-    for i in largest_first:
+    for i in (6,) + largest_first:
         arrive[i].start()
-    for i, target in enumerate(row_targets):
-        target[...] = small[i : i + 1, 0 : target.shape[1]]
+    arrive[6].wait()
+    for i in range(4):
+        row_held[i][...] = held[6][i : i + 1, 0 : row_held[i].shape[1]]
+        leave[6 + i].start()
     for i in largest_first:
         arrive[i].wait()
         leave[i].start()
@@ -1541,13 +1549,15 @@
         b_in.reshape(1, 128),
         w_qkv, w_attn, w_in, w_out, turn_tables(1024), inputs, cotangent)
     row = jax.ShapeDtypeStruct((1, 32), F32)
+    rows_out = (row, row, row, jax.ShapeDtypeStruct((1, 128), F32))
+    held = shapes + (jax.ShapeDtypeStruct((8, 128), F32),) + rows_out
     final = pl.pallas_call(
         publish,
-        out_shape=shapes + (row, row, row, jax.ShapeDtypeStruct((1, 128), F32)),
-        in_specs=[in_any] * 6 + [in_vmem],
-        out_specs=(in_any,) * 6 + (in_vmem,) * 4,
-        scratch_shapes=[pltpu.VMEM(v.shape, v.dtype) for v in shapes]
-        + [pltpu.SemaphoreType.DMA((6,)), pltpu.SemaphoreType.DMA((6,))],
+        out_shape=shapes + rows_out,
+        in_specs=[in_any] * 7,
+        out_specs=(in_any,) * 10,
+        scratch_shapes=[pltpu.VMEM(v.shape, v.dtype) for v in held]
+        + [pltpu.SemaphoreType.DMA((7,)), pltpu.SemaphoreType.DMA((10,))],
         compiler_params=pltpu.CompilerParams(vmem_limit_bytes=60 * 2**20),
     )(*results)
     out, grad_in, grad_q, grad_a, grad_i, grad_o, bias, gain, bias_out, bias_in = final

time: 166 us -> 165 us (level)
  no operation moved by 1% of the time
where the time goes in v5:
time: 165 us; the launch traced here: 164 us
  Pallas kernels  163 us (99%)
    pallas_call x1, Pallas kernels, fused_shards(): pl.pallas_call(fused_layer, out_shape=shapes + (jax.ShapeDtypeStruct((8,...  160 us
    pallas_call x1, Pallas kernels, fused_shards(): pl.pallas_call(publish, out_shape=shapes + rows_out, in_specs=[in_any] *...  3.91 us

profile of v5, /device:TPU:0, one launch (start us, length us, event | category | flops | bytes accessed | tf_op | source)
XLA Modules:
  0.0 164.3 jit_solution(9050010012724599999)
XLA Ops:
  0.6 159.5 %shard_map.195 = (bf16[2,256,1024]{2,1,0:T(8,128)(2,1)}, f32[2,256,1024]{2,1,0:T(8,128)}, f32[32,3072]{1,0:T(8,128)}, f32[32,1024]{1,0:T(8,128)}, f32[32,4096]{1...) custom-call(s32[2]{0:T(128)} %ends.1, bf16[1,32]{1,0:T(2,128)(2,1)} %bitcast.8, bf16[1,32]{1,0:T(2,128)(2,1)} %bitcast.9, ...), custom_call_target="tpu_custom_call" | custom-call | flops 46000001024 | bytes 10000000 | tf_op jit(solution)/shard_map/pallas_call | solution.py:1470
  160.2 3.9 %shard_map.196 = (bf16[2,256,1024]{2,1,0:T(8,128)(2,1)}, f32[2,256,1024]{2,1,0:T(8,128)}, f32[32,3072]{1,0:T(8,128)}, f32[32,1024]{1,0:T(8,128)}, f32[32,4096]{1...) custom-call(bf16[2,256,1024]{2,1,0:T(8,128)(2,1)} %get-tuple-element, ...), custom_call_target="tpu_custom_call" | custom-call | tf_op jit(solution)/shard_map/pallas_call | solution.py:1554

commit v6 on v5

--- a/solution.py
+++ b/solution.py
@@ -309,7 +309,8 @@
     )
 
 
-HB, SB = 4, 4
+SB = 4
+SEND_SEMS = 93
 NEG = -1e30
 BF, F32 = jnp.bfloat16, jnp.float32
 MESH = pl.DeviceIdType.MESH
@@ -342,24 +343,32 @@
 
 
 class Link:
+    slow = ("wox", "wol", "gf")
+
     def __init__(self, send_sems, recv_sems):
         self.send_sems, self.recv_sems = send_sems, recv_sems
-        self.first = {}
-        self.used = 0
-
-    def index(self, name, at, count):
-        if name not in self.first:
-            self.first[name] = self.used
-            self.used += count
-        return self.first[name] + at
+        self.receives, self.sends, self.slow_sends = {}, {}, {}
+
+    @staticmethod
+    def index(table, name, at, count):
+        if name not in table:
+            table[name] = (sum(size for _, size in table.values()), count)
+        return table[name][0] + at
+
+    def reuse(self):
+        self.sends = {}
 
     def copy(self, name, at, count, src, dst, device):
-        i = self.index(name, at, count)
+        if name in self.slow:
+            send = SEND_SEMS + self.index(self.slow_sends, name, at, count)
+        else:
+            send = self.index(self.sends, name, at, count)
+        receive = self.index(self.receives, name, at, count)
         return pltpu.make_async_remote_copy(
             src_ref=src,
             dst_ref=dst,
-            send_sem=self.send_sems.at[i],
-            recv_sem=self.recv_sems.at[i],
+            send_sem=self.send_sems.at[send],
+            recv_sem=self.recv_sems.at[receive],
             device_id=device,
             device_id_type=MESH,
         )
@@ -1180,6 +1189,17 @@
             ga_x(p).wait_recv()
         z_first(of_attn)
 
+    def sends_left():
+        for make in pending:
+            make().wait_send()
+        pending.clear()
+        seq_left("prms", lambda owner: prm_block(s), lambda: prm_block(s))
+        seq_left("wqs", lambda owner: PWQ.at[owner], lambda: wq_block(s))
+        for name in ("wi", "wq", "wa"):
+            for u in range(gathers[name][0]):
+                gather_left(name, u)
+        link.reuse()
+
     def attend_step(i, carry):
         w, p = i // 2, i % 2
         attend(w, p)
@@ -1190,6 +1210,7 @@
             gather_pass("wo", 3, 0)
             rows_pass("g", G, 1)
             qkv_step(1)
+            sends_left()
             gather_pass("wo", 3, 1)
             rows_end_far("g", G, 1)
             for j in range(2):
@@ -1221,9 +1242,10 @@
     ga_step(1)
 
     def in_step(j, carry):
-        units_back(j)
-        units_in(j)
-        i_x(chunk(j)).start()
+        turn_j = (j + 2) % 4
+        units_back(turn_j)
+        units_in(turn_j)
+        i_x(chunk(turn_j)).start()
 
         @pl.when(j == 0)
         def _():
@@ -1265,21 +1287,15 @@
         o_x(chunk(j)).start()
 
     def between_first():
-        first_i(chunk(0), True)
+        first_i(chunk(2), False)
         z_second(of_pair(1))
         z_second(of_attn)
 
     def between_second():
-        first_i(chunk(1), True)
-        second_i(chunk(0))
+        first_i(chunk(3), False)
 
     share_step(0, 1, between_first)
     share_step(1, 1, between_second)
-    for p in range(2):
-        total_q = z_total(of_pair(p)).T.astype(BF)
-        for owner in range(4):
-            SWQ[owner, :, 384 * p : 384 * p + 384] = total_q[32 * owner : 32 * owner + 32]
-    to_seq("swq", SWQ, RWQ)
     again = [
         pltpu.make_async_copy(x_in.at[w], N.at[w, 0:SL], local_sems.at[3 * w + 2]) for w in range(2)
     ]
@@ -1340,12 +1356,18 @@
         write(A.at[w, own], out_hbm.at[w])
         return write(grad_in, grad_in_hbm.at[w])
 
-    first_i(chunk(2), False)
+    first_i(chunk(0), True)
+    first_i(chunk(1), True)
+    second_i(chunk(0))
+    for p in range(2):
+        total_q = z_total(of_pair(p)).T.astype(BF)
+        for owner in range(4):
+            SWQ[owner, :, 384 * p : 384 * p + 384] = total_q[32 * owner : 32 * owner + 32]
+    to_seq("swq", SWQ, RWQ)
     second_i(chunk(1))
+    first_o(chunk(2))
     grad_a[...] = z_total(of_attn)
     write(grad_a, grad_a_hbm)
-    first_i(chunk(3), False)
-    first_o(chunk(2))
     first_rows = final_rows(0)
     tail_x()
     final_i()
@@ -1391,14 +1413,11 @@
 
     for make in pending:
         make().wait_send()
-    seq_left("prms", lambda owner: prm_block(s), lambda: prm_block(s))
-    seq_left("wqs", lambda owner: PWQ.at[owner], lambda: wq_block(s))
     seq_left("swi", lambda owner: SWI.at[owner], lambda: RWI.at[s])
     seq_left("swq", lambda owner: SWQ.at[owner], lambda: RWQ.at[s])
     seq_left("swt", lambda owner: SWT.at[owner], lambda: RWT.at[s])
-    for name, (parts, _) in gathers.items():
-        for u in range(parts):
-            gather_left(name, u)
+    for u in range(2):
+        gather_left("wo", u)
     for w in range(2):
         rows_left("g", G, w)
     for q in range(4):
@@ -1532,7 +1551,7 @@
             pltpu.VMEM((32, 3072), F32),
             pltpu.VMEM((32, 1024), F32),
             pltpu.VMEM((8, 128), F32),
-            pltpu.SemaphoreType.DMA((192,)),
+            pltpu.SemaphoreType.DMA((113,)),
             pltpu.SemaphoreType.DMA((192,)),
             pltpu.SemaphoreType.DMA((6,)),
             pltpu.SemaphoreType.DMA((14,)),

time: 165 us -> 164 us (level)
  no operation moved by 1% of the time
where the time goes in v6:
time: 164 us; the launch traced here: 163 us
  Pallas kernels  163 us (99%)
    pallas_call x1, Pallas kernels, fused_shards(): pl.pallas_call(fused_layer, out_shape=shapes + (jax.ShapeDtypeStruct((8,...  159 us
    pallas_call x1, Pallas kernels, fused_shards(): pl.pallas_call(publish, out_shape=shapes + rows_out, in_specs=[in_any] *...  3.91 us

profile of v6, /device:TPU:0, one launch (start us, length us, event | category | flops | bytes accessed | tf_op | source)
XLA Modules:
  0.0 163.5 jit_solution(5334320934278849951)
XLA Ops:
  0.6 158.7 %shard_map.195 = (bf16[2,256,1024]{2,1,0:T(8,128)(2,1)}, f32[2,256,1024]{2,1,0:T(8,128)}, f32[32,3072]{1,0:T(8,128)}, f32[32,1024]{1,0:T(8,128)}, f32[32,4096]{1...) custom-call(s32[2]{0:T(128)} %ends.1, bf16[1,32]{1,0:T(2,128)(2,1)} %bitcast.8, bf16[1,32]{1,0:T(2,128)(2,1)} %bitcast.9, ...), custom_call_target="tpu_custom_call" | custom-call | flops 46000001024 | bytes 10000000 | tf_op jit(solution)/shard_map/pallas_call | solution.py:1489
  159.4 3.9 %shard_map.196 = (bf16[2,256,1024]{2,1,0:T(8,128)(2,1)}, f32[2,256,1024]{2,1,0:T(8,128)}, f32[32,3072]{1,0:T(8,128)}, f32[32,1024]{1,0:T(8,128)}, f32[32,4096]{1...) custom-call(bf16[2,256,1024]{2,1,0:T(8,128)(2,1)} %get-tuple-element, ...), custom_call_target="tpu_custom_call" | custom-call | tf_op jit(solution)/shard_map/pallas_call | solution.py:1573
